TPU v7x, 256 devices: a whole 4x4x8 slice. The times are simulated.
256 devices in a mesh: role: 2 (over core), ctx: 4 (over y), req: 32 (over x, z).
Axes of the slice: x: 4, y: 4, z: 8, core: 2. Of those that a mesh axis runs over, the one named last changes fastest.
Arguments:
- cache: bfloat16 [64, 16384, 576], P(None, ('ctx', 'req'), 'role'), may hold values from -8 to 8
- lengths: int32 [64], replicated, may hold values from 2 to 16384
- request_decode_slot: int32 [64], replicated, may hold values from 0 to 63, as said below
- q_nope: bfloat16 [64, 4, 16384], P('req', None, ('role', 'ctx')), may hold values from -6 to 6
- q_rope: bfloat16 [64, 4, 8192], P('req', None, ('role', 'ctx')), may hold values from -8 to 8
- new_latent: bfloat16 [64, 4, 576], P('req'), may hold values from -4.1875 to 4.1875
- w_key: bfloat16 [128, 128, 512], P(('role', 'ctx')), may hold values from -0.5 to 0.5
- value_up_weight: bfloat16 [128, 512, 128], P(('role', 'ctx')), may hold values from -1 to 1
Outputs:
- attended: bfloat16 [64, 4, 16384], P('req', None, ('role', 'ctx'))
Inputs may be any that keep to these rules, and one draw needn't show every extreme that they name: A permutation of the slots; request r is owned by req index request_decode_slot[r] // 2.
All inputs are finite; a program needn't handle non-finite values.
Results may differ from a plain program's by a relative error of at most 0.007.
Values may be sent and summed in bfloat16 or wider, within the bound.
No kernel may reach another device: no remote copies, remote signals or barrier semaphores. Data moves between devices by JAX's collectives and lax.ppermute only.
A program may use at most 128 MiB of HBM per device.

v0:
```python
import functools

import jax
import jax.numpy as jnp
from jax import lax
from jax.experimental import pallas as pl
from jax.experimental.pallas import tpu as pltpu
from jax.sharding import PartitionSpec as P

NX, NZ = 4, 8
NC = 4
LANES = 128
NEG = -1e30


def z_to(z, c):
    return (z + (0, 1, -1, 2 if z % 2 == 0 else -2)[c]) % NZ


def move_z(a, c):
    if c == 0:
        return a
    return lax.ppermute(a, "req", [(x * NZ + z, x * NZ + z_to(z, c)) for x in range(NX) for z in range(NZ)])


def move_x(a, dx):
    if dx == 0:
        return a
    return lax.ppermute(a, "req", [(x * NZ + z, (x + dx) % NX * NZ + z) for x in range(NX) for z in range(NZ)])


def move_far(a):
    return lax.ppermute(a, "req", [(x * NZ + z, x * NZ + (z + 4) % NZ) for x in range(NX) for z in range(NZ)])


def swap_role(a):
    return lax.ppermute(a, "role", [(0, 1), (1, 0)])


def lookup(slots, values, want):
    return jnp.sum(jnp.where(slots == want[..., None], values, 0), axis=-1)


def attend_kernel(fresh, scale, scal_ref, q_ref, *rest):
    mine, recv = rest[:4], rest[4:8]
    rest = rest[8:]
    if fresh:
        new_ref, rest = rest[0], rest[1:]
    o_ref, kt, s_ref = rest
    half = mine[0].shape[1]
    latent = o_ref.shape[1] - LANES
    rows = q_ref.shape[0]
    role = scal_ref[16]
    at_mine = pl.ds(pl.multiple_of(role * half, 32), half)
    at_recv = pl.ds(pl.multiple_of((1 - role) * half, 32), half)
    chunk = 4 * LANES
    lane = lax.broadcasted_iota(jnp.int32, (1, LANES), 1)
    high = jnp.full((rows, LANES), NEG, jnp.float32)
    for j in range(4):
        for c in range(4):
            cols = slice(j * chunk + c * LANES, j * chunk + (c + 1) * LANES)
            kt[at_mine, cols] = mine[c][j]
            kt[at_recv, cols] = recv[j][c]
        s = jnp.dot(q_ref[...], kt[:, j * chunk:(j + 1) * chunk], preferred_element_type=jnp.float32)
        for c in range(4):
            t = s[:, c * LANES:(c + 1) * LANES] * scale
            t = jnp.where(lane < scal_ref[j * 4 + c], t, NEG)
            s_ref[:, j * chunk + c * LANES:j * chunk + (c + 1) * LANES] = t
            high = jnp.maximum(high, t)
    if fresh:
        t = jnp.dot(q_ref[...], new_ref[...], preferred_element_type=jnp.float32) * scale
        step = (lax.broadcasted_iota(jnp.int32, (rows, LANES), 0) // 16) % 4
        u = lax.broadcasted_iota(jnp.int32, (rows, LANES), 1)
        f = jnp.where((u <= step) & (scal_ref[17] == 0), t, NEG)
        high = jnp.maximum(high, f)
    m = jnp.maximum(jnp.max(high, axis=1, keepdims=True), -1e29)
    total = jnp.zeros((rows, LANES), jnp.float32)
    acc = jnp.zeros((rows, latent), jnp.float32)
    nt = (((1,), (1,)), ((), ()))
    for j in range(4):
        w = jnp.exp(s_ref[:, j * chunk:(j + 1) * chunk] - m)
        for c in range(4):
            total = total + w[:, c * LANES:(c + 1) * LANES]
        acc = acc + lax.dot_general(w.astype(jnp.bfloat16), kt[:latent, j * chunk:(j + 1) * chunk], nt,
                                    preferred_element_type=jnp.float32)
    if fresh:
        w = jnp.exp(f - m)
        total = total + w
        acc = acc + lax.dot_general(w.astype(jnp.bfloat16), new_ref[:latent, :], nt, preferred_element_type=jnp.float32)
    norm = jnp.sum(total, axis=1, keepdims=True)
    some = norm > 0.0
    safe = jnp.where(some, norm, 1.0)
    o_ref[:, :latent] = (acc / safe).astype(jnp.bfloat16)
    lse = jnp.where(some, m + jnp.log(safe), NEG)
    o_ref[:, latent:] = pack_columns(lse, lax.broadcasted_iota(jnp.int32, (rows, LANES), 1))


def pack_columns(lse, lane):
    a = lse.astype(jnp.bfloat16).astype(jnp.float32)
    b = (lse - a).astype(jnp.bfloat16).astype(jnp.float32)
    c = (lse - a) - b
    return jnp.where(lane == 0, a, jnp.where(lane == 1, b, jnp.where(lane == 2, c, 0.0))).astype(jnp.bfloat16)


def attend(scal, q, mine, recv, new, latent, scale):
    rows, width = q.shape
    fresh = new is not None
    vm = pl.BlockSpec(memory_space=pltpu.VMEM)
    args = [q, *mine, *recv] + ([new] if fresh else [])
    positions = 16 * LANES
    return pl.pallas_call(
        functools.partial(attend_kernel, fresh, scale),
        in_specs=[pl.BlockSpec(memory_space=pltpu.SMEM)] + [vm] * len(args),
        out_specs=vm,
        out_shape=jax.ShapeDtypeStruct((rows, latent + LANES), jnp.bfloat16),
        scratch_shapes=[pltpu.VMEM((width, positions), jnp.bfloat16), pltpu.VMEM((rows, positions), jnp.float32)],
        compiler_params=pltpu.CompilerParams(vmem_limit_bytes=40 * 1024 * 1024),
        cost_estimate=pl.CostEstimate(flops=2 * rows * positions * (width + latent),
                                      bytes_accessed=positions * width * 2 + rows * (width + latent) * 2,
                                      transcendentals=rows * positions),
    )(scal, *args)


def merge(parts, latent, axis):
    lse = jnp.sum(parts[..., latent:latent + 3].astype(jnp.float32), axis=-1, keepdims=True)
    top = jnp.max(lse, axis=axis, keepdims=True)
    w = jnp.exp(lse - top)
    norm = jnp.sum(w, axis=axis)
    rows = jnp.sum(parts[..., :latent].astype(jnp.float32) * w, axis=axis) / norm
    return rows, jnp.squeeze(top, axis) + jnp.log(norm)


def after(v, dep):
    return lax.optimization_barrier((v, dep))[0]


def exchange(by_x, away):
    got_x, got_z = [None] * 4, [None] * 4
    for i in (1, 2, 3, 0):
        got_z[i] = swap_role(away[i])
    for i in (1, 2, 3, 0):
        got_x[i] = move_x(by_x[i], i)
        got_z[i] = move_z(got_z[i], i)
    sides = []
    mine, recv = [None] * 4, [None] * 4
    for g in range(2):
        mine = [move_z(after(jnp.stack([got_x[d][g, c] for d in range(4)]), mine[c]), c) for c in range(4)]
        recv = [move_x(after(jnp.stack([got_z[c][g, d] for c in range(4)]), recv[d]), d) for d in range(4)]
        sides.append((mine, recv))
    return sides


def shards(cache, lengths, request_decode_slot, q_nope, q_rope, new_latent, w_key, value_up_weight):
    heads_dev, nope_dim, latent = w_key.shape
    req_dev, steps = q_nope.shape[:2]
    rope_dim = q_rope.shape[2] // heads_dev
    scale = (nope_dim + rope_dim) ** -0.5
    role, ctx, req = lax.axis_index("role"), lax.axis_index("ctx"), lax.axis_index("req")
    x, z = req // NZ, req % NZ
    total = request_decode_slot.shape[0]
    ids = jnp.arange(total, dtype=jnp.int32)
    dx = jnp.arange(NX, dtype=jnp.int32)[:, None]
    cls = jnp.arange(NC, dtype=jnp.int32)
    move = jnp.where(cls == 1, 1, jnp.where(cls == 2, -1, jnp.where(cls == 3, jnp.where(z % 2 == 0, 2, -2), 0)))[None, :]
    blocks = jnp.swapaxes(cache, 1, 2)

    far = jnp.array([4, 0], jnp.int32)[:, None, None]
    owner = (x + dx) % NX * NZ + (z + move + far + NZ) % NZ
    take_x = lookup(request_decode_slot, ids, 2 * owner + role)
    take_z = lookup(request_decode_slot, ids, 2 * owner + 1 - role)
    by_x = [blocks[take_x[:, d]] for d in range(NX)]
    away = [blocks[take_z[:, :, c]] for c in range(NC)]
    source = (x - dx + NX) % NX * NZ + (z - move + NZ) % NZ
    base = ctx * (NX * NZ * LANES) + source * LANES

    def scalars(far):
        want = 2 * (x * NZ + (z + far) % NZ) + role
        length = lookup(request_decode_slot, lengths, want)
        return jnp.concatenate([(length - base).reshape(-1), role[None], ctx[None]]).astype(jnp.int32)

    queries = q_nope.reshape(req_dev, steps, heads_dev, nope_dim)
    absorbed = jnp.einsum("bshd,hdk->bshk", queries, w_key, preferred_element_type=jnp.float32).astype(jnp.bfloat16)
    own = jnp.concatenate([absorbed, q_rope.reshape(req_dev, steps, heads_dev, rope_dim)], axis=3)
    both = jnp.stack([own, move_far(own)], axis=1)
    keep = jnp.where(role == 0, both[0], both[1])
    got = swap_role(jnp.where(role == 0, both[1], both[0]))
    pair = jnp.stack([jnp.where(role == 0, keep, got), jnp.where(role == 0, got, keep)], axis=1)
    every = lax.all_gather(pair, "ctx", axis=2, tiled=False)
    every = every.reshape(2, -1, latent + rope_dim)

    (mine_f, recv_f), (mine_n, recv_n) = exchange(by_x, away)
    part_f = attend(scalars(4), every[1], mine_f, recv_f, None, latent, scale)
    heads = 2 * lax.axis_size("ctx")
    part_f = lax.all_to_all(part_f.reshape(heads, -1, latent + LANES), ("role", "ctx"), 0, 0, tiled=True)
    rows_f, lse_f = merge(part_f.reshape(2, -1, *part_f.shape[1:]), latent, 1)
    packed = jnp.concatenate(
        [rows_f.astype(jnp.bfloat16), pack_columns(lse_f, lax.broadcasted_iota(jnp.int32, (*lse_f.shape[:2], LANES), 2))], axis=-1)
    packed = move_far(packed)

    new = jnp.where(role == 0, new_latent[0], new_latent[1])
    new = jnp.pad(new.T, ((0, 0), (0, LANES - steps)))
    part_n = attend(scalars(0), every[0], mine_n, recv_n, new, latent, scale)
    part_n = lax.all_to_all(part_n.reshape(heads, -1, latent + LANES), ("role", "ctx"), 0, 0, tiled=True)
    parts = jnp.concatenate([part_n.reshape(2, -1, *part_n.shape[1:]), packed[:, None]], axis=1)
    merged, _ = merge(parts, latent, 1)
    merged = merged.astype(jnp.bfloat16).reshape(req_dev, steps, heads_dev, latent)
    out = jnp.einsum("bshk,hkv->bshv", merged, value_up_weight, preferred_element_type=jnp.float32).astype(jnp.bfloat16)
    return out.reshape(req_dev, steps, -1)


def solution(mesh):
    placed = (
        P(None, ("ctx", "req"), "role"),
        P(),
        P(),
        P("req", None, ("role", "ctx")),
        P("req", None, ("role", "ctx")),
        P("req", None, None),
        P(("role", "ctx"), None, None),
        P(("role", "ctx"), None, None),
    )
    return jax.shard_map(
        shards,
        mesh=mesh,
        in_specs=placed,
        out_specs=P("req", None, ("role", "ctx")),
        check_vma=False,
    )
```

profile of v0, /device:TPU:41, one launch (start us, length us, event | category | flops | bytes accessed | tf_op | source)
XLA Modules:
  0.0 205.4 jit_solution(7961716003910948179)
XLA Ops:
  6.5 1.0 reshape.367
  8.1 1.1 fusion.7
  10.1 6.0 %collective-permute-start = (bf16[2,4,16,576]{3,1,0,2:T(4,128)(2,1)}, bf16[2,4,16,576]{3,1,0,2:T(4,128)(2,1)S(1)}, u32[]{:S(2)}, u32[]{:S(2)}) collective-permute-start(bf16[2,4,16,576]{3,1,0,2:T(4,128)(2,1)} %get-tuple-element.100), channel_id=1, source_target_pairs={{0,4},{1,5},{2,6},{3,7},{4,0},{5,1},{6,2},{7,3},{8,12},{9,13},{10,... | collective-permute-start | bytes 442376 | tf_op jit(solution)/shard_map/ppermute | solution.py:33
  17.1 3.8 %gather_fusion.5 = bf16[8,288,128]{2,1,0:T(8,128)(2,1)} fusion(bf16[64,288,128]{2,1,0:T(8,128)(2,1)} %bitcast.228, s32[1024]{0:T(1024)S(1)} %pad_clamp_fusion.2), kind=kCustom, calls=%fused_computation.5 | custom fusion | bytes 1179680 | tf_op jit(solution)/shard_map/gather | solution.py:172
  20.9 1.0 collective-permute-start.12
  21.9 3.8 %gather_fusion.6 = bf16[8,288,128]{2,1,0:T(8,128)(2,1)} fusion(bf16[64,288,128]{2,1,0:T(8,128)(2,1)} %bitcast.229, s32[1024]{0:T(1024)S(1)} %pad_clamp_fusion.1), kind=kCustom, calls=%fused_computation.6 | custom fusion | bytes 1179680 | tf_op jit(solution)/shard_map/gather | solution.py:172
  26.0 3.8 %gather_fusion.3 = bf16[8,288,128]{2,1,0:T(8,128)(2,1)} fusion(bf16[64,288,128]{2,1,0:T(8,128)(2,1)} %bitcast.230, s32[1024]{0:T(1024)S(1)} %pad_clamp_fusion.4), kind=kCustom, calls=%fused_computation.3 | custom fusion | bytes 1179680 | tf_op jit(solution)/shard_map/gather | solution.py:171
  29.8 2.5 %collective-permute-start.4 = (bf16[2,4,288,128]{3,2,1,0:T(8,128)(2,1)}, bf16[2,4,288,128]{3,2,1,0:T(8,128)(2,1)}, u32[]{:S(2)}, u32[]{:S(2)}) collective-permute-start(bf16[2,4,288,128]{3,2,1,0:T(8,128)(2,1)} %bitcast.26), channel_id=1, source_target_pairs={{0,24},{1,25},{2,26},{3,27},{4,28},{5,29},{6,30},{7,31},{8,0},{9,1... | collective-permute-start | bytes 1769480 | tf_op jit(solution)/shard_map/ppermute | solution.py:29
  32.6 3.8 %gather_fusion.2 = bf16[8,288,128]{2,1,0:T(8,128)(2,1)} fusion(bf16[64,288,128]{2,1,0:T(8,128)(2,1)} %bitcast.231, s32[1024]{0:T(1024)S(1)} %pad_clamp_fusion.5), kind=kCustom, calls=%fused_computation.2 | custom fusion | bytes 1179680 | tf_op jit(solution)/shard_map/gather | solution.py:171
  38.1 3.0 %gather_fusion = bf16[8,288,128]{2,1,0:T(8,128)(2,1)S(1)} fusion(bf16[64,288,128]{2,1,0:T(8,128)(2,1)} %bitcast.232, s32[1024]{0:T(1024)S(1)} %pad_clamp_fusion.7), kind=kCustom, calls=%fused_computation | custom fusion | bytes 1179680 | tf_op jit(solution)/shard_map/gather | solution.py:171
  41.1 0.9 slice_bitcast_fusion.35
  42.7 1.4 fusion.33
  44.5 1.2 collective-permute-start.1
  45.8 3.8 %gather_fusion.1 = bf16[8,288,128]{2,1,0:T(8,128)(2,1)} fusion(bf16[64,288,128]{2,1,0:T(8,128)(2,1)} %bitcast.233, s32[1024]{0:T(1024)S(1)} %pad_clamp_fusion.6), kind=kCustom, calls=%fused_computation.1 | custom fusion | bytes 1179680 | tf_op jit(solution)/shard_map/gather | solution.py:171
  49.6 3.8 %gather_fusion.4 = bf16[8,288,128]{2,1,0:T(8,128)(2,1)} fusion(bf16[64,288,128]{2,1,0:T(8,128)(2,1)} %bitcast.234, s32[1024]{0:T(1024)S(1)} %pad_clamp_fusion.3), kind=kCustom, calls=%fused_computation.4 | custom fusion | bytes 1179680 | tf_op jit(solution)/shard_map/gather | solution.py:172
  53.4 3.0 %gather_fusion.7 = bf16[8,288,128]{2,1,0:T(8,128)(2,1)S(1)} fusion(bf16[64,288,128]{2,1,0:T(8,128)(2,1)} %bitcast.235, s32[1024]{0:T(1024)S(1)} %pad_clamp_fusion), kind=kCustom, calls=%fused_computation.7 | custom fusion | bytes 1179680 | tf_op jit(solution)/shard_map/gather | solution.py:172
  58.8 1.8 slice_bitcast_fusion.32
  60.9 1.8 slice_bitcast_fusion.33
  62.8 10.2 %collective-permute-done.2 = bf16[2,4,288,128]{3,2,1,0:T(8,128)(2,1)} collective-permute-done((bf16[2,4,288,128]{3,2,1,0:T(8,128)(2,1)}, bf16[2,4,288,128]{3,2,1,0:T(8,128)(2,1)}, u32[]{:S(2)}, u32[]{:S(2)}) %collective-permute-start.2) | collective-permute-done | bytes 589856 | tf_op jit(solution)/shard_map/ppermute | solution.py:29
  73.0 1.8 slice_bitcast_fusion.34
  78.7 3.6 %collective-permute-start.9 = (bf16[4,288,128]{2,1,0:T(8,128)(2,1)S(1)}, bf16[4,288,128]{2,1,0:T(8,128)(2,1)S(1)}, u32[]{:S(2)}, u32[]{:S(2)}) collective-permute-start(bf16[4,288,128]{2,1,0:T(8,128)(2,1)S(1)} %pad_maximum_fusion.8), channel_id=1, source_target_pairs={{0,2},{1,7},{2,4},{3,1},{4,6},{5,3},{6,0},{7,5},{8,10},{9,15},{10,... | collective-permute-start | bytes 884744 | tf_op jit(solution)/shard_map/ppermute | solution.py:23
  83.1 1.2 collective-permute-start.17
  85.1 1.1 collective-permute-start.6
  86.2 3.8 %collective-permute-done.9.rest_3_ = bf16[4,288,128]{2,1,0:T(8,128)(2,1)S(1)} collective-permute-done((bf16[4,288,128]{2,1,0:T(8,128)(2,1)S(1)}, bf16[4,288,128]{2,1,0:T(8,128)(2,1)S(1)}, u32[]{:S(2)}, u32[]{:S(2)}) %collective-permute-start.9) | collective-permute-done | bytes 294944 | tf_op jit(solution)/shard_map/ppermute | solution.py:23
  90.0 12.0 %collective-permute-start.8 = (bf16[4,288,128]{2,1,0:T(8,128)(2,1)}, bf16[4,288,128]{2,1,0:T(8,128)(2,1)}, u32[]{:S(2)}, u32[]{:S(2)}) collective-permute-start(bf16[4,288,128]{2,1,0:T(8,128)(2,1)} %pad_maximum_fusion.5), channel_id=1, source_target_pairs={{0,7},{1,0},{2,1},{3,2},{4,3},{5,4},{6,5},{7,6},{8,15},{9,8},{10,9... | collective-permute-start | bytes 884744 | tf_op jit(solution)/shard_map/ppermute | solution.py:23
  102.7 0.8 collective-permute-done.15
  104.2 11.1 %collective-permute-done.17 = bf16[2,4,288,128]{3,2,1,0:T(8,128)(2,1)S(1)} collective-permute-done((bf16[2,4,288,128]{3,2,1,0:T(8,128)(2,1)S(1)}, bf16[2,4,288,128]{3,2,1,0:T(8,128)(2,1)S(1)}, u32[]{:S(2)}, u32[]{:S(2)}) %collective-permute-start.17) | collective-permute-done | bytes 589856 | tf_op jit(solution)/shard_map/ppermute | solution.py:23
  118.3 1.7 collective-permute-start.20
  119.9 1.6 collective-permute-start.22
  123.2 2.3 %fusion.47 = (bf16[1,2,16,16,576]{4,3,1,0,2:T(8,128)(2,1)S(1)}, bf16[1,2,16,16,576]{4,3,1,0,2:T(8,128)(2,1)}) fusion(bf16[2,2,16,16,576]{4,3,1,0,2:T(8,128)(2,1)} %all-gather.3.cloned.1.call-done), kind=kLoop, calls=%fused_computation.198 | loop fusion | bytes 2359296 | tf_op jit(solution)/shard_map/slice | solution.py:192
  125.5 2.2 %collective-permute-done.18.rest_5_ = bf16[4,288,128]{2,1,0:T(8,128)(2,1)} collective-permute-done((bf16[4,288,128]{2,1,0:T(8,128)(2,1)}, bf16[4,288,128]{2,1,0:T(8,128)(2,1)}, u32[]{:S(2)}, u32[]{:S(2)}) %collective-permute-start.18) | collective-permute-done | bytes 294944 | tf_op jit(solution)/shard_map/ppermute | solution.py:29
  127.7 3.7 %collective-permute-start.10 = (bf16[4,288,128]{2,1,0:T(8,128)(2,1)}, bf16[4,288,128]{2,1,0:T(8,128)(2,1)}, u32[]{:S(2)}, u32[]{:S(2)}) collective-permute-start(bf16[4,288,128]{2,1,0:T(8,128)(2,1)} %pad_maximum_fusion.7), channel_id=1, source_target_pairs={{0,2},{1,7},{2,4},{3,1},{4,6},{5,3},{6,0},{7,5},{8,10},{9,15},{10,... | collective-permute-start | bytes 884744 | tf_op jit(solution)/shard_map/ppermute | solution.py:23
  131.4 1.7 collective-permute-done.22.rest_7_
  133.1 6.2 %shard_map.92 = bf16[512,640]{1,0:T(8,128)(2,1)} custom-call(s32[18]{0:T(128)S(1)} %add_add_fusion.1.scal_ref, bf16[512,576]{1,0:T(8,128)(2,1)S(1)} %bitcast.225, bf16[4,288,128]{2,1,0:T(8,128)(2,1)S(1)} %pad_maximum_fusion.2.rest_0_, bf16[4,288,128]{2,1,0:T(8,128)(2,1)S(1)} %collective-permute-done.5.rest_1_, bf16[4,288,128]{2,1,0:T(8,128)(2,1)S(1)} %copy-done.2, ...), custom_call_target="tpu_custom_call" | custom-call | flops 2281701376 | bytes 3473408 | tf_op jit(solution)/shard_map/pallas_call | solution.py:111
  139.3 9.7 %all-to-all-start.1 = ((bf16[8,64,640]{2,1,0:T(8,128)(2,1)}), bf16[8,64,640]{2,1,0:T(8,128)(2,1)}, u32[]{:S(2)}, u32[]{:S(2)}) async-start(bf16[8,64,640]{2,1,0:T(8,128)(2,1)} %bitcast.97), calls=%async_computation.1 | async-start | bytes 1310720 | tf_op jit(solution)/shard_map/all_to_all | solution.py:194
  149.0 1.0 pad_maximum_fusion.11
  150.1 1.5 collective-permute-start.21
  151.7 1.1 collective-permute-start.23
  153.0 1.0 pad_maximum_fusion.9.rest_4_
  154.2 11.7 %collective-permute-done.19.rest_5_ = bf16[4,288,128]{2,1,0:T(8,128)(2,1)S(1)} collective-permute-done((bf16[4,288,128]{2,1,0:T(8,128)(2,1)S(1)}, bf16[4,288,128]{2,1,0:T(8,128)(2,1)S(1)}, u32[]{:S(2)}, u32[]{:S(2)}) %collective-permute-start.19) | collective-permute-done | bytes 294944 | tf_op jit(solution)/shard_map/ppermute | solution.py:29
  166.5 6.8 %shard_map.91 = bf16[512,640]{1,0:T(8,128)(2,1)} custom-call(s32[18]{0:T(128)S(1)} %add_add_fusion.scal_ref, bf16[512,576]{1,0:T(8,128)(2,1)S(1)} %bitcast.224, bf16[4,288,128]{2,1,0:T(8,128)(2,1)S(1)} %pad_maximum_fusion.1.rest_0_, bf16[4,288,128]{2,1,0:T(8,128)(2,1)S(1)} %collective-permute-done.6.rest_1_, ...), custom_call_target="tpu_custom_call" | custom-call | flops 2281701376 | bytes 3473408 | tf_op jit(solution)/shard_map/pallas_call | solution.py:111
  173.3 5.9 %all-to-all-start = ((bf16[8,64,640]{2,1,0:T(8,128)(2,1)}), bf16[8,64,640]{2,1,0:T(8,128)(2,1)S(1)}, u32[]{:S(2)}, u32[]{:S(2)}) async-start(bf16[8,64,640]{2,1,0:T(8,128)(2,1)} %bitcast.94), calls=%async_computation | async-start | bytes 1310720 | tf_op jit(solution)/shard_map/all_to_all | solution.py:203
  179.2 1.0 convert_reduce_fusion.1
  180.5 1.2 multiply_reduce_fusion.1
  181.8 1.3 collective-permute-start.24
  183.2 6.3 %all-to-all-done = bf16[8,64,640]{2,1,0:T(8,128)(2,1)S(1)} async-done(((bf16[8,64,640]{2,1,0:T(8,128)(2,1)}), bf16[8,64,640]{2,1,0:T(8,128)(2,1)S(1)}, u32[]{:S(2)}, u32[]{:S(2)}) %all-to-all-start) | async-done | bytes 655392 | tf_op jit(solution)/shard_map/all_to_all | solution.py:203
  189.4 5.8 %collective-permute-done.24 = bf16[2,64,640]{2,1,0:T(8,128)(2,1)S(1)} collective-permute-done((bf16[2,64,640]{2,1,0:T(8,128)(2,1)S(1)}, bf16[2,64,640]{2,1,0:T(8,128)(2,1)S(1)}, u32[]{:S(2)}, u32[]{:S(2)}) %collective-permute-start.24) | collective-permute-done | bytes 163872 | tf_op jit(solution)/shard_map/ppermute | solution.py:33
  195.9 2.0 fusion.13
  (156 shorter events, 22.7 us)
Async XLA Ops:
  6.5 9.6 %copy-start.20 = (s32[2]{0:T(128)S(1)}, s32[2]{0:T(128)}, u32[]{:S(2)}) copy-start(s32[2]{0:T(128)} %constant.124.clone) | copy-start | bytes 28
  6.5 9.7 %copy-start.18 = (s32[64]{0:T(128)S(1)}, s32[64]{0:T(128)}, u32[]{:S(2)}) copy-start(s32[64]{0:T(128)} %param.11) | copy-start | bytes 772
  6.5 116.6 %all-gather.3.cloned.1.call-start = ((), (), s32[]{:S(2)}) async-start(), calls=%async_computation.2 | async-start | bytes 1638400 | tf_op jit(solution)/shard_map/all_gather | solution.py:188
  10.1 34.2 %collective-permute-start = (bf16[2,4,16,576]{3,1,0,2:T(4,128)(2,1)}, bf16[2,4,16,576]{3,1,0,2:T(4,128)(2,1)S(1)}, u32[]{:S(2)}, u32[]{:S(2)}) collective-permute-start(bf16[2,4,16,576]{3,1,0,2:T(4,128)(2,1)} %get-tuple-element.100), channel_id=1, source_target_pairs={{0,4},{1,5},{2,6},{3,7},{4,0},{5,1},{6,2},{7,3},{8,12},{9,13},{10,... | collective-permute-start | bytes 442376 | tf_op jit(solution)/shard_map/ppermute | solution.py:33
  20.8 16.9 %copy-start.17 = (bf16[2,4,576]{2,1,0:T(4,128)(2,1)S(1)}, bf16[2,4,576]{2,1,0:T(4,128)(2,1)}, u32[]{:S(2)}) copy-start(bf16[2,4,576]{2,1,0:T(4,128)(2,1)} %param.14) | copy-start | bytes 27652
  20.9 54.8 %collective-permute-start.12 = (bf16[2,4,288,128]{3,2,1,0:T(8,128)(2,1)}, bf16[2,4,288,128]{3,2,1,0:T(8,128)(2,1)}, u32[]{:S(2)}, u32[]{:S(2)}) collective-permute-start(bf16[2,4,288,128]{3,2,1,0:T(8,128)(2,1)} %bitcast.58), channel_id=1, source_target_pairs={{0,128},{128,0},{1,129},{129,1},{2,130},{130,2},{3,131},{131,3},{4... | collective-permute-start | bytes 1769480 | tf_op jit(solution)/shard_map/ppermute | solution.py:37
  25.7 53.0 %collective-permute-start.14 = (bf16[2,4,288,128]{3,2,1,0:T(8,128)(2,1)}, bf16[2,4,288,128]{3,2,1,0:T(8,128)(2,1)}, u32[]{:S(2)}, u32[]{:S(2)}) collective-permute-start(bf16[2,4,288,128]{3,2,1,0:T(8,128)(2,1)} %bitcast.60), channel_id=1, source_target_pairs={{0,128},{128,0},{1,129},{129,1},{2,130},{130,2},{3,131},{131,3},{4... | collective-permute-start | bytes 1769480 | tf_op jit(solution)/shard_map/ppermute | solution.py:37
  29.8 12.2 %copy-start.19 = (s32[64]{0:T(128)S(1)}, s32[64]{0:T(128)}, u32[]{:S(2)}) copy-start(s32[64]{0:T(128)} %param.10) | copy-start | bytes 772
  29.8 28.6 %collective-permute-start.4 = (bf16[2,4,288,128]{3,2,1,0:T(8,128)(2,1)}, bf16[2,4,288,128]{3,2,1,0:T(8,128)(2,1)}, u32[]{:S(2)}, u32[]{:S(2)}) collective-permute-start(bf16[2,4,288,128]{3,2,1,0:T(8,128)(2,1)} %bitcast.26), channel_id=1, source_target_pairs={{0,24},{1,25},{2,26},{3,27},{4,28},{5,29},{6,30},{7,31},{8,0},{9,1... | collective-permute-start | bytes 1769480 | tf_op jit(solution)/shard_map/ppermute | solution.py:29
  36.4 24.2 %collective-permute-start.3 = (bf16[2,4,288,128]{3,2,1,0:T(8,128)(2,1)}, bf16[2,4,288,128]{3,2,1,0:T(8,128)(2,1)}, u32[]{:S(2)}, u32[]{:S(2)}) collective-permute-start(bf16[2,4,288,128]{3,2,1,0:T(8,128)(2,1)} %bitcast.23), channel_id=1, source_target_pairs={{0,16},{1,17},{2,18},{3,19},{4,20},{5,21},{6,22},{7,23},{8,24},{9,... | collective-permute-start | bytes 1769480 | tf_op jit(solution)/shard_map/ppermute | solution.py:29
  44.5 11.9 %collective-permute-start.1 = (bf16[2,4,16,576]{3,1,2,0:T(4,128)(2,1)S(1)}, bf16[2,4,16,576]{3,1,2,0:T(4,128)(2,1)S(1)}, u32[]{:S(2)}, u32[]{:S(2)}) collective-permute-start(bf16[2,4,16,576]{3,1,2,0:T(4,128)(2,1)S(1)} %fusion.17), channel_id=1, source_target_pairs={{0,128},{128,0},{1,129},{129,1},{2,130},{130,2},{3,131},{131,3},{4... | collective-permute-start | bytes 442376 | tf_op jit(solution)/shard_map/ppermute | solution.py:37
  56.4 16.6 %collective-permute-start.2 = (bf16[2,4,288,128]{3,2,1,0:T(8,128)(2,1)}, bf16[2,4,288,128]{3,2,1,0:T(8,128)(2,1)}, u32[]{:S(2)}, u32[]{:S(2)}) collective-permute-start(bf16[2,4,288,128]{3,2,1,0:T(8,128)(2,1)} %bitcast.244), channel_id=1, source_target_pairs={{0,8},{1,9},{2,10},{3,11},{4,12},{5,13},{6,14},{7,15},{8,16},{9,17... | collective-permute-start | bytes 1769480 | tf_op jit(solution)/shard_map/ppermute | solution.py:29
  58.4 16.4 %copy-start.16 = (bf16[1,288,128]{2,1,0:T(8,128)(2,1)S(1)}, bf16[1,288,128]{2,1,0:T(8,128)(2,1)}, u32[]{:S(2)}) copy-start(bf16[1,288,128]{2,1,0:T(8,128)(2,1)} %get-tuple-element.67) | copy-start | bytes 221188
  58.4 16.4 %copy-start.15 = (bf16[1,288,128]{2,1,0:T(8,128)(2,1)S(1)}, bf16[1,288,128]{2,1,0:T(8,128)(2,1)}, u32[]{:S(2)}) copy-start(bf16[1,288,128]{2,1,0:T(8,128)(2,1)} %get-tuple-element.69) | copy-start | bytes 221188
  58.5 23.8 %collective-permute-start.16 = (bf16[2,4,288,128]{3,2,1,0:T(8,128)(2,1)S(1)}, bf16[2,4,288,128]{3,2,1,0:T(8,128)(2,1)S(1)}, u32[]{:S(2)}, u32[]{:S(2)}) collective-permute-start(bf16[2,4,288,128]{3,2,1,0:T(8,128)(2,1)S(1)} %bitcast.242), channel_id=1, source_target_pairs={{0,128},{128,0},{1,129},{129,1},{2,130},{130,2},{3,131},{131,3},{4... | collective-permute-start | bytes 1769480 | tf_op jit(solution)/shard_map/ppermute | solution.py:37
  60.6 17.2 %copy-start.14 = (bf16[1,288,128]{2,1,0:T(8,128)(2,1)S(1)}, bf16[1,288,128]{2,1,0:T(8,128)(2,1)}, u32[]{:S(2)}) copy-start(bf16[1,288,128]{2,1,0:T(8,128)(2,1)} %get-tuple-element.65) | copy-start | bytes 221188
  60.6 15.8 %collective-permute-start.11 = (bf16[2,4,288,128]{3,2,1,0:T(8,128)(2,1)}, bf16[2,4,288,128]{3,2,1,0:T(8,128)(2,1)S(1)}, u32[]{:S(2)}, u32[]{:S(2)}) collective-permute-start(bf16[2,4,288,128]{3,2,1,0:T(8,128)(2,1)} %bitcast.243), channel_id=1, source_target_pairs={{0,128},{128,0},{1,129},{129,1},{2,130},{130,2},{3,131},{131,3},{4... | collective-permute-start | bytes 1769480 | tf_op jit(solution)/shard_map/ppermute | solution.py:37
  62.8 15.2 %copy-start.13 = (bf16[1,288,128]{2,1,0:T(8,128)(2,1)S(1)}, bf16[1,288,128]{2,1,0:T(8,128)(2,1)}, u32[]{:S(2)}) copy-start(bf16[1,288,128]{2,1,0:T(8,128)(2,1)} %get-tuple-element.66) | copy-start | bytes 221188
  62.8 19.5 %copy-start.12 = (bf16[1,288,128]{2,1,0:T(8,128)(2,1)S(1)}, bf16[1,288,128]{2,1,0:T(8,128)(2,1)}, u32[]{:S(2)}) copy-start(bf16[1,288,128]{2,1,0:T(8,128)(2,1)} %get-tuple-element.71) | copy-start | bytes 221188
  74.8 7.6 %copy-start.11 = (bf16[1,288,128]{2,1,0:T(8,128)(2,1)S(1)}, bf16[1,288,128]{2,1,0:T(8,128)(2,1)}, u32[]{:S(2)}) copy-start(bf16[1,288,128]{2,1,0:T(8,128)(2,1)} %get-tuple-element.68) | copy-start | bytes 221188
  74.8 9.5 %copy-start.10 = (bf16[1,288,128]{2,1,0:T(8,128)(2,1)S(1)}, bf16[1,288,128]{2,1,0:T(8,128)(2,1)}, u32[]{:S(2)}) copy-start(bf16[1,288,128]{2,1,0:T(8,128)(2,1)} %get-tuple-element.70) | copy-start | bytes 221188
  74.9 8.2 %collective-permute-start.5 = (bf16[4,288,128]{2,1,0:T(8,128)(2,1)S(1)}, bf16[4,288,128]{2,1,0:T(8,128)(2,1)S(1)}, u32[]{:S(2)}, u32[]{:S(2)}) collective-permute-start(bf16[4,288,128]{2,1,0:T(8,128)(2,1)S(1)} %pad_maximum_fusion.4), channel_id=1, source_target_pairs={{0,1},{1,2},{2,3},{3,4},{4,5},{5,6},{6,7},{7,0},{8,9},{9,10},{10,1... | collective-permute-start | bytes 884744 | tf_op jit(solution)/shard_map/ppermute | solution.py:23
  75.7 9.4 %collective-permute-start.7 = (bf16[4,288,128]{2,1,0:T(8,128)(2,1)S(1)}, bf16[4,288,128]{2,1,0:T(8,128)(2,1)S(1)}, u32[]{:S(2)}, u32[]{:S(2)}) collective-permute-start(bf16[4,288,128]{2,1,0:T(8,128)(2,1)S(1)} %pad_maximum_fusion.6), channel_id=1, source_target_pairs={{0,7},{1,0},{2,1},{3,2},{4,3},{5,4},{6,5},{7,6},{8,15},{9,8},{10,9... | collective-permute-start | bytes 884744 | tf_op jit(solution)/shard_map/ppermute | solution.py:23
  76.4 25.5 %collective-permute-start.13 = (bf16[2,4,288,128]{3,2,1,0:T(8,128)(2,1)}, bf16[2,4,288,128]{3,2,1,0:T(8,128)(2,1)S(1)}, u32[]{:S(2)}, u32[]{:S(2)}) collective-permute-start(bf16[2,4,288,128]{3,2,1,0:T(8,128)(2,1)} %collective-permute-done.12), channel_id=1, source_target_pairs={{0,1},{1,2},{2,3},{3,4},{4,5},{5,6},{6,7},{7,0},{8,9},{9,10},{10,1... | collective-permute-start | bytes 1769480 | tf_op jit(solution)/shard_map/ppermute | solution.py:23
  78.7 11.3 %collective-permute-start.9 = (bf16[4,288,128]{2,1,0:T(8,128)(2,1)S(1)}, bf16[4,288,128]{2,1,0:T(8,128)(2,1)S(1)}, u32[]{:S(2)}, u32[]{:S(2)}) collective-permute-start(bf16[4,288,128]{2,1,0:T(8,128)(2,1)S(1)} %pad_maximum_fusion.8), channel_id=1, source_target_pairs={{0,2},{1,7},{2,4},{3,1},{4,6},{5,3},{6,0},{7,5},{8,10},{9,15},{10,... | collective-permute-start | bytes 884744 | tf_op jit(solution)/shard_map/ppermute | solution.py:23
  82.3 21.2 %collective-permute-start.15 = (bf16[2,4,288,128]{3,2,1,0:T(8,128)(2,1)}, bf16[2,4,288,128]{3,2,1,0:T(8,128)(2,1)S(1)}, u32[]{:S(2)}, u32[]{:S(2)}) collective-permute-start(bf16[2,4,288,128]{3,2,1,0:T(8,128)(2,1)} %collective-permute-done.14), channel_id=1, source_target_pairs={{0,7},{1,0},{2,1},{3,2},{4,3},{5,4},{6,5},{7,6},{8,15},{9,8},{10,9... | collective-permute-start | bytes 1769480 | tf_op jit(solution)/shard_map/ppermute | solution.py:23
  83.1 32.2 %collective-permute-start.17 = (bf16[2,4,288,128]{3,2,1,0:T(8,128)(2,1)S(1)}, bf16[2,4,288,128]{3,2,1,0:T(8,128)(2,1)S(1)}, u32[]{:S(2)}, u32[]{:S(2)}) collective-permute-start(bf16[2,4,288,128]{3,2,1,0:T(8,128)(2,1)S(1)} %collective-permute-done.16), channel_id=1, source_target_pairs={{0,2},{1,7},{2,4},{3,1},{4,6},{5,3},{6,0},{7,5},{8,10},{9,15},{10,... | collective-permute-start | bytes 1769480 | tf_op jit(solution)/shard_map/ppermute | solution.py:23
  85.1 32.5 %copy-start.1 = (bf16[4,288,128]{2,1,0:T(8,128)(2,1)}, bf16[4,288,128]{2,1,0:T(8,128)(2,1)S(1)}, u32[]{:S(2)}) copy-start(bf16[4,288,128]{2,1,0:T(8,128)(2,1)S(1)} %collective-permute-done.7.rest_2_) | copy-start | bytes 884740
  85.1 66.6 %collective-permute-start.6 = (bf16[4,288,128]{2,1,0:T(8,128)(2,1)}, bf16[4,288,128]{2,1,0:T(8,128)(2,1)S(1)}, u32[]{:S(2)}, u32[]{:S(2)}) collective-permute-start(bf16[4,288,128]{2,1,0:T(8,128)(2,1)} %pad_maximum_fusion.3), channel_id=1, source_target_pairs={{0,1},{1,2},{2,3},{3,4},{4,5},{5,6},{6,7},{7,0},{8,9},{9,10},{10,1... | collective-permute-start | bytes 884744 | tf_op jit(solution)/shard_map/ppermute | solution.py:23
  90.0 27.6 %copy-start.3 = (bf16[4,288,128]{2,1,0:T(8,128)(2,1)}, bf16[4,288,128]{2,1,0:T(8,128)(2,1)S(1)}, u32[]{:S(2)}) copy-start(bf16[4,288,128]{2,1,0:T(8,128)(2,1)S(1)} %collective-permute-done.9.rest_3_) | copy-start | bytes 884740
  90.0 64.2 %collective-permute-start.8 = (bf16[4,288,128]{2,1,0:T(8,128)(2,1)}, bf16[4,288,128]{2,1,0:T(8,128)(2,1)}, u32[]{:S(2)}, u32[]{:S(2)}) collective-permute-start(bf16[4,288,128]{2,1,0:T(8,128)(2,1)} %pad_maximum_fusion.5), channel_id=1, source_target_pairs={{0,7},{1,0},{2,1},{3,2},{4,3},{5,4},{6,5},{7,6},{8,15},{9,8},{10,9... | collective-permute-start | bytes 884744 | tf_op jit(solution)/shard_map/ppermute | solution.py:23
  118.3 9.4 %collective-permute-start.18 = (bf16[4,288,128]{2,1,0:T(8,128)(2,1)}, bf16[4,288,128]{2,1,0:T(8,128)(2,1)}, u32[]{:S(2)}, u32[]{:S(2)}) collective-permute-start(bf16[4,288,128]{2,1,0:T(8,128)(2,1)} %pad_maximum_fusion.12), channel_id=1, source_target_pairs={{0,8},{1,9},{2,10},{3,11},{4,12},{5,13},{6,14},{7,15},{8,16},{9,17... | collective-permute-start | bytes 884744 | tf_op jit(solution)/shard_map/ppermute | solution.py:29
  118.3 13.1 %collective-permute-start.20 = (bf16[4,288,128]{2,1,0:T(8,128)(2,1)}, bf16[4,288,128]{2,1,0:T(8,128)(2,1)}, u32[]{:S(2)}, u32[]{:S(2)}) collective-permute-start(bf16[4,288,128]{2,1,0:T(8,128)(2,1)} %pad_maximum_fusion.14), channel_id=1, source_target_pairs={{0,16},{1,17},{2,18},{3,19},{4,20},{5,21},{6,22},{7,23},{8,24},{9,... | collective-permute-start | bytes 884744 | tf_op jit(solution)/shard_map/ppermute | solution.py:29
  119.9 13.2 %collective-permute-start.22 = (bf16[4,288,128]{2,1,0:T(8,128)(2,1)}, bf16[4,288,128]{2,1,0:T(8,128)(2,1)}, u32[]{:S(2)}, u32[]{:S(2)}) collective-permute-start(bf16[4,288,128]{2,1,0:T(8,128)(2,1)} %pad_maximum_fusion.16), channel_id=1, source_target_pairs={{0,24},{1,25},{2,26},{3,27},{4,28},{5,29},{6,30},{7,31},{8,0},{9,1... | collective-permute-start | bytes 884744 | tf_op jit(solution)/shard_map/ppermute | solution.py:29
  123.1 10.0 %copy-start.2 = (bf16[4,288,128]{2,1,0:T(8,128)(2,1)S(1)}, bf16[4,288,128]{2,1,0:T(8,128)(2,1)}, u32[]{:S(2)}) copy-start(bf16[4,288,128]{2,1,0:T(8,128)(2,1)} %copy-done.1) | copy-start | bytes 884740
  123.1 10.0 %copy-start.4 = (bf16[4,288,128]{2,1,0:T(8,128)(2,1)S(1)}, bf16[4,288,128]{2,1,0:T(8,128)(2,1)}, u32[]{:S(2)}) copy-start(bf16[4,288,128]{2,1,0:T(8,128)(2,1)} %copy-done.3) | copy-start | bytes 884740
  127.7 26.4 %collective-permute-start.10 = (bf16[4,288,128]{2,1,0:T(8,128)(2,1)}, bf16[4,288,128]{2,1,0:T(8,128)(2,1)}, u32[]{:S(2)}, u32[]{:S(2)}) collective-permute-start(bf16[4,288,128]{2,1,0:T(8,128)(2,1)} %pad_maximum_fusion.7), channel_id=1, source_target_pairs={{0,2},{1,7},{2,4},{3,1},{4,6},{5,3},{6,0},{7,5},{8,10},{9,15},{10,... | collective-permute-start | bytes 884744 | tf_op jit(solution)/shard_map/ppermute | solution.py:23
  139.3 13.6 %copy-start.6 = (bf16[1,288,128]{2,1,0:T(8,128)(2,1)S(1)}, bf16[1,288,128]{2,1,0:T(8,128)(2,1)}, u32[]{:S(2)}) copy-start(bf16[1,288,128]{2,1,0:T(8,128)(2,1)} %get-tuple-element.72) | copy-start | bytes 221188
  139.3 13.6 %copy-start.7 = (bf16[1,288,128]{2,1,0:T(8,128)(2,1)S(1)}, bf16[1,288,128]{2,1,0:T(8,128)(2,1)}, u32[]{:S(2)}) copy-start(bf16[1,288,128]{2,1,0:T(8,128)(2,1)} %get-tuple-element.96) | copy-start | bytes 221188
  139.3 13.6 %copy-start.8 = (bf16[1,288,128]{2,1,0:T(8,128)(2,1)S(1)}, bf16[1,288,128]{2,1,0:T(8,128)(2,1)}, u32[]{:S(2)}) copy-start(bf16[1,288,128]{2,1,0:T(8,128)(2,1)} %get-tuple-element.88) | copy-start | bytes 221188
  139.3 13.6 %copy-start.9 = (bf16[1,288,128]{2,1,0:T(8,128)(2,1)S(1)}, bf16[1,288,128]{2,1,0:T(8,128)(2,1)}, u32[]{:S(2)}) copy-start(bf16[1,288,128]{2,1,0:T(8,128)(2,1)} %get-tuple-element.80) | copy-start | bytes 221188
  139.3 14.7 %copy-start.5 = (bf16[1,2,16,16,576]{4,3,1,0,2:T(8,128)(2,1)S(1)}, bf16[1,2,16,16,576]{4,3,1,0,2:T(8,128)(2,1)}, u32[]{:S(2)}) copy-start(bf16[1,2,16,16,576]{4,3,1,0,2:T(8,128)(2,1)} %get-tuple-element.32) | copy-start | bytes 1769476
  139.3 33.9 %all-to-all-start.1 = ((bf16[8,64,640]{2,1,0:T(8,128)(2,1)}), bf16[8,64,640]{2,1,0:T(8,128)(2,1)}, u32[]{:S(2)}, u32[]{:S(2)}) async-start(bf16[8,64,640]{2,1,0:T(8,128)(2,1)} %bitcast.97), calls=%async_computation.1 | async-start | bytes 1310720 | tf_op jit(solution)/shard_map/all_to_all | solution.py:194
  150.1 15.8 %collective-permute-start.19 = (bf16[4,288,128]{2,1,0:T(8,128)(2,1)S(1)}, bf16[4,288,128]{2,1,0:T(8,128)(2,1)S(1)}, u32[]{:S(2)}, u32[]{:S(2)}) collective-permute-start(bf16[4,288,128]{2,1,0:T(8,128)(2,1)S(1)} %pad_maximum_fusion.11), channel_id=1, source_target_pairs={{0,8},{1,9},{2,10},{3,11},{4,12},{5,13},{6,14},{7,15},{8,16},{9,17... | collective-permute-start | bytes 884744 | tf_op jit(solution)/shard_map/ppermute | solution.py:29
  150.1 15.8 %collective-permute-start.21 = (bf16[4,288,128]{2,1,0:T(8,128)(2,1)}, bf16[4,288,128]{2,1,0:T(8,128)(2,1)S(1)}, u32[]{:S(2)}, u32[]{:S(2)}) collective-permute-start(bf16[4,288,128]{2,1,0:T(8,128)(2,1)} %pad_maximum_fusion.13), channel_id=1, source_target_pairs={{0,16},{1,17},{2,18},{3,19},{4,20},{5,21},{6,22},{7,23},{8,24},{9,... | collective-permute-start | bytes 884744 | tf_op jit(solution)/shard_map/ppermute | solution.py:29
  151.7 14.8 %collective-permute-start.23 = (bf16[4,288,128]{2,1,0:T(8,128)(2,1)}, bf16[4,288,128]{2,1,0:T(8,128)(2,1)S(1)}, u32[]{:S(2)}, u32[]{:S(2)}) collective-permute-start(bf16[4,288,128]{2,1,0:T(8,128)(2,1)} %pad_maximum_fusion.15), channel_id=1, source_target_pairs={{0,24},{1,25},{2,26},{3,27},{4,28},{5,29},{6,30},{7,31},{8,0},{9,1... | collective-permute-start | bytes 884744 | tf_op jit(solution)/shard_map/ppermute | solution.py:29
  173.3 16.2 %all-to-all-start = ((bf16[8,64,640]{2,1,0:T(8,128)(2,1)}), bf16[8,64,640]{2,1,0:T(8,128)(2,1)S(1)}, u32[]{:S(2)}, u32[]{:S(2)}) async-start(bf16[8,64,640]{2,1,0:T(8,128)(2,1)} %bitcast.94), calls=%async_computation | async-start | bytes 1310720 | tf_op jit(solution)/shard_map/all_to_all | solution.py:203
  181.8 13.4 %collective-permute-start.24 = (bf16[2,64,640]{2,1,0:T(8,128)(2,1)S(1)}, bf16[2,64,640]{2,1,0:T(8,128)(2,1)S(1)}, u32[]{:S(2)}, u32[]{:S(2)}) collective-permute-start(bf16[2,64,640]{2,1,0:T(8,128)(2,1)S(1)} %pad_maximum_fusion.20), channel_id=1, source_target_pairs={{0,4},{1,5},{2,6},{3,7},{4,0},{5,1},{6,2},{7,3},{8,12},{9,13},{10,... | collective-permute-start | bytes 491528 | tf_op jit(solution)/shard_map/ppermute | solution.py:33
  (1 other events, 1.6 us)
Sparse Core Ops, SparseCore 0:
  58.6 23.2 all-gather.2
where the time goes:
time: 206 us; the launch traced here: 205 us
  starting transfers between devices  59.3 us (29%)
  waiting for transfers between devices  54.3 us (26%)
  local copies, waits for them, and re-layouts  45 us (22%)
  other arithmetic  16.8 us (8%)
  between operations  13.9 us (7%)
  Pallas kernels  13 us (6%)
  matrix products  3.16 us (2%)
    ppermute x9, waiting for transfers between devices, move_x(): lax.ppermute(a, 'req', [(x * NZ + z, (x + dx) % NX * NZ + z) for x in ran...  26.4 us
    ppermute x9, starting transfers between devices, move_z(): lax.ppermute(a, 'req', [(x * NZ + z, x * NZ + z_to(z, c)) for x in range(...  23.9 us
    ppermute x9, waiting for transfers between devices, move_z(): lax.ppermute(a, 'req', [(x * NZ + z, x * NZ + z_to(z, c)) for x in range(...  15.7 us
    gather x4, local copies, waits for them, and re-layouts, shards(): by_x = [blocks[take_x[:, d]] for d in range(NX)]  14.4 us
    gather x4, local copies, waits for them, and re-layouts, shards(): away = [blocks[take_z[:, :, c]] for c in range(NC)]  14.3 us
    pallas_call x2, Pallas kernels, attend(): pl.pallas_call(functools.partial(attend_kernel, fresh, scale), in_specs=[...  13 us
    ppermute x9, starting transfers between devices, move_x(): lax.ppermute(a, 'req', [(x * NZ + z, (x + dx) % NX * NZ + z) for x in ran...  9.72 us
    all_to_all x1, starting transfers between devices, shards(): lax.all_to_all(part_f.reshape(heads, -1, latent + LANES), ('role', 'ctx')...  9.68 us
  transfers between devices with their start and end apart: 28, of which 10 were waited for; matrix products, arithmetic and copies ran while one was open for 28% of the time, Pallas kernels for 6%

commit v1 on v0

--- a/solution.py
+++ b/solution.py
@@ -17,10 +17,12 @@
     return (z + (0, 1, -1, 2 if z % 2 == 0 else -2)[c]) % NZ
 
 
-def move_z(a, c):
-    if c == 0:
+def move_z(a, c, flip=0):
+    if c == 0 and not flip:
         return a
-    return lax.ppermute(a, "req", [(x * NZ + z, x * NZ + z_to(z, c)) for x in range(NX) for z in range(NZ)])
+    n = NX * NZ
+    pairs = [(r * n + x * NZ + z, (r ^ flip) * n + x * NZ + z_to(z, c)) for r in range(2) for x in range(NX) for z in range(NZ)]
+    return lax.ppermute(a, ("role", "req"), pairs)
 
 
 def move_x(a, dx):
@@ -39,6 +41,47 @@
 
 def lookup(slots, values, want):
     return jnp.sum(jnp.where(slots == want[..., None], values, 0), axis=-1)
+
+
+def pick_kernel(idx_ref, k_ref, *outs):
+    for o, out in enumerate(outs):
+        for g in range(2):
+            for i in range(4):
+                out[g, i] = k_ref[idx_ref[o * 8 + g * 4 + i]]
+
+
+def pick(k, idx):
+    vm = pl.BlockSpec(memory_space=pltpu.VMEM)
+    block = k.shape[1:]
+    return pl.pallas_call(
+        pick_kernel,
+        in_specs=[pl.BlockSpec(memory_space=pltpu.SMEM), vm],
+        out_specs=[vm] * 8,
+        out_shape=[jax.ShapeDtypeStruct((2, 4, *block), k.dtype)] * 8,
+        compiler_params=pltpu.CompilerParams(vmem_limit_bytes=32 * 1024 * 1024),
+        cost_estimate=pl.CostEstimate(flops=0, bytes_accessed=2 * 64 * block[0] * block[1] * 2, transcendentals=0),
+    )(idx, k)
+
+
+def regroup_kernel(*refs):
+    for g in range(2):
+        for i in range(4):
+            for j in range(4):
+                refs[4 + g * 4 + i][j] = refs[j][g, i]
+
+
+def regroup(parts):
+    vm = pl.BlockSpec(memory_space=pltpu.VMEM)
+    shape = parts[0].shape[1:]
+    size = shape[0] * shape[1] * shape[2]
+    return pl.pallas_call(
+        regroup_kernel,
+        in_specs=[vm] * 4,
+        out_specs=[vm] * 8,
+        out_shape=[jax.ShapeDtypeStruct(shape, parts[0].dtype)] * 8,
+        compiler_params=pltpu.CompilerParams(vmem_limit_bytes=32 * 1024 * 1024),
+        cost_estimate=pl.CostEstimate(flops=0, bytes_accessed=2 * 8 * size * 2, transcendentals=0),
+    )(*parts)
 
 
 def attend_kernel(fresh, scale, scal_ref, q_ref, *rest):
@@ -134,20 +177,11 @@
     return lax.optimization_barrier((v, dep))[0]
 
 
-def exchange(by_x, away):
-    got_x, got_z = [None] * 4, [None] * 4
-    for i in (1, 2, 3, 0):
-        got_z[i] = swap_role(away[i])
-    for i in (1, 2, 3, 0):
-        got_x[i] = move_x(by_x[i], i)
-        got_z[i] = move_z(got_z[i], i)
-    sides = []
-    mine, recv = [None] * 4, [None] * 4
-    for g in range(2):
-        mine = [move_z(after(jnp.stack([got_x[d][g, c] for d in range(4)]), mine[c]), c) for c in range(4)]
-        recv = [move_x(after(jnp.stack([got_z[c][g, d] for c in range(4)]), recv[d]), d) for d in range(4)]
-        sides.append((mine, recv))
-    return sides
+def second(parts, move):
+    parts = regroup(parts)
+    far = [move(parts[i], i) for i in range(4)]
+    near = [move(after(parts[4 + i], far[i]), i) for i in range(4)]
+    return far, near
 
 
 def shards(cache, lengths, request_decode_slot, q_nope, q_rope, new_latent, w_key, value_up_weight):
@@ -168,8 +202,15 @@
     owner = (x + dx) % NX * NZ + (z + move + far + NZ) % NZ
     take_x = lookup(request_decode_slot, ids, 2 * owner + role)
     take_z = lookup(request_decode_slot, ids, 2 * owner + 1 - role)
-    by_x = [blocks[take_x[:, d]] for d in range(NX)]
-    away = [blocks[take_z[:, :, c]] for c in range(NC)]
+    index = jnp.concatenate([jnp.moveaxis(take_z, 2, 0).reshape(-1), jnp.moveaxis(take_x, 1, 0).reshape(-1)])
+    picked = pick(blocks, index)
+    got_z = [None, move_z(picked[1], 1, 1), move_z(picked[2], 2, 1), None]
+    got_x = [picked[4], move_x(picked[5], 1), None, move_x(picked[7], 3)]
+    got_z[3] = move_z(after(picked[3], got_z[1]), 3, 1)
+    got_x[2] = move_x(after(picked[6], got_x[1]), 2)
+    got_z[0] = move_z(after(picked[0], got_z[2]), 0, 1)
+    mine_f, mine_n = second(got_x, move_z)
+    recv_f, recv_n = second(got_z, move_x)
     source = (x - dx + NX) % NX * NZ + (z - move + NZ) % NZ
     base = ctx * (NX * NZ * LANES) + source * LANES
 
@@ -178,6 +219,7 @@
         length = lookup(request_decode_slot, lengths, want)
         return jnp.concatenate([(length - base).reshape(-1), role[None], ctx[None]]).astype(jnp.int32)
 
+    q_nope = after(q_nope, picked[1])
     queries = q_nope.reshape(req_dev, steps, heads_dev, nope_dim)
     absorbed = jnp.einsum("bshd,hdk->bshk", queries, w_key, preferred_element_type=jnp.float32).astype(jnp.bfloat16)
     own = jnp.concatenate([absorbed, q_rope.reshape(req_dev, steps, heads_dev, rope_dim)], axis=3)
@@ -188,8 +230,7 @@
     every = lax.all_gather(pair, "ctx", axis=2, tiled=False)
     every = every.reshape(2, -1, latent + rope_dim)
 
-    (mine_f, recv_f), (mine_n, recv_n) = exchange(by_x, away)
-    part_f = attend(scalars(4), every[1], mine_f, recv_f, None, latent, scale)
+    part_f = attend(scalars(4), after(every[1], (mine_n[1], recv_n[1])), mine_f, recv_f, None, latent, scale)
     heads = 2 * lax.axis_size("ctx")
     part_f = lax.all_to_all(part_f.reshape(heads, -1, latent + LANES), ("role", "ctx"), 0, 0, tiled=True)
     rows_f, lse_f = merge(part_f.reshape(2, -1, *part_f.shape[1:]), latent, 1)

time: 206 us -> 195 us (0.947)
  the two profiles are of different devices: /device:TPU:41 before, /device:TPU:1 now
where the time goes in v1:
time: 195 us; the launch traced here: 194 us
  waiting for transfers between devices  65.6 us (34%)
  starting transfers between devices  53 us (27%)
  local copies, waits for them, and re-layouts  31 us (16%)
  Pallas kernels  18.6 us (10%)
  between operations  13.7 us (7%)
  other arithmetic  9.92 us (5%)
  matrix products  2.4 us (1%)
    ppermute x10, waiting for transfers between devices, move_z(): return lax.ppermute(a, ('role', 'req'), pairs)  36.7 us
    unnamed x78, local copies, waits for them, and re-layouts  23.6 us
    ppermute x9, starting transfers between devices, move_x(): lax.ppermute(a, 'req', [(x * NZ + z, (x + dx) % NX * NZ + z) for x in ran...  15.2 us
    ppermute x10, starting transfers between devices, move_z(): return lax.ppermute(a, ('role', 'req'), pairs)  15.1 us
    ppermute x9, waiting for transfers between devices, move_x(): lax.ppermute(a, 'req', [(x * NZ + z, (x + dx) % NX * NZ + z) for x in ran...  15 us
    pallas_call x2, Pallas kernels, attend(): pl.pallas_call(functools.partial(attend_kernel, fresh, scale), in_specs=[...  12.6 us
    ppermute x2, starting transfers between devices, move_far(): lax.ppermute(a, 'req', [(x * NZ + z, x * NZ + (z + 4) % NZ) for x in rang...  10.6 us
    ppermute x2, waiting for transfers between devices, move_far(): lax.ppermute(a, 'req', [(x * NZ + z, x * NZ + (z + 4) % NZ) for x in rang...  8.29 us
  transfers between devices with their start and end apart: 25, of which 10 were waited for; matrix products, arithmetic and copies ran while one was open for 7% of the time, Pallas kernels for 5%

profile of v1, /device:TPU:1, one launch (start us, length us, event | category | flops | bytes accessed | tf_op | source)
XLA Modules:
  0.0 194.2 jit_solution(12786951963402763598)
XLA Ops:
  6.6 0.9 and_select_fusion
  7.5 1.1 select_reduce_fusion.1
  9.0 2.3 %copy-done.1 = bf16[64,128,288]{1,2,0:T(8,128)(2,1)S(1)} copy-done((bf16[64,128,288]{1,2,0:T(8,128)(2,1)S(1)}, bf16[64,128,288]{1,2,0:T(8,128)(2,1)}, u32[]{:S(2)}) %copy-start.1) | copy-done | bytes 4718616
  11.3 1.9 shard_map.91
  14.0 0.8 copy-done.3
  18.0 7.8 %collective-permute-start = (bf16[2,4,16,576]{3,1,0,2:T(4,128)(2,1)S(1)}, bf16[2,4,16,576]{3,1,0,2:T(4,128)(2,1)S(1)}, u32[]{:S(2)}, u32[]{:S(2)}) collective-permute-start(bf16[2,4,16,576]{3,1,0,2:T(4,128)(2,1)S(1)} %get-tuple-element.90), channel_id=1, source_target_pairs={{0,4},{1,5},{2,6},{3,7},{4,0},{5,1},{6,2},{7,3},{8,12},{9,13},{10,... | collective-permute-start | bytes 442376 | tf_op jit(solution)/shard_map/ppermute | solution.py:35
  25.8 3.4 %collective-permute-done = bf16[2,4,16,576]{3,1,0,2:T(4,128)(2,1)S(1)} collective-permute-done((bf16[2,4,16,576]{3,1,0,2:T(4,128)(2,1)S(1)}, bf16[2,4,16,576]{3,1,0,2:T(4,128)(2,1)S(1)}, u32[]{:S(2)}, u32[]{:S(2)}) %collective-permute-start) | collective-permute-done | bytes 147488 | tf_op jit(solution)/shard_map/ppermute | solution.py:35
  29.4 2.0 %collective-permute-start.1 = (bf16[2,4,16,576]{3,1,2,0:T(4,128)(2,1)S(1)}, bf16[2,4,16,576]{3,1,2,0:T(4,128)(2,1)S(1)}, u32[]{:S(2)}, u32[]{:S(2)}) collective-permute-start(bf16[2,4,16,576]{3,1,2,0:T(4,128)(2,1)S(1)} %fusion.17), channel_id=1, source_target_pairs={{0,128},{128,0},{1,129},{129,1},{2,130},{130,2},{3,131},{131,3},{4... | collective-permute-start | bytes 442376 | tf_op jit(solution)/shard_map/ppermute | solution.py:39
  31.4 3.9 %collective-permute-start.13 = (bf16[2,4,288,128]{3,2,1,0:T(8,128)(2,1)}, bf16[2,4,288,128]{3,2,1,0:T(8,128)(2,1)}, u32[]{:S(2)}, u32[]{:S(2)}) collective-permute-start(bf16[2,4,288,128]{3,2,1,0:T(8,128)(2,1)} %get-tuple-element.42), channel_id=1, source_target_pairs={{0,129},{1,130},{2,131},{3,132},{4,133},{5,134},{6,135},{7,128},{8... | collective-permute-start | bytes 1769480 | tf_op jit(solution)/shard_map/ppermute | solution.py:25
  35.2 2.6 %collective-permute-start.11 = (bf16[2,4,288,128]{3,2,1,0:T(8,128)(2,1)}, bf16[2,4,288,128]{3,2,1,0:T(8,128)(2,1)}, u32[]{:S(2)}, u32[]{:S(2)}) collective-permute-start(bf16[2,4,288,128]{3,2,1,0:T(8,128)(2,1)} %get-tuple-element.62), channel_id=1, source_target_pairs={{0,135},{1,128},{2,129},{3,130},{4,131},{5,132},{6,133},{7,134},{8... | collective-permute-start | bytes 1769480 | tf_op jit(solution)/shard_map/ppermute | solution.py:25
  39.2 1.3 collective-permute-start.2
  40.5 10.8 %collective-permute-done.11.refs_2_ = bf16[2,4,288,128]{3,2,1,0:T(8,128)(2,1)} collective-permute-done((bf16[2,4,288,128]{3,2,1,0:T(8,128)(2,1)}, bf16[2,4,288,128]{3,2,1,0:T(8,128)(2,1)}, u32[]{:S(2)}, u32[]{:S(2)}) %collective-permute-start.11) | collective-permute-done | bytes 589856 | tf_op jit(solution)/shard_map/ppermute | solution.py:25
  51.9 2.6 %collective-permute-start.14 = (bf16[2,4,288,128]{3,2,1,0:T(8,128)(2,1)}, bf16[2,4,288,128]{3,2,1,0:T(8,128)(2,1)S(1)}, u32[]{:S(2)}, u32[]{:S(2)}) collective-permute-start(bf16[2,4,288,128]{3,2,1,0:T(8,128)(2,1)} %copy-done.4), channel_id=1, source_target_pairs={{0,130},{1,135},{2,132},{3,129},{4,134},{5,131},{6,128},{7,133},{8... | collective-permute-start | bytes 1769480 | tf_op jit(solution)/shard_map/ppermute | solution.py:25
  54.5 2.5 %collective-permute-start.4 = (bf16[2,4,288,128]{3,2,1,0:T(8,128)(2,1)}, bf16[2,4,288,128]{3,2,1,0:T(8,128)(2,1)}, u32[]{:S(2)}, u32[]{:S(2)}) collective-permute-start(bf16[2,4,288,128]{3,2,1,0:T(8,128)(2,1)} %copy-done.3), channel_id=1, source_target_pairs={{0,24},{1,25},{2,26},{3,27},{4,28},{5,29},{6,30},{7,31},{8,0},{9,1... | collective-permute-start | bytes 1769480 | tf_op jit(solution)/shard_map/ppermute | solution.py:31
  57.5 12.2 %collective-permute-done.14.refs_3_ = bf16[2,4,288,128]{3,2,1,0:T(8,128)(2,1)S(1)} collective-permute-done((bf16[2,4,288,128]{3,2,1,0:T(8,128)(2,1)}, bf16[2,4,288,128]{3,2,1,0:T(8,128)(2,1)S(1)}, u32[]{:S(2)}, u32[]{:S(2)}) %collective-permute-start.14) | collective-permute-done | bytes 589856 | tf_op jit(solution)/shard_map/ppermute | solution.py:25
  69.7 2.1 %shard_map.93 = (bf16[4,288,128]{2,1,0:T(8,128)(2,1)S(1)}, bf16[4,288,128]{2,1,0:T(8,128)(2,1)}, bf16[4,288,128]{2,1,0:T(8,128)(2,1)S(1)}, bf16[4,288,128]{2,1,0...) custom-call(bf16[2,4,288,128]{3,2,1,0:T(8,128)(2,1)S(1)} %collective, ...), custom_call_target="tpu_custom_call" | custom-call | bytes 4718592 | tf_op jit(solution)/shard_map/pallas_call | solution.py:77
  77.7 4.9 %collective-permute-done.4.refs_3_ = bf16[2,4,288,128]{3,2,1,0:T(8,128)(2,1)} collective-permute-done((bf16[2,4,288,128]{3,2,1,0:T(8,128)(2,1)}, bf16[2,4,288,128]{3,2,1,0:T(8,128)(2,1)}, u32[]{:S(2)}, u32[]{:S(2)}) %collective-permute-start.4) | collective-permute-done | bytes 589856 | tf_op jit(solution)/shard_map/ppermute | solution.py:31
  82.5 2.0 %shard_map.92 = (bf16[4,288,128]{2,1,0:T(8,128)(2,1)S(1)}, bf16[4,288,128]{2,1,0:T(8,128)(2,1)}, bf16[4,288,128]{2,1,0:T(8,128)(2,1)S(1)}, bf16[4,288,128]{2,1,0...) custom-call(bf16[2,4,288,128]{3,2,1,0:T(8,128)(2,1)S(1)} %get-tuple-, ...), custom_call_target="tpu_custom_call" | custom-call | bytes 4718592 | tf_op jit(solution)/shard_map/pallas_call | solution.py:77
  89.6 3.2 %collective-permute-start.16 = (bf16[4,288,128]{2,1,0:T(8,128)(2,1)}, bf16[4,288,128]{2,1,0:T(8,128)(2,1)S(1)}, u32[]{:S(2)}, u32[]{:S(2)}) collective-permute-start(bf16[4,288,128]{2,1,0:T(8,128)(2,1)} %get-tuple-element.71), channel_id=1, source_target_pairs={{0,8},{1,9},{2,10},{3,11},{4,12},{5,13},{6,14},{7,15},{8,16},{9,17... | collective-permute-start | bytes 884744 | tf_op jit(solution)/shard_map/ppermute | solution.py:31
  92.8 1.4 fusion.25
  94.3 2.8 %collective-permute-start.17 = (bf16[4,288,128]{2,1,0:T(8,128)(2,1)}, bf16[4,288,128]{2,1,0:T(8,128)(2,1)S(1)}, u32[]{:S(2)}, u32[]{:S(2)}) collective-permute-start(bf16[4,288,128]{2,1,0:T(8,128)(2,1)} %copy-done.16), channel_id=1, source_target_pairs={{0,16},{1,17},{2,18},{3,19},{4,20},{5,21},{6,22},{7,23},{8,24},{9,... | collective-permute-start | bytes 884744 | tf_op jit(solution)/shard_map/ppermute | solution.py:31
  97.1 1.4 collective-permute-start.7
  99.4 1.4 collective-permute-start.9
  101.5 1.5 collective-permute-start.6
  104.1 2.3 %fusion.39 = (bf16[1,2,16,16,576]{4,3,1,0,2:T(8,128)(2,1)S(1)}, bf16[1,2,16,16,576]{4,3,1,0,2:T(8,128)(2,1)}) fusion(bf16[2,2,16,16,576]{4,3,1,0,2:T(8,128)(2,1)} %all-gather.3.cloned.1.call-done), kind=kLoop, calls=%fused_computation.87 | loop fusion | bytes 2359296 | tf_op jit(solution)/shard_map/slice | solution.py:233
  106.4 10.4 %collective-permute-done.6.rest_1_ = bf16[4,288,128]{2,1,0:T(8,128)(2,1)S(1)} collective-permute-done((bf16[4,288,128]{2,1,0:T(8,128)(2,1)}, bf16[4,288,128]{2,1,0:T(8,128)(2,1)S(1)}, u32[]{:S(2)}, u32[]{:S(2)}) %collective-permute-start.6) | collective-permute-done | bytes 294944 | tf_op jit(solution)/shard_map/ppermute | solution.py:25
  118.4 1.0 copy-done.26
  119.3 1.0 copy-done.30
  120.3 1.0 copy-done.33
  121.2 6.3 %shard_map.95 = bf16[512,640]{1,0:T(8,128)(2,1)} custom-call(s32[18]{0:T(128)S(1)} %add_add_fusion.1.scal_ref, bf16[512,576]{1,0:T(8,128)(2,1)S(1)} %bitcast.87, bf16[4,288,128]{2,1,0:T(8,128)(2,1)S(1)} %copy-done.26, bf16[4,288,128]{2,1,0:T(8,128)(2,1)S(1)} %copy-done.30, bf16[4,288,128]{2,1,0:T(8,128)(2,1)} %collective-permute-done.7.rest_2_, ...), custom_call_target="tpu_custom_call" | custom-call | flops 2281701376 | bytes 3473408 | tf_op jit(solution)/shard_map/pallas_call | solution.py:154
  127.6 5.2 %all-to-all-start.1 = ((bf16[8,64,640]{2,1,0:T(8,128)(2,1)}), bf16[8,64,640]{2,1,0:T(8,128)(2,1)}, u32[]{:S(2)}, u32[]{:S(2)}) async-start(bf16[8,64,640]{2,1,0:T(8,128)(2,1)} %bitcast.23), calls=%async_computation.1 | async-start | bytes 1310720 | tf_op jit(solution)/shard_map/all_to_all | solution.py:235
  132.7 1.6 select_bitcast_fusion.2
  134.4 0.9 pad.4.rest_8_
  135.4 3.8 %collective-permute-start.20 = (bf16[4,288,128]{2,1,0:T(8,128)(2,1)S(1)}, bf16[4,288,128]{2,1,0:T(8,128)(2,1)S(1)}, u32[]{:S(2)}, u32[]{:S(2)}) collective-permute-start(bf16[4,288,128]{2,1,0:T(8,128)(2,1)S(1)} %copy-done.12), channel_id=1, source_target_pairs={{0,24},{1,25},{2,26},{3,27},{4,28},{5,29},{6,30},{7,31},{8,0},{9,1... | collective-permute-start | bytes 884744 | tf_op jit(solution)/shard_map/ppermute | solution.py:31
  139.4 1.2 collective-permute-start.8
  140.7 1.1 copy.54
  141.8 10.1 %collective-permute-done.20.rest_7_ = bf16[4,288,128]{2,1,0:T(8,128)(2,1)S(1)} collective-permute-done((bf16[4,288,128]{2,1,0:T(8,128)(2,1)S(1)}, bf16[4,288,128]{2,1,0:T(8,128)(2,1)S(1)}, u32[]{:S(2)}, u32[]{:S(2)}) %collective-permute-start.20) | collective-permute-done | bytes 294944 | tf_op jit(solution)/shard_map/ppermute | solution.py:31
  151.9 3.0 %collective-permute-done.8.rest_2_ = bf16[4,288,128]{2,1,0:T(8,128)(2,1)S(1)} collective-permute-done((bf16[4,288,128]{2,1,0:T(8,128)(2,1)}, bf16[4,288,128]{2,1,0:T(8,128)(2,1)S(1)}, u32[]{:S(2)}, u32[]{:S(2)}) %collective-permute-start.8) | collective-permute-done | bytes 294944 | tf_op jit(solution)/shard_map/ppermute | solution.py:25
  154.9 1.0 copy-done.22
  155.9 1.0 copy-done.24
  156.9 6.3 %shard_map.94 = bf16[512,640]{1,0:T(8,128)(2,1)} custom-call(s32[18]{0:T(128)S(1)} %add_add_fusion.scal_ref, bf16[512,576]{1,0:T(8,128)(2,1)S(1)} %bitcast.88, bf16[4,288,128]{2,1,0:T(8,128)(2,1)S(1)} %copy-done.18, bf16[4,288,128]{2,1,0:T(8,128)(2,1)S(1)} %copy-done.24, bf16[4,288,128]{2,1,0:T(8,128)(2,1)S(1)} %collective-permute-done.8.rest_2_, ...), custom_call_target="tpu_custom_call" | custom-call | flops 2281701376 | bytes 3473408 | tf_op jit(solution)/shard_map/pallas_call | solution.py:154
  163.2 5.0 %all-to-all-start = ((bf16[8,64,640]{2,1,0:T(8,128)(2,1)}), bf16[8,64,640]{2,1,0:T(8,128)(2,1)S(1)}, u32[]{:S(2)}, u32[]{:S(2)}) async-start(bf16[8,64,640]{2,1,0:T(8,128)(2,1)} %bitcast.20), calls=%async_computation | async-start | bytes 1310720 | tf_op jit(solution)/shard_map/all_to_all | solution.py:244
  168.1 1.0 convert_reduce_fusion.1
  169.4 1.2 multiply_reduce_fusion.1
  170.8 2.8 %collective-permute-start.21 = (bf16[2,64,640]{2,1,0:T(8,128)(2,1)S(1)}, bf16[2,64,640]{2,1,0:T(8,128)(2,1)S(1)}, u32[]{:S(2)}, u32[]{:S(2)}) collective-permute-start(bf16[2,64,640]{2,1,0:T(8,128)(2,1)S(1)} %pad_maximum_fusion.4), channel_id=1, source_target_pairs={{0,4},{1,5},{2,6},{3,7},{4,0},{5,1},{6,2},{7,3},{8,12},{9,13},{10,... | collective-permute-start | bytes 491528 | tf_op jit(solution)/shard_map/ppermute | solution.py:35
  173.5 5.7 %all-to-all-done = bf16[8,64,640]{2,1,0:T(8,128)(2,1)S(1)} async-done(((bf16[8,64,640]{2,1,0:T(8,128)(2,1)}), bf16[8,64,640]{2,1,0:T(8,128)(2,1)S(1)}, u32[]{:S(2)}, u32[]{:S(2)}) %all-to-all-start) | async-done | bytes 655392 | tf_op jit(solution)/shard_map/all_to_all | solution.py:244
  179.2 4.9 %collective-permute-done.21 = bf16[2,64,640]{2,1,0:T(8,128)(2,1)S(1)} collective-permute-done((bf16[2,64,640]{2,1,0:T(8,128)(2,1)S(1)}, bf16[2,64,640]{2,1,0:T(8,128)(2,1)S(1)}, u32[]{:S(2)}, u32[]{:S(2)}) %collective-permute-start.21) | collective-permute-done | bytes 163872 | tf_op jit(solution)/shard_map/ppermute | solution.py:35
  184.7 2.0 %fusion.13 = bf16[16,2,1,4,128]{4,3,2,1,0:T(4,128)(2,1)S(1)} fusion(bf16[16,512,128]{2,1,0:T(8,128)(2,1)} %param.16, bf16[2,4,16,512]{3,2,1,0:T(8,128)(2,1)S(1)} %divide_convert_fusion), kind=kOutput, calls=%fused_computation.8 | convolution fusion | flops 16793600 | bytes 2260992 | tf_op jit(solution)/shard_map/bshk,hkv->bshv/dot_general | solution.py:248
  (136 shorter events, 24.1 us)
Async XLA Ops:
  6.5 10.9 %copy-start = (bf16[16,128,512]{2,1,0:T(8,128)(2,1)S(1)}, bf16[16,128,512]{2,1,0:T(8,128)(2,1)}, u32[]{:S(2)}) copy-start(bf16[16,128,512]{2,1,0:T(8,128)(2,1)} %param.15) | copy-start | bytes 6291460
  6.5 97.6 %all-gather.3.cloned.1.call-start = ((), (), s32[]{:S(2)}) async-start(), calls=%async_computation.2 | async-start | bytes 1638400 | tf_op jit(solution)/shard_map/all_gather | solution.py:230
  9.0 2.3 %copy-start.1 = (bf16[64,128,288]{1,2,0:T(8,128)(2,1)S(1)}, bf16[64,128,288]{1,2,0:T(8,128)(2,1)}, u32[]{:S(2)}) copy-start(bf16[64,128,288]{1,2,0:T(8,128)(2,1)} %param.9) | copy-start | bytes 14155780
  11.3 6.0 %copy-start.35 = (bf16[2,4,1024]{2,1,0:T(4,128)(2,1)S(1)}, bf16[2,4,1024]{2,1,0:T(4,128)(2,1)}, u32[]{:S(2)}) copy-start(bf16[2,4,1024]{2,1,0:T(4,128)(2,1)} %param.13) | copy-start | bytes 49156
  11.3 6.1 %copy-start.34 = (bf16[2,4,2048]{2,1,0:T(4,128)(2,1)S(1)}, bf16[2,4,2048]{2,1,0:T(4,128)(2,1)}, u32[]{:S(2)}) copy-start(bf16[2,4,2048]{2,1,0:T(4,128)(2,1)} %param.12) | copy-start | bytes 98308
  13.2 0.8 copy-start.2
  14.0 0.8 copy-start.3
  14.9 0.8 copy-start.4
  15.7 0.8 copy-start.5
  16.5 0.8 copy-start.6
  18.0 11.2 %collective-permute-start = (bf16[2,4,16,576]{3,1,0,2:T(4,128)(2,1)S(1)}, bf16[2,4,16,576]{3,1,0,2:T(4,128)(2,1)S(1)}, u32[]{:S(2)}, u32[]{:S(2)}) collective-permute-start(bf16[2,4,16,576]{3,1,0,2:T(4,128)(2,1)S(1)} %get-tuple-element.90), channel_id=1, source_target_pairs={{0,4},{1,5},{2,6},{3,7},{4,0},{5,1},{6,2},{7,3},{8,12},{9,13},{10,... | collective-permute-start | bytes 442376 | tf_op jit(solution)/shard_map/ppermute | solution.py:35
  29.4 8.4 %collective-permute-start.1 = (bf16[2,4,16,576]{3,1,2,0:T(4,128)(2,1)S(1)}, bf16[2,4,16,576]{3,1,2,0:T(4,128)(2,1)S(1)}, u32[]{:S(2)}, u32[]{:S(2)}) collective-permute-start(bf16[2,4,16,576]{3,1,2,0:T(4,128)(2,1)S(1)} %fusion.17), channel_id=1, source_target_pairs={{0,128},{128,0},{1,129},{129,1},{2,130},{130,2},{3,131},{131,3},{4... | collective-permute-start | bytes 442376 | tf_op jit(solution)/shard_map/ppermute | solution.py:39
  31.4 20.5 %collective-permute-start.13 = (bf16[2,4,288,128]{3,2,1,0:T(8,128)(2,1)}, bf16[2,4,288,128]{3,2,1,0:T(8,128)(2,1)}, u32[]{:S(2)}, u32[]{:S(2)}) collective-permute-start(bf16[2,4,288,128]{3,2,1,0:T(8,128)(2,1)} %get-tuple-element.42), channel_id=1, source_target_pairs={{0,129},{1,130},{2,131},{3,132},{4,133},{5,134},{6,135},{7,128},{8... | collective-permute-start | bytes 1769480 | tf_op jit(solution)/shard_map/ppermute | solution.py:25
  35.2 16.0 %collective-permute-start.11 = (bf16[2,4,288,128]{3,2,1,0:T(8,128)(2,1)}, bf16[2,4,288,128]{3,2,1,0:T(8,128)(2,1)}, u32[]{:S(2)}, u32[]{:S(2)}) collective-permute-start(bf16[2,4,288,128]{3,2,1,0:T(8,128)(2,1)} %get-tuple-element.62), channel_id=1, source_target_pairs={{0,135},{1,128},{2,129},{3,130},{4,131},{5,132},{6,133},{7,134},{8... | collective-permute-start | bytes 1769480 | tf_op jit(solution)/shard_map/ppermute | solution.py:25
  38.1 38.8 %copy-start.37 = (s32[64]{0:T(128)S(1)}, s32[64]{0:T(128)}, u32[]{:S(2)}) copy-start(s32[64]{0:T(128)} %param.11) | copy-start | bytes 772
  38.1 38.8 %copy-start.38 = (s32[64]{0:T(128)S(1)}, s32[64]{0:T(128)}, u32[]{:S(2)}) copy-start(s32[64]{0:T(128)} %param.10) | copy-start | bytes 772
  39.2 17.8 %collective-permute-start.2 = (bf16[2,4,288,128]{3,2,1,0:T(8,128)(2,1)}, bf16[2,4,288,128]{3,2,1,0:T(8,128)(2,1)S(1)}, u32[]{:S(2)}, u32[]{:S(2)}) collective-permute-start(bf16[2,4,288,128]{3,2,1,0:T(8,128)(2,1)} %copy-done.6), channel_id=1, source_target_pairs={{0,8},{1,9},{2,10},{3,11},{4,12},{5,13},{6,14},{7,15},{8,16},{9,17... | collective-permute-start | bytes 1769480 | tf_op jit(solution)/shard_map/ppermute | solution.py:31
  51.2 6.3 %collective-permute-start.12 = (bf16[2,4,288,128]{3,2,1,0:T(8,128)(2,1)}, bf16[2,4,288,128]{3,2,1,0:T(8,128)(2,1)S(1)}, u32[]{:S(2)}, u32[]{:S(2)}) collective-permute-start(bf16[2,4,288,128]{3,2,1,0:T(8,128)(2,1)} %copy-done.5), channel_id=1, source_target_pairs={{0,128},{1,129},{2,130},{3,131},{4,132},{5,133},{6,134},{7,135},{8... | collective-permute-start | bytes 1769480 | tf_op jit(solution)/shard_map/ppermute | solution.py:25
  51.9 17.9 %collective-permute-start.14 = (bf16[2,4,288,128]{3,2,1,0:T(8,128)(2,1)}, bf16[2,4,288,128]{3,2,1,0:T(8,128)(2,1)S(1)}, u32[]{:S(2)}, u32[]{:S(2)}) collective-permute-start(bf16[2,4,288,128]{3,2,1,0:T(8,128)(2,1)} %copy-done.4), channel_id=1, source_target_pairs={{0,130},{1,135},{2,132},{3,129},{4,134},{5,131},{6,128},{7,133},{8... | collective-permute-start | bytes 1769480 | tf_op jit(solution)/shard_map/ppermute | solution.py:25
  54.5 28.1 %collective-permute-start.4 = (bf16[2,4,288,128]{3,2,1,0:T(8,128)(2,1)}, bf16[2,4,288,128]{3,2,1,0:T(8,128)(2,1)}, u32[]{:S(2)}, u32[]{:S(2)}) collective-permute-start(bf16[2,4,288,128]{3,2,1,0:T(8,128)(2,1)} %copy-done.3), channel_id=1, source_target_pairs={{0,24},{1,25},{2,26},{3,27},{4,28},{5,29},{6,30},{7,31},{8,0},{9,1... | collective-permute-start | bytes 1769480 | tf_op jit(solution)/shard_map/ppermute | solution.py:31
  57.0 37.3 %copy-start.36 = (bf16[2,4,576]{2,1,0:T(4,128)(2,1)S(1)}, bf16[2,4,576]{2,1,0:T(4,128)(2,1)}, u32[]{:S(2)}) copy-start(bf16[2,4,576]{2,1,0:T(4,128)(2,1)} %param.14) | copy-start | bytes 27652
  57.0 25.6 %collective-permute-start.3 = (bf16[2,4,288,128]{3,2,1,0:T(8,128)(2,1)}, bf16[2,4,288,128]{3,2,1,0:T(8,128)(2,1)}, u32[]{:S(2)}, u32[]{:S(2)}) collective-permute-start(bf16[2,4,288,128]{3,2,1,0:T(8,128)(2,1)} %copy-done.2), channel_id=1, source_target_pairs={{0,16},{1,17},{2,18},{3,19},{4,20},{5,21},{6,22},{7,23},{8,24},{9,... | collective-permute-start | bytes 1769480 | tf_op jit(solution)/shard_map/ppermute | solution.py:31
  76.1 13.5 %collective-permute-start.15 = (bf16[4,288,128]{2,1,0:T(8,128)(2,1)}, bf16[4,288,128]{2,1,0:T(8,128)(2,1)}, u32[]{:S(2)}, u32[]{:S(2)}) collective-permute-start(bf16[4,288,128]{2,1,0:T(8,128)(2,1)} %get-tuple-element.70), channel_id=1, source_target_pairs={{0,8},{1,9},{2,10},{3,11},{4,12},{5,13},{6,14},{7,15},{8,16},{9,17... | collective-permute-start | bytes 884744 | tf_op jit(solution)/shard_map/ppermute | solution.py:31
  89.6 9.0 %collective-permute-start.5 = (bf16[4,288,128]{2,1,0:T(8,128)(2,1)}, bf16[4,288,128]{2,1,0:T(8,128)(2,1)S(1)}, u32[]{:S(2)}, u32[]{:S(2)}) collective-permute-start(bf16[4,288,128]{2,1,0:T(8,128)(2,1)} %get-tuple-element.53), channel_id=1, source_target_pairs={{0,1},{1,2},{2,3},{3,4},{4,5},{5,6},{6,7},{7,0},{8,9},{9,10},{10,1... | collective-permute-start | bytes 884744 | tf_op jit(solution)/shard_map/ppermute | solution.py:25
  89.6 11.2 %collective-permute-start.16 = (bf16[4,288,128]{2,1,0:T(8,128)(2,1)}, bf16[4,288,128]{2,1,0:T(8,128)(2,1)S(1)}, u32[]{:S(2)}, u32[]{:S(2)}) collective-permute-start(bf16[4,288,128]{2,1,0:T(8,128)(2,1)} %get-tuple-element.71), channel_id=1, source_target_pairs={{0,8},{1,9},{2,10},{3,11},{4,12},{5,13},{6,14},{7,15},{8,16},{9,17... | collective-permute-start | bytes 884744 | tf_op jit(solution)/shard_map/ppermute | solution.py:31
  94.3 23.3 %collective-permute-start.17 = (bf16[4,288,128]{2,1,0:T(8,128)(2,1)}, bf16[4,288,128]{2,1,0:T(8,128)(2,1)S(1)}, u32[]{:S(2)}, u32[]{:S(2)}) collective-permute-start(bf16[4,288,128]{2,1,0:T(8,128)(2,1)} %copy-done.16), channel_id=1, source_target_pairs={{0,16},{1,17},{2,18},{3,19},{4,20},{5,21},{6,22},{7,23},{8,24},{9,... | collective-permute-start | bytes 884744 | tf_op jit(solution)/shard_map/ppermute | solution.py:31
  97.1 21.2 %collective-permute-start.19 = (bf16[4,288,128]{2,1,0:T(8,128)(2,1)}, bf16[4,288,128]{2,1,0:T(8,128)(2,1)}, u32[]{:S(2)}, u32[]{:S(2)}) collective-permute-start(bf16[4,288,128]{2,1,0:T(8,128)(2,1)} %copy-done.15), channel_id=1, source_target_pairs={{0,24},{1,25},{2,26},{3,27},{4,28},{5,29},{6,30},{7,31},{8,0},{9,1... | collective-permute-start | bytes 884744 | tf_op jit(solution)/shard_map/ppermute | solution.py:31
  97.1 21.2 %collective-permute-start.7 = (bf16[4,288,128]{2,1,0:T(8,128)(2,1)}, bf16[4,288,128]{2,1,0:T(8,128)(2,1)}, u32[]{:S(2)}, u32[]{:S(2)}) collective-permute-start(bf16[4,288,128]{2,1,0:T(8,128)(2,1)} %copy-done.28), channel_id=1, source_target_pairs={{0,7},{1,0},{2,1},{3,2},{4,3},{5,4},{6,5},{7,6},{8,15},{9,8},{10,9... | collective-permute-start | bytes 884744 | tf_op jit(solution)/shard_map/ppermute | solution.py:25
  98.6 0.8 copy-start.29
  99.4 19.0 %collective-permute-start.9 = (bf16[4,288,128]{2,1,0:T(8,128)(2,1)}, bf16[4,288,128]{2,1,0:T(8,128)(2,1)}, u32[]{:S(2)}, u32[]{:S(2)}) collective-permute-start(bf16[4,288,128]{2,1,0:T(8,128)(2,1)} %copy-done.27), channel_id=1, source_target_pairs={{0,2},{1,7},{2,4},{3,1},{4,6},{5,3},{6,0},{7,5},{8,10},{9,15},{10,... | collective-permute-start | bytes 884744 | tf_op jit(solution)/shard_map/ppermute | solution.py:25
  101.5 15.3 %collective-permute-start.6 = (bf16[4,288,128]{2,1,0:T(8,128)(2,1)}, bf16[4,288,128]{2,1,0:T(8,128)(2,1)S(1)}, u32[]{:S(2)}, u32[]{:S(2)}) collective-permute-start(bf16[4,288,128]{2,1,0:T(8,128)(2,1)} %copy-done.31), channel_id=1, source_target_pairs={{0,1},{1,2},{2,3},{3,4},{4,5},{5,6},{6,7},{7,0},{8,9},{9,10},{10,1... | collective-permute-start | bytes 884744 | tf_op jit(solution)/shard_map/ppermute | solution.py:25
  103.1 15.3 %copy-start.14 = (bf16[4,288,128]{2,1,0:T(8,128)(2,1)S(1)}, bf16[4,288,128]{2,1,0:T(8,128)(2,1)}, u32[]{:S(2)}) copy-start(bf16[4,288,128]{2,1,0:T(8,128)(2,1)} %copy-done.13) | copy-start | bytes 884740
  118.3 1.0 copy-start.26
  119.3 1.0 copy-start.30
  120.3 1.0 copy-start.33
  121.2 14.1 %copy-start.12 = (bf16[4,288,128]{2,1,0:T(8,128)(2,1)S(1)}, bf16[4,288,128]{2,1,0:T(8,128)(2,1)}, u32[]{:S(2)}) copy-start(bf16[4,288,128]{2,1,0:T(8,128)(2,1)} %copy-done.11) | copy-start | bytes 884740
  121.2 17.9 %copy-start.10 = (bf16[4,288,128]{2,1,0:T(8,128)(2,1)S(1)}, bf16[4,288,128]{2,1,0:T(8,128)(2,1)}, u32[]{:S(2)}) copy-start(bf16[4,288,128]{2,1,0:T(8,128)(2,1)} %copy-done.9) | copy-start | bytes 884740
  127.6 27.4 %copy-start.8 = (bf16[4,288,128]{2,1,0:T(8,128)(2,1)S(1)}, bf16[4,288,128]{2,1,0:T(8,128)(2,1)}, u32[]{:S(2)}) copy-start(bf16[4,288,128]{2,1,0:T(8,128)(2,1)} %copy-done.7) | copy-start | bytes 884740
  127.6 27.4 %copy-start.18 = (bf16[4,288,128]{2,1,0:T(8,128)(2,1)S(1)}, bf16[4,288,128]{2,1,0:T(8,128)(2,1)}, u32[]{:S(2)}) copy-start(bf16[4,288,128]{2,1,0:T(8,128)(2,1)} %copy-done.17) | copy-start | bytes 884740
  127.6 35.6 %all-to-all-start.1 = ((bf16[8,64,640]{2,1,0:T(8,128)(2,1)}), bf16[8,64,640]{2,1,0:T(8,128)(2,1)}, u32[]{:S(2)}, u32[]{:S(2)}) async-start(bf16[8,64,640]{2,1,0:T(8,128)(2,1)} %bitcast.23), calls=%async_computation.1 | async-start | bytes 1310720 | tf_op jit(solution)/shard_map/all_to_all | solution.py:235
  135.4 16.5 %collective-permute-start.20 = (bf16[4,288,128]{2,1,0:T(8,128)(2,1)S(1)}, bf16[4,288,128]{2,1,0:T(8,128)(2,1)S(1)}, u32[]{:S(2)}, u32[]{:S(2)}) collective-permute-start(bf16[4,288,128]{2,1,0:T(8,128)(2,1)S(1)} %copy-done.12), channel_id=1, source_target_pairs={{0,24},{1,25},{2,26},{3,27},{4,28},{5,29},{6,30},{7,31},{8,0},{9,1... | collective-permute-start | bytes 884744 | tf_op jit(solution)/shard_map/ppermute | solution.py:31
  139.2 12.7 %collective-permute-start.18 = (bf16[4,288,128]{2,1,0:T(8,128)(2,1)S(1)}, bf16[4,288,128]{2,1,0:T(8,128)(2,1)S(1)}, u32[]{:S(2)}, u32[]{:S(2)}) collective-permute-start(bf16[4,288,128]{2,1,0:T(8,128)(2,1)S(1)} %copy-done.10), channel_id=1, source_target_pairs={{0,16},{1,17},{2,18},{3,19},{4,20},{5,21},{6,22},{7,23},{8,24},{9,... | collective-permute-start | bytes 884744 | tf_op jit(solution)/shard_map/ppermute | solution.py:31
  139.4 12.5 %collective-permute-start.10 = (bf16[4,288,128]{2,1,0:T(8,128)(2,1)}, bf16[4,288,128]{2,1,0:T(8,128)(2,1)S(1)}, u32[]{:S(2)}, u32[]{:S(2)}) collective-permute-start(bf16[4,288,128]{2,1,0:T(8,128)(2,1)} %copy-done.20), channel_id=1, source_target_pairs={{0,2},{1,7},{2,4},{3,1},{4,6},{5,3},{6,0},{7,5},{8,10},{9,15},{10,... | collective-permute-start | bytes 884744 | tf_op jit(solution)/shard_map/ppermute | solution.py:25
  139.4 15.5 %collective-permute-start.8 = (bf16[4,288,128]{2,1,0:T(8,128)(2,1)}, bf16[4,288,128]{2,1,0:T(8,128)(2,1)S(1)}, u32[]{:S(2)}, u32[]{:S(2)}) collective-permute-start(bf16[4,288,128]{2,1,0:T(8,128)(2,1)} %copy-done.19), channel_id=1, source_target_pairs={{0,7},{1,0},{2,1},{3,2},{4,3},{5,4},{6,5},{7,6},{8,15},{9,8},{10,9... | collective-permute-start | bytes 884744 | tf_op jit(solution)/shard_map/ppermute | solution.py:25
  154.9 1.0 copy-start.22
  155.9 1.0 copy-start.24
  163.2 16.0 %all-to-all-start = ((bf16[8,64,640]{2,1,0:T(8,128)(2,1)}), bf16[8,64,640]{2,1,0:T(8,128)(2,1)S(1)}, u32[]{:S(2)}, u32[]{:S(2)}) async-start(bf16[8,64,640]{2,1,0:T(8,128)(2,1)} %bitcast.20), calls=%async_computation | async-start | bytes 1310720 | tf_op jit(solution)/shard_map/all_to_all | solution.py:244
  170.8 13.3 %collective-permute-start.21 = (bf16[2,64,640]{2,1,0:T(8,128)(2,1)S(1)}, bf16[2,64,640]{2,1,0:T(8,128)(2,1)S(1)}, u32[]{:S(2)}, u32[]{:S(2)}) collective-permute-start(bf16[2,64,640]{2,1,0:T(8,128)(2,1)S(1)} %pad_maximum_fusion.4), channel_id=1, source_target_pairs={{0,4},{1,5},{2,6},{3,7},{4,0},{5,1},{6,2},{7,3},{8,12},{9,13},{10,... | collective-permute-start | bytes 491528 | tf_op jit(solution)/shard_map/ppermute | solution.py:35
  (16 other events, 11.5 us)
Sparse Core Ops, SparseCore 0:
  39.3 26.5 all-gather.2

commit v2 on v1

--- a/solution.py
+++ b/solution.py
@@ -40,7 +40,7 @@
 
 
 def lookup(slots, values, want):
-    return jnp.sum(jnp.where(slots == want[..., None], values, 0), axis=-1)
+    return jnp.max(jnp.where(slots == want[..., None], values, 0), axis=-1)
 
 
 def pick_kernel(idx_ref, k_ref, *outs):
@@ -57,8 +57,8 @@
         pick_kernel,
         in_specs=[pl.BlockSpec(memory_space=pltpu.SMEM), vm],
         out_specs=[vm] * 8,
-        out_shape=[jax.ShapeDtypeStruct((2, 4, *block), k.dtype)] * 8,
-        compiler_params=pltpu.CompilerParams(vmem_limit_bytes=32 * 1024 * 1024),
+        out_shape=[pltpu.VMEM((2, 4, *block), k.dtype)] * 8,
+        compiler_params=pltpu.CompilerParams(vmem_limit_bytes=12 * 1024 * 1024),
         cost_estimate=pl.CostEstimate(flops=0, bytes_accessed=2 * 64 * block[0] * block[1] * 2, transcendentals=0),
     )(idx, k)
 
@@ -78,8 +78,8 @@
         regroup_kernel,
         in_specs=[vm] * 4,
         out_specs=[vm] * 8,
-        out_shape=[jax.ShapeDtypeStruct(shape, parts[0].dtype)] * 8,
-        compiler_params=pltpu.CompilerParams(vmem_limit_bytes=32 * 1024 * 1024),
+        out_shape=[pltpu.VMEM(shape, parts[0].dtype)] * 8,
+        compiler_params=pltpu.CompilerParams(vmem_limit_bytes=8 * 1024 * 1024),
         cost_estimate=pl.CostEstimate(flops=0, bytes_accessed=2 * 8 * size * 2, transcendentals=0),
     )(*parts)
 
@@ -157,8 +157,8 @@
         out_specs=vm,
         out_shape=jax.ShapeDtypeStruct((rows, latent + LANES), jnp.bfloat16),
         scratch_shapes=[pltpu.VMEM((width, positions), jnp.bfloat16), pltpu.VMEM((rows, positions), jnp.float32)],
-        compiler_params=pltpu.CompilerParams(vmem_limit_bytes=40 * 1024 * 1024),
-        cost_estimate=pl.CostEstimate(flops=2 * rows * positions * (width + latent),
+        compiler_params=pltpu.CompilerParams(vmem_limit_bytes=20 * 1024 * 1024),
+        cost_estimate=pl.CostEstimate(flops=16 * rows * positions * (width + latent),
                                       bytes_accessed=positions * width * 2 + rows * (width + latent) * 2,
                                       transcendentals=rows * positions),
     )(scal, *args)
@@ -204,11 +204,19 @@
     take_z = lookup(request_decode_slot, ids, 2 * owner + 1 - role)
     index = jnp.concatenate([jnp.moveaxis(take_z, 2, 0).reshape(-1), jnp.moveaxis(take_x, 1, 0).reshape(-1)])
     picked = pick(blocks, index)
-    got_z = [None, move_z(picked[1], 1, 1), move_z(picked[2], 2, 1), None]
-    got_x = [picked[4], move_x(picked[5], 1), None, move_x(picked[7], 3)]
-    got_z[3] = move_z(after(picked[3], got_z[1]), 3, 1)
-    got_x[2] = move_x(after(picked[6], got_x[1]), 2)
-    got_z[0] = move_z(after(picked[0], got_z[2]), 0, 1)
+    q_nope = after(q_nope, picked[1])
+    queries = q_nope.reshape(req_dev, steps, heads_dev, nope_dim)
+    absorbed = jnp.einsum("bshd,hdk->bshk", queries, w_key, preferred_element_type=jnp.float32).astype(jnp.bfloat16)
+    own = jnp.concatenate([absorbed, q_rope.reshape(req_dev, steps, heads_dev, rope_dim)], axis=3)
+
+    got_x = [move_x(picked[4 + i], i) for i in range(4)]
+    got_z = [move_z(picked[i], i, 1) for i in range(4)]
+    got_x, got_z, both = lax.optimization_barrier((got_x, got_z, (own, move_far(own))))
+    both = jnp.stack(both, axis=1)
+    heads = 2 * lax.axis_size("ctx")
+    spread = jnp.broadcast_to(both[:, None], (req_dev, lax.axis_size("ctx"), *both.shape[1:]))
+    every = lax.all_to_all(spread.reshape(heads, *both.shape[1:]), ("role", "ctx"), 0, 0, tiled=True)
+    every = jnp.moveaxis(every, 1, 0).reshape(2, -1, latent + rope_dim)
     mine_f, mine_n = second(got_x, move_z)
     recv_f, recv_n = second(got_z, move_x)
     source = (x - dx + NX) % NX * NZ + (z - move + NZ) % NZ
@@ -219,19 +227,7 @@
         length = lookup(request_decode_slot, lengths, want)
         return jnp.concatenate([(length - base).reshape(-1), role[None], ctx[None]]).astype(jnp.int32)
 
-    q_nope = after(q_nope, picked[1])
-    queries = q_nope.reshape(req_dev, steps, heads_dev, nope_dim)
-    absorbed = jnp.einsum("bshd,hdk->bshk", queries, w_key, preferred_element_type=jnp.float32).astype(jnp.bfloat16)
-    own = jnp.concatenate([absorbed, q_rope.reshape(req_dev, steps, heads_dev, rope_dim)], axis=3)
-    both = jnp.stack([own, move_far(own)], axis=1)
-    keep = jnp.where(role == 0, both[0], both[1])
-    got = swap_role(jnp.where(role == 0, both[1], both[0]))
-    pair = jnp.stack([jnp.where(role == 0, keep, got), jnp.where(role == 0, got, keep)], axis=1)
-    every = lax.all_gather(pair, "ctx", axis=2, tiled=False)
-    every = every.reshape(2, -1, latent + rope_dim)
-
-    part_f = attend(scalars(4), after(every[1], (mine_n[1], recv_n[1])), mine_f, recv_f, None, latent, scale)
-    heads = 2 * lax.axis_size("ctx")
+    part_f = attend(scalars(4), every[1], mine_f, recv_f, None, latent, scale)
     part_f = lax.all_to_all(part_f.reshape(heads, -1, latent + LANES), ("role", "ctx"), 0, 0, tiled=True)
     rows_f, lse_f = merge(part_f.reshape(2, -1, *part_f.shape[1:]), latent, 1)
     packed = jnp.concatenate(

time: 195 us -> 151 us (0.77)
  the two profiles are of different devices: /device:TPU:1 before, /device:TPU:110 now
where the time goes in v2:
time: 151 us; the launch traced here: 150 us
  waiting for transfers between devices  68.7 us (45%)
  starting transfers between devices  32.4 us (21%)
  Pallas kernels  20.2 us (13%)
  local copies, waits for them, and re-layouts  17.8 us (12%)
  other arithmetic  8.59 us (6%)
  matrix products  2.4 us (2%)
    ppermute x9, waiting for transfers between devices, move_x(): lax.ppermute(a, 'req', [(x * NZ + z, (x + dx) % NX * NZ + z) for x in ran...  27.5 us
    ppermute x10, waiting for transfers between devices, move_z(): return lax.ppermute(a, ('role', 'req'), pairs)  21.2 us
    ppermute x2, waiting for transfers between devices, move_far(): lax.ppermute(a, 'req', [(x * NZ + z, x * NZ + (z + 4) % NZ) for x in rang...  13.4 us
    pallas_call x2, Pallas kernels, attend(): pl.pallas_call(functools.partial(attend_kernel, fresh, scale), in_specs=[...  12.7 us
    unnamed x62, local copies, waits for them, and re-layouts  12.6 us
    ppermute x9, starting transfers between devices, move_x(): lax.ppermute(a, 'req', [(x * NZ + z, (x + dx) % NX * NZ + z) for x in ran...  8.33 us
    ppermute x2, starting transfers between devices, move_far(): lax.ppermute(a, 'req', [(x * NZ + z, x * NZ + (z + 4) % NZ) for x in rang...  6.05 us
    all_to_all x1, waiting for transfers between devices, shards(): lax.all_to_all(part_n.reshape(heads, -1, latent + LANES), ('role', 'ctx')...  5.74 us
  transfers between devices with their start and end apart: 24, of which 13 were waited for; matrix products, arithmetic and copies ran while one was open for 5% of the time, Pallas kernels for 12%

profile of v2, /device:TPU:110, one launch (start us, length us, event | category | flops | bytes accessed | tf_op | source)
XLA Modules:
  0.0 150.5 jit_solution(9936052686319612474)
XLA Ops:
  0.1 0.9 and_select_fusion
  1.0 1.1 select_reduce_fusion.1
  2.4 2.3 %copy-done.1 = bf16[64,128,288]{1,2,0:T(8,128)(2,1)S(1)} copy-done((bf16[64,128,288]{1,2,0:T(8,128)(2,1)S(1)}, bf16[64,128,288]{1,2,0:T(8,128)(2,1)}, u32[]{:S(2)}) %copy-start.1) | copy-done | bytes 4718616
  4.8 2.8 %shard_map.91 = (bf16[2,4,288,128]{3,2,1,0:T(8,128)(2,1)}, bf16[2,4,288,128]{3,2,1,0:T(8,128)(2,1)}, bf16[2,4,288,128]{3,2,1,0:T(8,128)(2,1)}, bf16[2,4,288,128]...) custom-call(s32[64]{0:T(128)S(1)} %pad_add_fusion.idx_ref, ...), custom_call_target="tpu_custom_call" | custom-call | bytes 9437184 | tf_op jit(solution)/shard_map/pallas_call | solution.py:56
  8.0 2.4 %collective-permute-start.1 = (bf16[2,4,288,128]{3,2,1,0:T(8,128)(2,1)}, bf16[2,4,288,128]{3,2,1,0:T(8,128)(2,1)}, u32[]{:S(2)}, u32[]{:S(2)}) collective-permute-start(bf16[2,4,288,128]{3,2,1,0:T(8,128)(2,1)} %get-tuple-element.50), channel_id=1, source_target_pairs={{0,16},{1,17},{2,18},{3,19},{4,20},{5,21},{6,22},{7,23},{8,24},{9,... | collective-permute-start | bytes 1769480 | tf_op jit(solution)/shard_map/ppermute | solution.py:31
  11.1 4.6 %collective-permute-start.7 = (bf16[2,4,16,576]{3,1,0,2:T(4,128)(2,1)S(1)}, bf16[2,4,16,576]{3,1,0,2:T(4,128)(2,1)S(1)}, u32[]{:S(2)}, u32[]{:S(2)}) collective-permute-start(bf16[2,4,16,576]{3,1,0,2:T(4,128)(2,1)S(1)} %pad_maximum_fusion.2), channel_id=1, source_target_pairs={{0,4},{1,5},{2,6},{3,7},{4,0},{5,1},{6,2},{7,3},{8,12},{9,13},{10,... | collective-permute-start | bytes 442376 | tf_op jit(solution)/shard_map/ppermute | solution.py:35
  15.6 6.8 %collective-permute-done.7 = bf16[2,4,16,576]{3,1,0,2:T(4,128)(2,1)S(1)} collective-permute-done((bf16[2,4,16,576]{3,1,0,2:T(4,128)(2,1)S(1)}, bf16[2,4,16,576]{3,1,0,2:T(4,128)(2,1)S(1)}, u32[]{:S(2)}, u32[]{:S(2)}) %collective-permute-start.7) | collective-permute-done | bytes 147488 | tf_op jit(solution)/shard_map/ppermute | solution.py:35
  22.5 1.5 collective-permute-done.refs_1_
  24.0 1.0 collective-permute-start.5
  25.0 1.1 collective-permute-done.1.refs_2_
  26.9 10.4 %collective-permute-done.2.refs_3_ = bf16[2,4,288,128]{3,2,1,0:T(8,128)(2,1)} collective-permute-done((bf16[2,4,288,128]{3,2,1,0:T(8,128)(2,1)}, bf16[2,4,288,128]{3,2,1,0:T(8,128)(2,1)}, u32[]{:S(2)}, u32[]{:S(2)}) %collective-permute-start.2) | collective-permute-done | bytes 589856 | tf_op jit(solution)/shard_map/ppermute | solution.py:31
  37.3 4.0 %collective-permute-done.5.refs_2_ = bf16[2,4,288,128]{3,2,1,0:T(8,128)(2,1)} collective-permute-done((bf16[2,4,288,128]{3,2,1,0:T(8,128)(2,1)}, bf16[2,4,288,128]{3,2,1,0:T(8,128)(2,1)}, u32[]{:S(2)}, u32[]{:S(2)}) %collective-permute-start.5) | collective-permute-done | bytes 589856 | tf_op jit(solution)/shard_map/ppermute | solution.py:25
  41.3 15.1 %collective-permute-done.6.refs_3_ = bf16[2,4,288,128]{3,2,1,0:T(8,128)(2,1)} collective-permute-done((bf16[2,4,288,128]{3,2,1,0:T(8,128)(2,1)}, bf16[2,4,288,128]{3,2,1,0:T(8,128)(2,1)}, u32[]{:S(2)}, u32[]{:S(2)}) %collective-permute-start.6) | collective-permute-done | bytes 589856 | tf_op jit(solution)/shard_map/ppermute | solution.py:25
  56.4 1.2 pad_maximum_fusion
  57.6 1.3 broadcast_in_dim.93
  58.9 4.9 %all-to-all-start = ((bf16[8,2,4,16,576]{4,3,2,1,0:T(8,128)(2,1)}), bf16[8,2,4,16,576]{4,3,2,1,0:T(8,128)(2,1)}, u32[]{:S(2)}, u32[]{:S(2)}) async-start(bf16[8,2,4,16,576]{4,3,2,1,0:T(8,128)(2,1)} %bitcast.60), calls=%async_computation | async-start | bytes 2621440 | tf_op jit(solution)/shard_map/all_to_all | solution.py:218
  63.8 1.2 fusion.22
  65.4 0.8 copy.35
  66.2 2.6 %shard_map.93 = (bf16[4,288,128]{2,1,0:T(8,128)(2,1)S(1)}, bf16[4,288,128]{2,1,0:T(8,128)(2,1)S(1)}, bf16[4,288,128]{2,1,0:T(8,128)(2,1)S(1)}, bf16[4,288,128]{2...) custom-call(bf16[2,4,288,128]{3,2,1,0:T(8,128)(2,1)} %collective-per, ...), custom_call_target="tpu_custom_call" | custom-call | bytes 4718592 | tf_op jit(solution)/shard_map/pallas_call | solution.py:77
  70.3 3.3 %collective-permute-start.16 = (bf16[4,288,128]{2,1,0:T(8,128)(2,1)S(1)}, bf16[4,288,128]{2,1,0:T(8,128)(2,1)S(1)}, u32[]{:S(2)}, u32[]{:S(2)}) collective-permute-start(bf16[4,288,128]{2,1,0:T(8,128)(2,1)S(1)} %get-tuple-element.86), channel_id=1, source_target_pairs={{0,16},{1,17},{2,18},{3,19},{4,20},{5,21},{6,22},{7,23},{8,24},{9,... | collective-permute-start | bytes 884744 | tf_op jit(solution)/shard_map/ppermute | solution.py:31
  74.2 2.2 %shard_map.92 = (bf16[4,288,128]{2,1,0:T(8,128)(2,1)S(1)}, bf16[4,288,128]{2,1,0:T(8,128)(2,1)S(1)}, bf16[4,288,128]{2,1,0:T(8,128)(2,1)S(1)}, bf16[4,288,128]{2...) custom-call(bf16[2,4,288,128]{3,2,1,0:T(8,128)(2,1)S(1)} %get-tuple-, ...), custom_call_target="tpu_custom_call" | custom-call | bytes 4718592 | tf_op jit(solution)/shard_map/pallas_call | solution.py:77
  76.4 0.7 copy-done.14
  77.1 4.2 %collective-permute-done.18.rest_7_ = bf16[4,288,128]{2,1,0:T(8,128)(2,1)S(1)} collective-permute-done((bf16[4,288,128]{2,1,0:T(8,128)(2,1)S(1)}, bf16[4,288,128]{2,1,0:T(8,128)(2,1)S(1)}, u32[]{:S(2)}, u32[]{:S(2)}) %collective-permute-start.18) | collective-permute-done | bytes 294944 | tf_op jit(solution)/shard_map/ppermute | solution.py:31
  82.0 4.8 %collective-permute-done.16.rest_6_ = bf16[4,288,128]{2,1,0:T(8,128)(2,1)S(1)} collective-permute-done((bf16[4,288,128]{2,1,0:T(8,128)(2,1)S(1)}, bf16[4,288,128]{2,1,0:T(8,128)(2,1)S(1)}, u32[]{:S(2)}, u32[]{:S(2)}) %collective-permute-start.16) | collective-permute-done | bytes 294944 | tf_op jit(solution)/shard_map/ppermute | solution.py:31
  87.7 0.8 copy-done.12
  88.5 0.9 collective-permute-start.17
  89.5 2.0 %collective-permute-done.12.rest_3_ = bf16[4,288,128]{2,1,0:T(8,128)(2,1)S(1)} collective-permute-done((bf16[4,288,128]{2,1,0:T(8,128)(2,1)S(1)}, bf16[4,288,128]{2,1,0:T(8,128)(2,1)S(1)}, u32[]{:S(2)}, u32[]{:S(2)}) %collective-permute-start.12) | collective-permute-done | bytes 294944 | tf_op jit(solution)/shard_map/ppermute | solution.py:25
  92.9 0.7 copy-done.18
  93.6 1.3 collective-permute-start.13
  94.9 0.8 copy-done.22
  95.7 0.8 collective-permute-start.11
  96.6 1.5 %fusion.35 = (bf16[1,8,4,16,576]{4,3,2,0,1:T(8,128)(2,1)S(1)}, bf16[1,8,4,16,576]{4,3,2,0,1:T(8,128)(2,1)S(1)}) fusion(bf16[2,8,4,16,576]{4,3,2,0,1:T(8,128)(2,1)} %bitcast.11), kind=kLoop, calls=%fused_computation.76 | loop fusion | bytes 2359296 | tf_op jit(solution)/shard_map/slice | solution.py:230
  98.1 5.5 %collective-permute-done.19.rest_7_ = bf16[4,288,128]{2,1,0:T(8,128)(2,1)S(1)} collective-permute-done((bf16[4,288,128]{2,1,0:T(8,128)(2,1)}, bf16[4,288,128]{2,1,0:T(8,128)(2,1)S(1)}, u32[]{:S(2)}, u32[]{:S(2)}) %collective-permute-start.19) | collective-permute-done | bytes 294944 | tf_op jit(solution)/shard_map/ppermute | solution.py:31
  103.6 0.7 copy-done.16
  104.7 1.0 copy-done.7
  105.7 5.6 %shard_map.95 = bf16[512,640]{1,0:T(8,128)(2,1)} custom-call(s32[18]{0:T(128)S(1)} %add_add_fusion.1.scal_ref, bf16[512,576]{1,0:T(8,128)(2,1)S(1)} %bitcast.57, bf16[4,288,128]{2,1,0:T(8,128)(2,1)S(1)} %copy-done.15, bf16[4,288,128]{2,1,0:T(8,128)(2,1)S(1)} %copy-done.23, bf16[4,288,128]{2,1,0:T(8,128)(2,1)S(1)} %copy-done.19, ...), custom_call_target="tpu_custom_call" | custom-call | flops 18253611008 | bytes 3473408 | tf_op jit(solution)/shard_map/pallas_call | solution.py:154
  111.2 4.8 %all-to-all-start.2 = ((bf16[8,64,640]{2,1,0:T(8,128)(2,1)}), bf16[8,64,640]{2,1,0:T(8,128)(2,1)}, u32[]{:S(2)}, u32[]{:S(2)}) async-start(bf16[8,64,640]{2,1,0:T(8,128)(2,1)} %bitcast.18), calls=%async_computation.2 | async-start | bytes 1310720 | tf_op jit(solution)/shard_map/all_to_all | solution.py:231
  116.1 1.0 copy-done.5
  117.1 1.0 copy-done.17
  118.1 7.1 %shard_map.94 = bf16[512,640]{1,0:T(8,128)(2,1)} custom-call(s32[18]{0:T(128)S(1)} %add_add_fusion.scal_ref, bf16[512,576]{1,0:T(8,128)(2,1)S(1)} %bitcast.56, bf16[4,288,128]{2,1,0:T(8,128)(2,1)S(1)} %copy-done.5, bf16[4,288,128]{2,1,0:T(8,128)(2,1)} %collective-permute-done.9.rest_1_, bf16[4,288,128]{2,1,0:T(8,128)(2,1)} %collective-permute-done.11.rest_2_, ...), custom_call_target="tpu_custom_call" | custom-call | flops 18253611008 | bytes 3473408 | tf_op jit(solution)/shard_map/pallas_call | solution.py:154
  125.2 0.8 all-to-all-done.2
  126.0 4.8 %all-to-all-start.1 = ((bf16[8,64,640]{2,1,0:T(8,128)(2,1)}), bf16[8,64,640]{2,1,0:T(8,128)(2,1)S(1)}, u32[]{:S(2)}, u32[]{:S(2)}) async-start(bf16[8,64,640]{2,1,0:T(8,128)(2,1)} %bitcast.15), calls=%async_computation.1 | async-start | bytes 1310720 | tf_op jit(solution)/shard_map/all_to_all | solution.py:240
  130.8 1.0 convert_reduce_fusion.1
  132.1 1.2 multiply_reduce_fusion.1
  133.4 1.5 collective-permute-start.20
  134.9 5.7 %all-to-all-done.1 = bf16[8,64,640]{2,1,0:T(8,128)(2,1)S(1)} async-done(((bf16[8,64,640]{2,1,0:T(8,128)(2,1)}), bf16[8,64,640]{2,1,0:T(8,128)(2,1)S(1)}, u32[]{:S(2)}, u32[]{:S(2)}) %all-to-all-start.1) | async-done | bytes 655392 | tf_op jit(solution)/shard_map/all_to_all | solution.py:240
  140.6 6.6 %collective-permute-done.20 = bf16[2,64,640]{2,1,0:T(8,128)(2,1)S(1)} collective-permute-done((bf16[2,64,640]{2,1,0:T(8,128)(2,1)S(1)}, bf16[2,64,640]{2,1,0:T(8,128)(2,1)S(1)}, u32[]{:S(2)}, u32[]{:S(2)}) %collective-permute-start.20) | collective-permute-done | bytes 163872 | tf_op jit(solution)/shard_map/ppermute | solution.py:35
  147.8 2.0 %fusion.13 = bf16[16,2,1,4,128]{4,3,2,1,0:T(4,128)(2,1)S(1)} fusion(bf16[16,512,128]{2,1,0:T(8,128)(2,1)} %param.16, bf16[2,4,16,512]{3,2,1,0:T(8,128)(2,1)S(1)} %divide_convert_fusion), kind=kOutput, calls=%fused_computation.8 | convolution fusion | flops 16793600 | bytes 2260992 | tf_op jit(solution)/shard_map/bshk,hkv->bshv/dot_general | solution.py:244
  (114 shorter events, 9.6 us)
Async XLA Ops:
  0.0 10.6 %copy-start = (bf16[16,128,512]{2,1,0:T(8,128)(2,1)S(1)}, bf16[16,128,512]{2,1,0:T(8,128)(2,1)}, u32[]{:S(2)}) copy-start(bf16[16,128,512]{2,1,0:T(8,128)(2,1)} %param.15) | copy-start | bytes 6291460
  2.4 2.3 %copy-start.1 = (bf16[64,128,288]{1,2,0:T(8,128)(2,1)S(1)}, bf16[64,128,288]{1,2,0:T(8,128)(2,1)}, u32[]{:S(2)}) copy-start(bf16[64,128,288]{1,2,0:T(8,128)(2,1)} %param.9) | copy-start | bytes 14155780
  4.8 5.7 %copy-start.27 = (bf16[2,4,1024]{2,1,0:T(4,128)(2,1)S(1)}, bf16[2,4,1024]{2,1,0:T(4,128)(2,1)}, u32[]{:S(2)}) copy-start(bf16[2,4,1024]{2,1,0:T(4,128)(2,1)} %param.13) | copy-start | bytes 49156
  4.8 5.8 %copy-start.26 = (bf16[2,4,2048]{2,1,0:T(4,128)(2,1)S(1)}, bf16[2,4,2048]{2,1,0:T(4,128)(2,1)}, u32[]{:S(2)}) copy-start(bf16[2,4,2048]{2,1,0:T(4,128)(2,1)} %param.12) | copy-start | bytes 98308
  7.6 18.6 %copy-start.29 = (s32[64]{0:T(128)S(1)}, s32[64]{0:T(128)}, u32[]{:S(2)}) copy-start(s32[64]{0:T(128)} %param.11) | copy-start | bytes 772
  7.6 18.6 %copy-start.30 = (s32[64]{0:T(128)S(1)}, s32[64]{0:T(128)}, u32[]{:S(2)}) copy-start(s32[64]{0:T(128)} %param.10) | copy-start | bytes 772
  7.6 16.4 %collective-permute-start = (bf16[2,4,288,128]{3,2,1,0:T(8,128)(2,1)}, bf16[2,4,288,128]{3,2,1,0:T(8,128)(2,1)S(1)}, u32[]{:S(2)}, u32[]{:S(2)}) collective-permute-start(bf16[2,4,288,128]{3,2,1,0:T(8,128)(2,1)} %get-tuple-element.49), channel_id=1, source_target_pairs={{0,8},{1,9},{2,10},{3,11},{4,12},{5,13},{6,14},{7,15},{8,16},{9,17... | collective-permute-start | bytes 1769480 | tf_op jit(solution)/shard_map/ppermute | solution.py:31
  8.0 18.1 %collective-permute-start.1 = (bf16[2,4,288,128]{3,2,1,0:T(8,128)(2,1)}, bf16[2,4,288,128]{3,2,1,0:T(8,128)(2,1)}, u32[]{:S(2)}, u32[]{:S(2)}) collective-permute-start(bf16[2,4,288,128]{3,2,1,0:T(8,128)(2,1)} %get-tuple-element.50), channel_id=1, source_target_pairs={{0,16},{1,17},{2,18},{3,19},{4,20},{5,21},{6,22},{7,23},{8,24},{9,... | collective-permute-start | bytes 1769480 | tf_op jit(solution)/shard_map/ppermute | solution.py:31
  11.1 11.4 %collective-permute-start.7 = (bf16[2,4,16,576]{3,1,0,2:T(4,128)(2,1)S(1)}, bf16[2,4,16,576]{3,1,0,2:T(4,128)(2,1)S(1)}, u32[]{:S(2)}, u32[]{:S(2)}) collective-permute-start(bf16[2,4,16,576]{3,1,0,2:T(4,128)(2,1)S(1)} %pad_maximum_fusion.2), channel_id=1, source_target_pairs={{0,4},{1,5},{2,6},{3,7},{4,0},{5,1},{6,2},{7,3},{8,12},{9,13},{10,... | collective-permute-start | bytes 442376 | tf_op jit(solution)/shard_map/ppermute | solution.py:35
  15.6 21.6 %collective-permute-start.4 = (bf16[2,4,288,128]{3,2,1,0:T(8,128)(2,1)}, bf16[2,4,288,128]{3,2,1,0:T(8,128)(2,1)}, u32[]{:S(2)}, u32[]{:S(2)}) collective-permute-start(bf16[2,4,288,128]{3,2,1,0:T(8,128)(2,1)} %get-tuple-element.53), channel_id=1, source_target_pairs={{0,129},{1,130},{2,131},{3,132},{4,133},{5,134},{6,135},{7,128},{8... | collective-permute-start | bytes 1769480 | tf_op jit(solution)/shard_map/ppermute | solution.py:25
  15.6 21.6 %collective-permute-start.2 = (bf16[2,4,288,128]{3,2,1,0:T(8,128)(2,1)}, bf16[2,4,288,128]{3,2,1,0:T(8,128)(2,1)}, u32[]{:S(2)}, u32[]{:S(2)}) collective-permute-start(bf16[2,4,288,128]{3,2,1,0:T(8,128)(2,1)} %get-tuple-element.51), channel_id=1, source_target_pairs={{0,24},{1,25},{2,26},{3,27},{4,28},{5,29},{6,30},{7,31},{8,0},{9,1... | collective-permute-start | bytes 1769480 | tf_op jit(solution)/shard_map/ppermute | solution.py:31
  22.5 1.5 %copy-start.25 = (bf16[2,4,16,576]{3,1,0,2:T(4,128)(2,1)}, bf16[2,4,16,576]{3,1,0,2:T(4,128)(2,1)S(1)}, u32[]{:S(2)}) copy-start(bf16[2,4,16,576]{3,1,0,2:T(4,128)(2,1)S(1)} %collective-permute-done.7) | copy-start | bytes 442372
  22.5 14.8 %collective-permute-start.3 = (bf16[2,4,288,128]{3,2,1,0:T(8,128)(2,1)}, bf16[2,4,288,128]{3,2,1,0:T(8,128)(2,1)}, u32[]{:S(2)}, u32[]{:S(2)}) collective-permute-start(bf16[2,4,288,128]{3,2,1,0:T(8,128)(2,1)} %get-tuple-element.52), channel_id=1, source_target_pairs={{0,128},{1,129},{2,130},{3,131},{4,132},{5,133},{6,134},{7,135},{8... | collective-permute-start | bytes 1769480 | tf_op jit(solution)/shard_map/ppermute | solution.py:25
  24.0 17.3 %collective-permute-start.5 = (bf16[2,4,288,128]{3,2,1,0:T(8,128)(2,1)}, bf16[2,4,288,128]{3,2,1,0:T(8,128)(2,1)}, u32[]{:S(2)}, u32[]{:S(2)}) collective-permute-start(bf16[2,4,288,128]{3,2,1,0:T(8,128)(2,1)} %get-tuple-element.54), channel_id=1, source_target_pairs={{0,135},{1,128},{2,129},{3,130},{4,131},{5,132},{6,133},{7,134},{8... | collective-permute-start | bytes 1769480 | tf_op jit(solution)/shard_map/ppermute | solution.py:25
  26.2 30.3 %collective-permute-start.6 = (bf16[2,4,288,128]{3,2,1,0:T(8,128)(2,1)}, bf16[2,4,288,128]{3,2,1,0:T(8,128)(2,1)}, u32[]{:S(2)}, u32[]{:S(2)}) collective-permute-start(bf16[2,4,288,128]{3,2,1,0:T(8,128)(2,1)} %get-tuple-element.55), channel_id=1, source_target_pairs={{0,130},{1,135},{2,132},{3,129},{4,134},{5,131},{6,128},{7,133},{8... | collective-permute-start | bytes 1769480 | tf_op jit(solution)/shard_map/ppermute | solution.py:25
  57.6 7.6 %copy-start.28 = (bf16[2,4,576]{2,1,0:T(4,128)(2,1)S(1)}, bf16[2,4,576]{2,1,0:T(4,128)(2,1)}, u32[]{:S(2)}) copy-start(bf16[2,4,576]{2,1,0:T(4,128)(2,1)} %param.14) | copy-start | bytes 27652
  58.9 37.6 %all-to-all-start = ((bf16[8,2,4,16,576]{4,3,2,1,0:T(8,128)(2,1)}), bf16[8,2,4,16,576]{4,3,2,1,0:T(8,128)(2,1)}, u32[]{:S(2)}, u32[]{:S(2)}) async-start(bf16[8,2,4,16,576]{4,3,2,1,0:T(8,128)(2,1)} %bitcast.60), calls=%async_computation | async-start | bytes 2621440 | tf_op jit(solution)/shard_map/all_to_all | solution.py:218
  66.2 15.8 %copy-start.24 = (bf16[1,4,576]{1,2,0:T(8,128)(2,1)S(1)}, bf16[1,4,576]{1,2,0:T(8,128)(2,1)}, u32[]{:S(2)}) copy-start(bf16[1,4,576]{1,2,0:T(8,128)(2,1)} %copy.35) | copy-start | bytes 13828
  70.3 11.0 %collective-permute-start.18 = (bf16[4,288,128]{2,1,0:T(8,128)(2,1)S(1)}, bf16[4,288,128]{2,1,0:T(8,128)(2,1)S(1)}, u32[]{:S(2)}, u32[]{:S(2)}) collective-permute-start(bf16[4,288,128]{2,1,0:T(8,128)(2,1)S(1)} %get-tuple-element.89), channel_id=1, source_target_pairs={{0,24},{1,25},{2,26},{3,27},{4,28},{5,29},{6,30},{7,31},{8,0},{9,1... | collective-permute-start | bytes 884744 | tf_op jit(solution)/shard_map/ppermute | solution.py:31
  70.3 16.6 %collective-permute-start.16 = (bf16[4,288,128]{2,1,0:T(8,128)(2,1)S(1)}, bf16[4,288,128]{2,1,0:T(8,128)(2,1)S(1)}, u32[]{:S(2)}, u32[]{:S(2)}) collective-permute-start(bf16[4,288,128]{2,1,0:T(8,128)(2,1)S(1)} %get-tuple-element.86), channel_id=1, source_target_pairs={{0,16},{1,17},{2,18},{3,19},{4,20},{5,21},{6,22},{7,23},{8,24},{9,... | collective-permute-start | bytes 884744 | tf_op jit(solution)/shard_map/ppermute | solution.py:31
  73.7 14.0 %collective-permute-start.14 = (bf16[4,288,128]{2,1,0:T(8,128)(2,1)S(1)}, bf16[4,288,128]{2,1,0:T(8,128)(2,1)S(1)}, u32[]{:S(2)}, u32[]{:S(2)}) collective-permute-start(bf16[4,288,128]{2,1,0:T(8,128)(2,1)S(1)} %get-tuple-element.83), channel_id=1, source_target_pairs={{0,8},{1,9},{2,10},{3,11},{4,12},{5,13},{6,14},{7,15},{8,16},{9,17... | collective-permute-start | bytes 884744 | tf_op jit(solution)/shard_map/ppermute | solution.py:31
  77.1 10.5 %copy-start.4 = (bf16[4,288,128]{2,1,0:T(8,128)(2,1)}, bf16[4,288,128]{2,1,0:T(8,128)(2,1)S(1)}, u32[]{:S(2)}) copy-start(bf16[4,288,128]{2,1,0:T(8,128)(2,1)S(1)} %get-tuple-element.65.rest_0_) | copy-start | bytes 884740
  77.1 15.8 %collective-permute-start.10 = (bf16[4,288,128]{2,1,0:T(8,128)(2,1)S(1)}, bf16[4,288,128]{2,1,0:T(8,128)(2,1)S(1)}, u32[]{:S(2)}, u32[]{:S(2)}) collective-permute-start(bf16[4,288,128]{2,1,0:T(8,128)(2,1)S(1)} %get-tuple-element.70), channel_id=1, source_target_pairs={{0,7},{1,0},{2,1},{3,2},{4,3},{5,4},{6,5},{7,6},{8,15},{9,8},{10,9... | collective-permute-start | bytes 884744 | tf_op jit(solution)/shard_map/ppermute | solution.py:25
  77.1 14.4 %collective-permute-start.12 = (bf16[4,288,128]{2,1,0:T(8,128)(2,1)S(1)}, bf16[4,288,128]{2,1,0:T(8,128)(2,1)S(1)}, u32[]{:S(2)}, u32[]{:S(2)}) collective-permute-start(bf16[4,288,128]{2,1,0:T(8,128)(2,1)S(1)} %get-tuple-element.73), channel_id=1, source_target_pairs={{0,2},{1,7},{2,4},{3,1},{4,6},{5,3},{6,0},{7,5},{8,10},{9,15},{10,... | collective-permute-start | bytes 884744 | tf_op jit(solution)/shard_map/ppermute | solution.py:25
  82.0 12.9 %collective-permute-start.8 = (bf16[4,288,128]{2,1,0:T(8,128)(2,1)S(1)}, bf16[4,288,128]{2,1,0:T(8,128)(2,1)S(1)}, u32[]{:S(2)}, u32[]{:S(2)}) collective-permute-start(bf16[4,288,128]{2,1,0:T(8,128)(2,1)S(1)} %get-tuple-element.67), channel_id=1, source_target_pairs={{0,1},{1,2},{2,3},{3,4},{4,5},{5,6},{6,7},{7,0},{8,9},{9,10},{10,1... | collective-permute-start | bytes 884744 | tf_op jit(solution)/shard_map/ppermute | solution.py:25
  87.6 16.0 %collective-permute-start.19 = (bf16[4,288,128]{2,1,0:T(8,128)(2,1)}, bf16[4,288,128]{2,1,0:T(8,128)(2,1)S(1)}, u32[]{:S(2)}, u32[]{:S(2)}) collective-permute-start(bf16[4,288,128]{2,1,0:T(8,128)(2,1)} %get-tuple-element.90), channel_id=1, source_target_pairs={{0,24},{1,25},{2,26},{3,27},{4,28},{5,29},{6,30},{7,31},{8,0},{9,1... | collective-permute-start | bytes 884744 | tf_op jit(solution)/shard_map/ppermute | solution.py:31
  87.7 0.8 copy-start.12
  88.5 27.6 %collective-permute-start.17 = (bf16[4,288,128]{2,1,0:T(8,128)(2,1)}, bf16[4,288,128]{2,1,0:T(8,128)(2,1)}, u32[]{:S(2)}, u32[]{:S(2)}) collective-permute-start(bf16[4,288,128]{2,1,0:T(8,128)(2,1)} %get-tuple-element.87), channel_id=1, source_target_pairs={{0,16},{1,17},{2,18},{3,19},{4,20},{5,21},{6,22},{7,23},{8,24},{9,... | collective-permute-start | bytes 884744 | tf_op jit(solution)/shard_map/ppermute | solution.py:31
  92.2 23.9 %collective-permute-start.15 = (bf16[4,288,128]{2,1,0:T(8,128)(2,1)}, bf16[4,288,128]{2,1,0:T(8,128)(2,1)}, u32[]{:S(2)}, u32[]{:S(2)}) collective-permute-start(bf16[4,288,128]{2,1,0:T(8,128)(2,1)} %get-tuple-element.84), channel_id=1, source_target_pairs={{0,8},{1,9},{2,10},{3,11},{4,12},{5,13},{6,14},{7,15},{8,16},{9,17... | collective-permute-start | bytes 884744 | tf_op jit(solution)/shard_map/ppermute | solution.py:31
  92.9 0.7 copy-start.18
  93.6 22.5 %collective-permute-start.13 = (bf16[4,288,128]{2,1,0:T(8,128)(2,1)}, bf16[4,288,128]{2,1,0:T(8,128)(2,1)}, u32[]{:S(2)}, u32[]{:S(2)}) collective-permute-start(bf16[4,288,128]{2,1,0:T(8,128)(2,1)} %get-tuple-element.74), channel_id=1, source_target_pairs={{0,2},{1,7},{2,4},{3,1},{4,6},{5,3},{6,0},{7,5},{8,10},{9,15},{10,... | collective-permute-start | bytes 884744 | tf_op jit(solution)/shard_map/ppermute | solution.py:25
  94.9 0.8 copy-start.22
  95.7 20.4 %collective-permute-start.11 = (bf16[4,288,128]{2,1,0:T(8,128)(2,1)}, bf16[4,288,128]{2,1,0:T(8,128)(2,1)}, u32[]{:S(2)}, u32[]{:S(2)}) collective-permute-start(bf16[4,288,128]{2,1,0:T(8,128)(2,1)} %get-tuple-element.71), channel_id=1, source_target_pairs={{0,7},{1,0},{2,1},{3,2},{4,3},{5,4},{6,5},{7,6},{8,15},{9,8},{10,9... | collective-permute-start | bytes 884744 | tf_op jit(solution)/shard_map/ppermute | solution.py:25
  96.5 8.1 %copy-start.9 = (bf16[4,288,128]{2,1,0:T(8,128)(2,1)S(1)}, bf16[4,288,128]{2,1,0:T(8,128)(2,1)}, u32[]{:S(2)}) copy-start(bf16[4,288,128]{2,1,0:T(8,128)(2,1)} %copy-done.8) | copy-start | bytes 884740
  96.5 8.1 %copy-start.11 = (bf16[4,288,128]{2,1,0:T(8,128)(2,1)S(1)}, bf16[4,288,128]{2,1,0:T(8,128)(2,1)}, u32[]{:S(2)}) copy-start(bf16[4,288,128]{2,1,0:T(8,128)(2,1)} %copy-done.10) | copy-start | bytes 884740
  96.5 8.1 %copy-start.13 = (bf16[4,288,128]{2,1,0:T(8,128)(2,1)S(1)}, bf16[4,288,128]{2,1,0:T(8,128)(2,1)}, u32[]{:S(2)}) copy-start(bf16[4,288,128]{2,1,0:T(8,128)(2,1)} %copy-done.12) | copy-start | bytes 884740
  96.5 8.1 %copy-start.15 = (bf16[4,288,128]{2,1,0:T(8,128)(2,1)S(1)}, bf16[4,288,128]{2,1,0:T(8,128)(2,1)}, u32[]{:S(2)}) copy-start(bf16[4,288,128]{2,1,0:T(8,128)(2,1)} %copy-done.14) | copy-start | bytes 884740
  96.5 8.1 %copy-start.19 = (bf16[4,288,128]{2,1,0:T(8,128)(2,1)S(1)}, bf16[4,288,128]{2,1,0:T(8,128)(2,1)}, u32[]{:S(2)}) copy-start(bf16[4,288,128]{2,1,0:T(8,128)(2,1)} %copy-done.18) | copy-start | bytes 884740
  96.5 8.1 %copy-start.21 = (bf16[4,288,128]{2,1,0:T(8,128)(2,1)S(1)}, bf16[4,288,128]{2,1,0:T(8,128)(2,1)}, u32[]{:S(2)}) copy-start(bf16[4,288,128]{2,1,0:T(8,128)(2,1)} %copy-done.20) | copy-start | bytes 884740
  96.6 8.1 %copy-start.23 = (bf16[4,288,128]{2,1,0:T(8,128)(2,1)S(1)}, bf16[4,288,128]{2,1,0:T(8,128)(2,1)}, u32[]{:S(2)}) copy-start(bf16[4,288,128]{2,1,0:T(8,128)(2,1)} %copy-done.22) | copy-start | bytes 884740
  104.3 11.8 %collective-permute-start.9 = (bf16[4,288,128]{2,1,0:T(8,128)(2,1)}, bf16[4,288,128]{2,1,0:T(8,128)(2,1)}, u32[]{:S(2)}, u32[]{:S(2)}) collective-permute-start(bf16[4,288,128]{2,1,0:T(8,128)(2,1)} %get-tuple-element.68), channel_id=1, source_target_pairs={{0,1},{1,2},{2,3},{3,4},{4,5},{5,6},{6,7},{7,0},{8,9},{9,10},{10,1... | collective-permute-start | bytes 884744 | tf_op jit(solution)/shard_map/ppermute | solution.py:25
  104.7 1.0 copy-start.7
  105.7 10.5 %copy-start.3 = (bf16[4,288,128]{2,1,0:T(8,128)(2,1)S(1)}, bf16[4,288,128]{2,1,0:T(8,128)(2,1)}, u32[]{:S(2)}) copy-start(bf16[4,288,128]{2,1,0:T(8,128)(2,1)} %copy-done.2) | copy-start | bytes 884740
  111.2 14.8 %all-to-all-start.2 = ((bf16[8,64,640]{2,1,0:T(8,128)(2,1)}), bf16[8,64,640]{2,1,0:T(8,128)(2,1)}, u32[]{:S(2)}, u32[]{:S(2)}) async-start(bf16[8,64,640]{2,1,0:T(8,128)(2,1)} %bitcast.18), calls=%async_computation.2 | async-start | bytes 1310720 | tf_op jit(solution)/shard_map/all_to_all | solution.py:231
  116.1 1.0 copy-start.5
  117.1 1.0 copy-start.17
  126.0 14.6 %all-to-all-start.1 = ((bf16[8,64,640]{2,1,0:T(8,128)(2,1)}), bf16[8,64,640]{2,1,0:T(8,128)(2,1)S(1)}, u32[]{:S(2)}, u32[]{:S(2)}) async-start(bf16[8,64,640]{2,1,0:T(8,128)(2,1)} %bitcast.15), calls=%async_computation.1 | async-start | bytes 1310720 | tf_op jit(solution)/shard_map/all_to_all | solution.py:240
  133.4 13.8 %collective-permute-start.20 = (bf16[2,64,640]{2,1,0:T(8,128)(2,1)S(1)}, bf16[2,64,640]{2,1,0:T(8,128)(2,1)S(1)}, u32[]{:S(2)}, u32[]{:S(2)}) collective-permute-start(bf16[2,64,640]{2,1,0:T(8,128)(2,1)S(1)} %pad_maximum_fusion.3), channel_id=1, source_target_pairs={{0,4},{1,5},{2,6},{3,7},{4,0},{5,1},{6,2},{7,3},{8,12},{9,13},{10,... | collective-permute-start | bytes 491528 | tf_op jit(solution)/shard_map/ppermute | solution.py:35
  (7 other events, 5.1 us)

commit v3 on v2

--- a/solution.py
+++ b/solution.py
@@ -204,18 +204,20 @@
     take_z = lookup(request_decode_slot, ids, 2 * owner + 1 - role)
     index = jnp.concatenate([jnp.moveaxis(take_z, 2, 0).reshape(-1), jnp.moveaxis(take_x, 1, 0).reshape(-1)])
     picked = pick(blocks, index)
-    q_nope = after(q_nope, picked[1])
     queries = q_nope.reshape(req_dev, steps, heads_dev, nope_dim)
     absorbed = jnp.einsum("bshd,hdk->bshk", queries, w_key, preferred_element_type=jnp.float32).astype(jnp.bfloat16)
     own = jnp.concatenate([absorbed, q_rope.reshape(req_dev, steps, heads_dev, rope_dim)], axis=3)
 
-    got_x = [move_x(picked[4 + i], i) for i in range(4)]
-    got_z = [move_z(picked[i], i, 1) for i in range(4)]
-    got_x, got_z, both = lax.optimization_barrier((got_x, got_z, (own, move_far(own))))
+    picked, both = lax.optimization_barrier((picked, (own, move_far(own))))
     both = jnp.stack(both, axis=1)
     heads = 2 * lax.axis_size("ctx")
     spread = jnp.broadcast_to(both[:, None], (req_dev, lax.axis_size("ctx"), *both.shape[1:]))
     every = lax.all_to_all(spread.reshape(heads, *both.shape[1:]), ("role", "ctx"), 0, 0, tiled=True)
+    first = [move_z(picked[1], 1, 1), move_x(picked[5], 1), move_z(picked[2], 2, 1), move_x(picked[7], 3),
+             move_z(picked[3], 3, 1), move_x(picked[6], 2), move_z(picked[0], 0, 1)]
+    first, every = lax.optimization_barrier((first, every))
+    got_z = [first[6], first[0], first[2], first[4]]
+    got_x = [picked[4], first[1], first[5], first[3]]
     every = jnp.moveaxis(every, 1, 0).reshape(2, -1, latent + rope_dim)
     mine_f, mine_n = second(got_x, move_z)
     recv_f, recv_n = second(got_z, move_x)

time: 151 us -> 138 us (0.914)
  the two profiles are of different devices: /device:TPU:110 before, /device:TPU:1 now
where the time goes in v3:
time: 138 us; the launch traced here: 137 us
  starting transfers between devices  64.1 us (46%)
  waiting for transfers between devices  26.2 us (19%)
  Pallas kernels  19.3 us (14%)
  local copies, waits for them, and re-layouts  17.2 us (12%)
  other arithmetic  7.25 us (5%)
  matrix products  3.16 us (2%)
    ppermute x10, starting transfers between devices, move_z(): return lax.ppermute(a, ('role', 'req'), pairs)  17.3 us
    ppermute x9, starting transfers between devices, move_x(): lax.ppermute(a, 'req', [(x * NZ + z, (x + dx) % NX * NZ + z) for x in ran...  16.8 us
    ppermute x10, waiting for transfers between devices, move_z(): return lax.ppermute(a, ('role', 'req'), pairs)  14.5 us
    pallas_call x2, Pallas kernels, attend(): pl.pallas_call(functools.partial(attend_kernel, fresh, scale), in_specs=[...  12.7 us
    ppermute x2, starting transfers between devices, move_far(): lax.ppermute(a, 'req', [(x * NZ + z, x * NZ + (z + 4) % NZ) for x in rang...  12.1 us
    unnamed x38, local copies, waits for them, and re-layouts  11.3 us
    all_to_all x1, starting transfers between devices, shards(): lax.all_to_all(part_f.reshape(heads, -1, latent + LANES), ('role', 'ctx')...  9.3 us
    ppermute x2, waiting for transfers between devices, move_far(): lax.ppermute(a, 'req', [(x * NZ + z, x * NZ + (z + 4) % NZ) for x in rang...  7.62 us
  transfers between devices with their start and end apart: 24, of which 10 were waited for; matrix products, arithmetic and copies ran while one was open for 8% of the time, Pallas kernels for 12%

profile of v3, /device:TPU:1, one launch (start us, length us, event | category | flops | bytes accessed | tf_op | source)
XLA Modules:
  0.0 137.4 jit_solution(2921289167355169201)
XLA Ops:
  0.0 1.0 reshape.263
  1.6 1.1 fusion.7
  2.8 7.8 %collective-permute-start = (bf16[2,4,16,576]{3,1,0,2:T(4,128)(2,1)S(1)}, bf16[2,4,16,576]{3,1,0,2:T(4,128)(2,1)S(1)}, u32[]{:S(2)}, u32[]{:S(2)}) collective-permute-start(bf16[2,4,16,576]{3,1,0,2:T(4,128)(2,1)S(1)} %pad_maximum_fusion.2), channel_id=1, source_target_pairs={{0,4},{1,5},{2,6},{3,7},{4,0},{5,1},{6,2},{7,3},{8,12},{9,13},{10,... | collective-permute-start | bytes 442376 | tf_op jit(solution)/shard_map/ppermute | solution.py:35
  11.7 2.3 %copy-done.1 = bf16[64,128,288]{1,2,0:T(8,128)(2,1)S(1)} copy-done((bf16[64,128,288]{1,2,0:T(8,128)(2,1)S(1)}, bf16[64,128,288]{1,2,0:T(8,128)(2,1)}, u32[]{:S(2)}) %copy-start.1) | copy-done | bytes 4718616
  14.0 1.9 %shard_map.91 = (bf16[2,4,288,128]{3,2,1,0:T(8,128)(2,1)S(1)}, bf16[2,4,288,128]{3,2,1,0:T(8,128)(2,1)}, bf16[2,4,288,128]{3,2,1,0:T(8,128)(2,1)S(1)}, bf16[2,4,...) custom-call(s32[64]{0:T(128)S(1)} %pad_add_fusion.idx_ref, ...), custom_call_target="tpu_custom_call" | custom-call | bytes 9437184 | tf_op jit(solution)/shard_map/pallas_call | solution.py:56
  17.5 0.8 copy-done.4
  20.7 1.6 %collective-permute-start.1 = (bf16[2,4,288,128]{3,2,1,0:T(8,128)(2,1)}, bf16[2,4,288,128]{3,2,1,0:T(8,128)(2,1)S(1)}, u32[]{:S(2)}, u32[]{:S(2)}) collective-permute-start(bf16[2,4,288,128]{3,2,1,0:T(8,128)(2,1)} %get-tuple-element.63), channel_id=1, source_target_pairs={{0,129},{1,130},{2,131},{3,132},{4,133},{5,134},{6,135},{7,128},{8... | collective-permute-start | bytes 1769480 | tf_op jit(solution)/shard_map/ppermute | solution.py:25
  22.2 1.2 collective-permute-start.2
  23.5 1.2 pad_maximum_fusion
  24.7 1.2 broadcast_in_dim.93
  25.9 4.6 %all-to-all-start = ((bf16[8,2,4,16,576]{4,3,2,1,0:T(8,128)(2,1)}), bf16[8,2,4,16,576]{4,3,2,1,0:T(8,128)(2,1)}, u32[]{:S(2)}, u32[]{:S(2)}) async-start(bf16[8,2,4,16,576]{4,3,2,1,0:T(8,128)(2,1)} %bitcast.60), calls=%async_computation | async-start | bytes 2621440 | tf_op jit(solution)/shard_map/all_to_all | solution.py:215
  31.2 1.8 %collective-permute-start.3 = (bf16[2,4,288,128]{3,2,1,0:T(8,128)(2,1)}, bf16[2,4,288,128]{3,2,1,0:T(8,128)(2,1)}, u32[]{:S(2)}, u32[]{:S(2)}) collective-permute-start(bf16[2,4,288,128]{3,2,1,0:T(8,128)(2,1)} %copy-done.6), channel_id=1, source_target_pairs={{0,135},{1,128},{2,129},{3,130},{4,131},{5,132},{6,133},{7,134},{8... | collective-permute-start | bytes 1769480 | tf_op jit(solution)/shard_map/ppermute | solution.py:25
  33.0 1.5 %collective-permute-start.4 = (bf16[2,4,288,128]{3,2,1,0:T(8,128)(2,1)}, bf16[2,4,288,128]{3,2,1,0:T(8,128)(2,1)}, u32[]{:S(2)}, u32[]{:S(2)}) collective-permute-start(bf16[2,4,288,128]{3,2,1,0:T(8,128)(2,1)} %copy-done.5), channel_id=1, source_target_pairs={{0,24},{1,25},{2,26},{3,27},{4,28},{5,29},{6,30},{7,31},{8,0},{9,1... | collective-permute-start | bytes 1769480 | tf_op jit(solution)/shard_map/ppermute | solution.py:31
  35.1 2.7 %collective-permute-done.1.refs_1_ = bf16[2,4,288,128]{3,2,1,0:T(8,128)(2,1)S(1)} collective-permute-done((bf16[2,4,288,128]{3,2,1,0:T(8,128)(2,1)}, bf16[2,4,288,128]{3,2,1,0:T(8,128)(2,1)S(1)}, u32[]{:S(2)}, u32[]{:S(2)}) %collective-permute-start.1) | collective-permute-done | bytes 589856 | tf_op jit(solution)/shard_map/ppermute | solution.py:25
  37.8 2.7 %collective-permute-start.6 = (bf16[2,4,288,128]{3,2,1,0:T(8,128)(2,1)}, bf16[2,4,288,128]{3,2,1,0:T(8,128)(2,1)}, u32[]{:S(2)}, u32[]{:S(2)}) collective-permute-start(bf16[2,4,288,128]{3,2,1,0:T(8,128)(2,1)} %copy-done.3), channel_id=1, source_target_pairs={{0,16},{1,17},{2,18},{3,19},{4,20},{5,21},{6,22},{7,23},{8,24},{9,... | collective-permute-start | bytes 1769480 | tf_op jit(solution)/shard_map/ppermute | solution.py:31
  40.6 0.8 collective-permute-start.7
  41.4 1.3 fusion.22
  44.0 3.4 %collective-permute-done.3.refs_2_ = bf16[2,4,288,128]{3,2,1,0:T(8,128)(2,1)} collective-permute-done((bf16[2,4,288,128]{3,2,1,0:T(8,128)(2,1)}, bf16[2,4,288,128]{3,2,1,0:T(8,128)(2,1)}, u32[]{:S(2)}, u32[]{:S(2)}) %collective-permute-start.3) | collective-permute-done | bytes 589856 | tf_op jit(solution)/shard_map/ppermute | solution.py:25
  47.7 5.0 %collective-permute-done.5.refs_3_ = bf16[2,4,288,128]{3,2,1,0:T(8,128)(2,1)} collective-permute-done((bf16[2,4,288,128]{3,2,1,0:T(8,128)(2,1)}, bf16[2,4,288,128]{3,2,1,0:T(8,128)(2,1)}, u32[]{:S(2)}, u32[]{:S(2)}) %collective-permute-start.5) | collective-permute-done | bytes 589856 | tf_op jit(solution)/shard_map/ppermute | solution.py:25
  52.8 1.2 collective-permute-done.6.refs_2_
  54.0 2.3 %shard_map.92 = (bf16[4,288,128]{2,1,0:T(8,128)(2,1)S(1)}, bf16[4,288,128]{2,1,0:T(8,128)(2,1)S(1)}, bf16[4,288,128]{2,1,0:T(8,128)(2,1)S(1)}, bf16[4,288,128]{2...) custom-call(bf16[2,4,288,128]{3,2,1,0:T(8,128)(2,1)S(1)} %get-tuple-, ...), custom_call_target="tpu_custom_call" | custom-call | bytes 4718592 | tf_op jit(solution)/shard_map/pallas_call | solution.py:77
  57.0 6.6 %collective-permute-start.8 = (bf16[4,288,128]{2,1,0:T(8,128)(2,1)S(1)}, bf16[4,288,128]{2,1,0:T(8,128)(2,1)S(1)}, u32[]{:S(2)}, u32[]{:S(2)}) collective-permute-start(bf16[4,288,128]{2,1,0:T(8,128)(2,1)S(1)} %get-tuple-element.81), channel_id=1, source_target_pairs={{0,1},{1,2},{2,3},{3,4},{4,5},{5,6},{6,7},{7,0},{8,9},{9,10},{10,1... | collective-permute-start | bytes 884744 | tf_op jit(solution)/shard_map/ppermute | solution.py:25
  63.7 1.7 %collective-permute-start.10 = (bf16[4,288,128]{2,1,0:T(8,128)(2,1)S(1)}, bf16[4,288,128]{2,1,0:T(8,128)(2,1)S(1)}, u32[]{:S(2)}, u32[]{:S(2)}) collective-permute-start(bf16[4,288,128]{2,1,0:T(8,128)(2,1)S(1)} %get-tuple-element.84), channel_id=1, source_target_pairs={{0,7},{1,0},{2,1},{3,2},{4,3},{5,4},{6,5},{7,6},{8,15},{9,8},{10,9... | collective-permute-start | bytes 884744 | tf_op jit(solution)/shard_map/ppermute | solution.py:25
  65.4 1.0 collective-permute-start.12
  66.4 2.4 %shard_map.93 = (bf16[4,288,128]{2,1,0:T(8,128)(2,1)S(1)}, bf16[4,288,128]{2,1,0:T(8,128)(2,1)S(1)}, bf16[4,288,128]{2,1,0:T(8,128)(2,1)S(1)}, bf16[4,288,128]{2...) custom-call(bf16[2,4,288,128]{3,2,1,0:T(8,128)(2,1)} %collective-per, ...), custom_call_target="tpu_custom_call" | custom-call | bytes 4718592 | tf_op jit(solution)/shard_map/pallas_call | solution.py:77
  68.8 1.7 %collective-permute-start.14 = (bf16[4,288,128]{2,1,0:T(8,128)(2,1)S(1)}, bf16[4,288,128]{2,1,0:T(8,128)(2,1)S(1)}, u32[]{:S(2)}, u32[]{:S(2)}) collective-permute-start(bf16[4,288,128]{2,1,0:T(8,128)(2,1)S(1)} %get-tuple-element.97), channel_id=1, source_target_pairs={{0,8},{1,9},{2,10},{3,11},{4,12},{5,13},{6,14},{7,15},{8,16},{9,17... | collective-permute-start | bytes 884744 | tf_op jit(solution)/shard_map/ppermute | solution.py:31
  70.5 1.8 %collective-permute-start.16 = (bf16[4,288,128]{2,1,0:T(8,128)(2,1)S(1)}, bf16[4,288,128]{2,1,0:T(8,128)(2,1)S(1)}, u32[]{:S(2)}, u32[]{:S(2)}) collective-permute-start(bf16[4,288,128]{2,1,0:T(8,128)(2,1)S(1)} %get-tuple-element.100), channel_id=1, source_target_pairs={{0,16},{1,17},{2,18},{3,19},{4,20},{5,21},{6,22},{7,23},{8,24},{9,... | collective-permute-start | bytes 884744 | tf_op jit(solution)/shard_map/ppermute | solution.py:31
  72.3 1.7 %collective-permute-start.18 = (bf16[4,288,128]{2,1,0:T(8,128)(2,1)S(1)}, bf16[4,288,128]{2,1,0:T(8,128)(2,1)S(1)}, u32[]{:S(2)}, u32[]{:S(2)}) collective-permute-start(bf16[4,288,128]{2,1,0:T(8,128)(2,1)S(1)} %get-tuple-element.103), channel_id=1, source_target_pairs={{0,24},{1,25},{2,26},{3,27},{4,28},{5,29},{6,30},{7,31},{8,0},{9,1... | collective-permute-start | bytes 884744 | tf_op jit(solution)/shard_map/ppermute | solution.py:31
  73.9 1.1 collective-permute-start.9
  75.2 1.4 %fusion.35 = (bf16[1,8,4,16,576]{4,3,2,0,1:T(8,128)(2,1)S(1)}, bf16[1,8,4,16,576]{4,3,2,0,1:T(8,128)(2,1)S(1)}) fusion(bf16[2,8,4,16,576]{4,3,2,0,1:T(8,128)(2,1)} %bitcast.11), kind=kLoop, calls=%fused_computation.76 | loop fusion | bytes 2359296 | tf_op jit(solution)/shard_map/slice | solution.py:232
  76.6 3.4 %collective-permute-done.12.rest_3_ = bf16[4,288,128]{2,1,0:T(8,128)(2,1)S(1)} collective-permute-done((bf16[4,288,128]{2,1,0:T(8,128)(2,1)S(1)}, bf16[4,288,128]{2,1,0:T(8,128)(2,1)S(1)}, u32[]{:S(2)}, u32[]{:S(2)}) %collective-permute-start.12) | collective-permute-done | bytes 294944 | tf_op jit(solution)/shard_map/ppermute | solution.py:25
  80.3 1.7 %collective-permute-start.13 = (bf16[4,288,128]{2,1,0:T(8,128)(2,1)}, bf16[4,288,128]{2,1,0:T(8,128)(2,1)}, u32[]{:S(2)}, u32[]{:S(2)}) collective-permute-start(bf16[4,288,128]{2,1,0:T(8,128)(2,1)} %get-tuple-element.88), channel_id=1, source_target_pairs={{0,2},{1,7},{2,4},{3,1},{4,6},{5,3},{6,0},{7,5},{8,10},{9,15},{10,... | collective-permute-start | bytes 884744 | tf_op jit(solution)/shard_map/ppermute | solution.py:25
  82.0 1.5 %collective-permute-done.16.rest_6_ = bf16[4,288,128]{2,1,0:T(8,128)(2,1)S(1)} collective-permute-done((bf16[4,288,128]{2,1,0:T(8,128)(2,1)S(1)}, bf16[4,288,128]{2,1,0:T(8,128)(2,1)S(1)}, u32[]{:S(2)}, u32[]{:S(2)}) %collective-permute-start.16) | collective-permute-done | bytes 294944 | tf_op jit(solution)/shard_map/ppermute | solution.py:31
  83.6 3.3 %collective-permute-start.17 = (bf16[4,288,128]{2,1,0:T(8,128)(2,1)}, bf16[4,288,128]{2,1,0:T(8,128)(2,1)}, u32[]{:S(2)}, u32[]{:S(2)}) collective-permute-start(bf16[4,288,128]{2,1,0:T(8,128)(2,1)} %get-tuple-element.101), channel_id=1, source_target_pairs={{0,16},{1,17},{2,18},{3,19},{4,20},{5,21},{6,22},{7,23},{8,24},{9,... | collective-permute-start | bytes 884744 | tf_op jit(solution)/shard_map/ppermute | solution.py:31
  86.9 2.9 %collective-permute-start.19 = (bf16[4,288,128]{2,1,0:T(8,128)(2,1)}, bf16[4,288,128]{2,1,0:T(8,128)(2,1)}, u32[]{:S(2)}, u32[]{:S(2)}) collective-permute-start(bf16[4,288,128]{2,1,0:T(8,128)(2,1)} %get-tuple-element.104), channel_id=1, source_target_pairs={{0,24},{1,25},{2,26},{3,27},{4,28},{5,29},{6,30},{7,31},{8,0},{9,1... | collective-permute-start | bytes 884744 | tf_op jit(solution)/shard_map/ppermute | solution.py:31
  89.8 5.6 %shard_map.95 = bf16[512,640]{1,0:T(8,128)(2,1)} custom-call(s32[18]{0:T(128)S(1)} %add_add_fusion.1.scal_ref, bf16[512,576]{1,0:T(8,128)(2,1)S(1)} %bitcast.57, bf16[4,288,128]{2,1,0:T(8,128)(2,1)S(1)} %get-tuple-element.78.rest_0_, bf16[4,288,128]{2,1,0:T(8,128)(2,1)S(1)} %collective-permute-done.8.rest_1_, ...), custom_call_target="tpu_custom_call" | custom-call | flops 18253611008 | bytes 3473408 | tf_op jit(solution)/shard_map/pallas_call | solution.py:154
  95.4 9.3 %all-to-all-start.2 = ((bf16[8,64,640]{2,1,0:T(8,128)(2,1)}), bf16[8,64,640]{2,1,0:T(8,128)(2,1)}, u32[]{:S(2)}, u32[]{:S(2)}) async-start(bf16[8,64,640]{2,1,0:T(8,128)(2,1)} %bitcast.18), calls=%async_computation.2 | async-start | bytes 1310720 | tf_op jit(solution)/shard_map/all_to_all | solution.py:233
  104.7 1.0 copy-done.8
  105.7 1.0 copy-done.10
  106.7 1.0 copy-done.12
  107.6 7.1 %shard_map.94 = bf16[512,640]{1,0:T(8,128)(2,1)} custom-call(s32[18]{0:T(128)S(1)} %add_add_fusion.scal_ref, bf16[512,576]{1,0:T(8,128)(2,1)S(1)} %bitcast.56, bf16[4,288,128]{2,1,0:T(8,128)(2,1)S(1)} %copy-done.8, bf16[4,288,128]{2,1,0:T(8,128)(2,1)S(1)} %copy-done.12, bf16[4,288,128]{2,1,0:T(8,128)(2,1)} %collective-permute-done.11.rest_2_, ...), custom_call_target="tpu_custom_call" | custom-call | flops 18253611008 | bytes 3473408 | tf_op jit(solution)/shard_map/pallas_call | solution.py:154
  114.7 0.8 all-to-all-done.2
  115.6 4.0 %all-to-all-start.1 = ((bf16[8,64,640]{2,1,0:T(8,128)(2,1)}), bf16[8,64,640]{2,1,0:T(8,128)(2,1)S(1)}, u32[]{:S(2)}, u32[]{:S(2)}) async-start(bf16[8,64,640]{2,1,0:T(8,128)(2,1)} %bitcast.15), calls=%async_computation.1 | async-start | bytes 1310720 | tf_op jit(solution)/shard_map/all_to_all | solution.py:242
  119.5 1.0 convert_reduce_fusion.1
  120.8 1.2 multiply_reduce_fusion.1
  122.2 4.3 %collective-permute-start.20 = (bf16[2,64,640]{2,1,0:T(8,128)(2,1)S(1)}, bf16[2,64,640]{2,1,0:T(8,128)(2,1)S(1)}, u32[]{:S(2)}, u32[]{:S(2)}) collective-permute-start(bf16[2,64,640]{2,1,0:T(8,128)(2,1)S(1)} %pad_maximum_fusion.3), channel_id=1, source_target_pairs={{0,4},{1,5},{2,6},{3,7},{4,0},{5,1},{6,2},{7,3},{8,12},{9,13},{10,... | collective-permute-start | bytes 491528 | tf_op jit(solution)/shard_map/ppermute | solution.py:35
  126.5 7.6 %collective-permute-done.20 = bf16[2,64,640]{2,1,0:T(8,128)(2,1)S(1)} collective-permute-done((bf16[2,64,640]{2,1,0:T(8,128)(2,1)S(1)}, bf16[2,64,640]{2,1,0:T(8,128)(2,1)S(1)}, u32[]{:S(2)}, u32[]{:S(2)}) %collective-permute-start.20) | collective-permute-done | bytes 163872 | tf_op jit(solution)/shard_map/ppermute | solution.py:35
  134.7 2.0 %fusion.13 = bf16[16,2,1,4,128]{4,3,2,1,0:T(4,128)(2,1)S(1)} fusion(bf16[16,512,128]{2,1,0:T(8,128)(2,1)} %param.16, bf16[2,4,16,512]{3,2,1,0:T(8,128)(2,1)S(1)} %divide_convert_fusion), kind=kOutput, calls=%fused_computation.8 | convolution fusion | flops 16793600 | bytes 2260992 | tf_op jit(solution)/shard_map/bshk,hkv->bshv/dot_general | solution.py:246
  (90 shorter events, 11.5 us)
Async XLA Ops:
  0.0 1.6 %copy-start = (bf16[16,128,512]{2,1,0:T(8,128)(2,1)S(1)}, bf16[16,128,512]{2,1,0:T(8,128)(2,1)}, u32[]{:S(2)}) copy-start(bf16[16,128,512]{2,1,0:T(8,128)(2,1)} %param.15) | copy-start | bytes 6291460
  0.0 10.7 %copy-start.18 = (s32[2]{0:T(128)S(1)}, s32[2]{0:T(128)}, u32[]{:S(2)}) copy-start(s32[2]{0:T(128)} %constant.123.clone) | copy-start | bytes 28
  0.0 10.9 %copy-start.16 = (s32[64]{0:T(128)S(1)}, s32[64]{0:T(128)}, u32[]{:S(2)}) copy-start(s32[64]{0:T(128)} %param.11) | copy-start | bytes 772
  2.8 17.2 %collective-permute-start = (bf16[2,4,16,576]{3,1,0,2:T(4,128)(2,1)S(1)}, bf16[2,4,16,576]{3,1,0,2:T(4,128)(2,1)S(1)}, u32[]{:S(2)}, u32[]{:S(2)}) collective-permute-start(bf16[2,4,16,576]{3,1,0,2:T(4,128)(2,1)S(1)} %pad_maximum_fusion.2), channel_id=1, source_target_pairs={{0,4},{1,5},{2,6},{3,7},{4,0},{5,1},{6,2},{7,3},{8,12},{9,13},{10,... | collective-permute-start | bytes 442376 | tf_op jit(solution)/shard_map/ppermute | solution.py:35
  11.7 2.3 %copy-start.1 = (bf16[64,128,288]{1,2,0:T(8,128)(2,1)S(1)}, bf16[64,128,288]{1,2,0:T(8,128)(2,1)}, u32[]{:S(2)}) copy-start(bf16[64,128,288]{1,2,0:T(8,128)(2,1)} %param.9) | copy-start | bytes 14155780
  15.9 0.8 copy-start.2
  16.7 0.8 copy-start.3
  17.5 0.8 copy-start.4
  18.4 0.8 copy-start.5
  19.2 0.8 copy-start.6
  20.0 0.6 copy-start.14
  20.7 17.2 %collective-permute-start.1 = (bf16[2,4,288,128]{3,2,1,0:T(8,128)(2,1)}, bf16[2,4,288,128]{3,2,1,0:T(8,128)(2,1)S(1)}, u32[]{:S(2)}, u32[]{:S(2)}) collective-permute-start(bf16[2,4,288,128]{3,2,1,0:T(8,128)(2,1)} %get-tuple-element.63), channel_id=1, source_target_pairs={{0,129},{1,130},{2,131},{3,132},{4,133},{5,134},{6,135},{7,128},{8... | collective-permute-start | bytes 1769480 | tf_op jit(solution)/shard_map/ppermute | solution.py:25
  22.2 18.3 %collective-permute-start.2 = (bf16[2,4,288,128]{3,2,1,0:T(8,128)(2,1)}, bf16[2,4,288,128]{3,2,1,0:T(8,128)(2,1)}, u32[]{:S(2)}, u32[]{:S(2)}) collective-permute-start(bf16[2,4,288,128]{3,2,1,0:T(8,128)(2,1)} %get-tuple-element.64), channel_id=1, source_target_pairs={{0,8},{1,9},{2,10},{3,11},{4,12},{5,13},{6,14},{7,15},{8,16},{9,17... | collective-permute-start | bytes 1769480 | tf_op jit(solution)/shard_map/ppermute | solution.py:31
  24.7 5.8 %copy-start.17 = (s32[64]{0:T(128)S(1)}, s32[64]{0:T(128)}, u32[]{:S(2)}) copy-start(s32[64]{0:T(128)} %param.10) | copy-start | bytes 772
  24.7 18.2 %copy-start.15 = (bf16[2,4,576]{2,1,0:T(4,128)(2,1)S(1)}, bf16[2,4,576]{2,1,0:T(4,128)(2,1)}, u32[]{:S(2)}) copy-start(bf16[2,4,576]{2,1,0:T(4,128)(2,1)} %param.14) | copy-start | bytes 27652
  25.9 28.1 %all-to-all-start = ((bf16[8,2,4,16,576]{4,3,2,1,0:T(8,128)(2,1)}), bf16[8,2,4,16,576]{4,3,2,1,0:T(8,128)(2,1)}, u32[]{:S(2)}, u32[]{:S(2)}) async-start(bf16[8,2,4,16,576]{4,3,2,1,0:T(8,128)(2,1)} %bitcast.60), calls=%async_computation | async-start | bytes 2621440 | tf_op jit(solution)/shard_map/all_to_all | solution.py:215
  31.2 16.2 %collective-permute-start.3 = (bf16[2,4,288,128]{3,2,1,0:T(8,128)(2,1)}, bf16[2,4,288,128]{3,2,1,0:T(8,128)(2,1)}, u32[]{:S(2)}, u32[]{:S(2)}) collective-permute-start(bf16[2,4,288,128]{3,2,1,0:T(8,128)(2,1)} %copy-done.6), channel_id=1, source_target_pairs={{0,135},{1,128},{2,129},{3,130},{4,131},{5,132},{6,133},{7,134},{8... | collective-permute-start | bytes 1769480 | tf_op jit(solution)/shard_map/ppermute | solution.py:25
  33.0 14.7 %collective-permute-start.4 = (bf16[2,4,288,128]{3,2,1,0:T(8,128)(2,1)}, bf16[2,4,288,128]{3,2,1,0:T(8,128)(2,1)}, u32[]{:S(2)}, u32[]{:S(2)}) collective-permute-start(bf16[2,4,288,128]{3,2,1,0:T(8,128)(2,1)} %copy-done.5), channel_id=1, source_target_pairs={{0,24},{1,25},{2,26},{3,27},{4,28},{5,29},{6,30},{7,31},{8,0},{9,1... | collective-permute-start | bytes 1769480 | tf_op jit(solution)/shard_map/ppermute | solution.py:31
  34.5 18.3 %collective-permute-start.5 = (bf16[2,4,288,128]{3,2,1,0:T(8,128)(2,1)}, bf16[2,4,288,128]{3,2,1,0:T(8,128)(2,1)}, u32[]{:S(2)}, u32[]{:S(2)}) collective-permute-start(bf16[2,4,288,128]{3,2,1,0:T(8,128)(2,1)} %copy-done.4), channel_id=1, source_target_pairs={{0,130},{1,135},{2,132},{3,129},{4,134},{5,131},{6,128},{7,133},{8... | collective-permute-start | bytes 1769480 | tf_op jit(solution)/shard_map/ppermute | solution.py:25
  37.8 16.1 %collective-permute-start.6 = (bf16[2,4,288,128]{3,2,1,0:T(8,128)(2,1)}, bf16[2,4,288,128]{3,2,1,0:T(8,128)(2,1)}, u32[]{:S(2)}, u32[]{:S(2)}) collective-permute-start(bf16[2,4,288,128]{3,2,1,0:T(8,128)(2,1)} %copy-done.3), channel_id=1, source_target_pairs={{0,16},{1,17},{2,18},{3,19},{4,20},{5,21},{6,22},{7,23},{8,24},{9,... | collective-permute-start | bytes 1769480 | tf_op jit(solution)/shard_map/ppermute | solution.py:31
  40.6 13.4 %collective-permute-start.7 = (bf16[2,4,288,128]{3,2,1,0:T(8,128)(2,1)}, bf16[2,4,288,128]{3,2,1,0:T(8,128)(2,1)}, u32[]{:S(2)}, u32[]{:S(2)}) collective-permute-start(bf16[2,4,288,128]{3,2,1,0:T(8,128)(2,1)} %copy-done.2), channel_id=1, source_target_pairs={{0,128},{1,129},{2,130},{3,131},{4,132},{5,133},{6,134},{7,135},{8... | collective-permute-start | bytes 1769480 | tf_op jit(solution)/shard_map/ppermute | solution.py:25
  54.0 11.4 %copy-start.13 = (bf16[1,4,576]{1,2,0:T(8,128)(2,1)S(1)}, bf16[1,4,576]{1,2,0:T(8,128)(2,1)}, u32[]{:S(2)}) copy-start(bf16[1,4,576]{1,2,0:T(8,128)(2,1)} %copy.35) | copy-start | bytes 13828
  56.3 0.7 copy-start.7
  57.0 15.3 %collective-permute-start.8 = (bf16[4,288,128]{2,1,0:T(8,128)(2,1)S(1)}, bf16[4,288,128]{2,1,0:T(8,128)(2,1)S(1)}, u32[]{:S(2)}, u32[]{:S(2)}) collective-permute-start(bf16[4,288,128]{2,1,0:T(8,128)(2,1)S(1)} %get-tuple-element.81), channel_id=1, source_target_pairs={{0,1},{1,2},{2,3},{3,4},{4,5},{5,6},{6,7},{7,0},{8,9},{9,10},{10,1... | collective-permute-start | bytes 884744 | tf_op jit(solution)/shard_map/ppermute | solution.py:25
  63.7 10.3 %collective-permute-start.10 = (bf16[4,288,128]{2,1,0:T(8,128)(2,1)S(1)}, bf16[4,288,128]{2,1,0:T(8,128)(2,1)S(1)}, u32[]{:S(2)}, u32[]{:S(2)}) collective-permute-start(bf16[4,288,128]{2,1,0:T(8,128)(2,1)S(1)} %get-tuple-element.84), channel_id=1, source_target_pairs={{0,7},{1,0},{2,1},{3,2},{4,3},{5,4},{6,5},{7,6},{8,15},{9,8},{10,9... | collective-permute-start | bytes 884744 | tf_op jit(solution)/shard_map/ppermute | solution.py:25
  65.4 14.6 %collective-permute-start.12 = (bf16[4,288,128]{2,1,0:T(8,128)(2,1)S(1)}, bf16[4,288,128]{2,1,0:T(8,128)(2,1)S(1)}, u32[]{:S(2)}, u32[]{:S(2)}) collective-permute-start(bf16[4,288,128]{2,1,0:T(8,128)(2,1)S(1)} %get-tuple-element.87), channel_id=1, source_target_pairs={{0,2},{1,7},{2,4},{3,1},{4,6},{5,3},{6,0},{7,5},{8,10},{9,15},{10,... | collective-permute-start | bytes 884744 | tf_op jit(solution)/shard_map/ppermute | solution.py:25
  68.8 6.4 %copy-start.9 = (bf16[4,288,128]{2,1,0:T(8,128)(2,1)}, bf16[4,288,128]{2,1,0:T(8,128)(2,1)S(1)}, u32[]{:S(2)}) copy-start(bf16[4,288,128]{2,1,0:T(8,128)(2,1)S(1)} %get-tuple-element.95.rest_4_) | copy-start | bytes 884740
  68.8 11.5 %collective-permute-start.14 = (bf16[4,288,128]{2,1,0:T(8,128)(2,1)S(1)}, bf16[4,288,128]{2,1,0:T(8,128)(2,1)S(1)}, u32[]{:S(2)}, u32[]{:S(2)}) collective-permute-start(bf16[4,288,128]{2,1,0:T(8,128)(2,1)S(1)} %get-tuple-element.97), channel_id=1, source_target_pairs={{0,8},{1,9},{2,10},{3,11},{4,12},{5,13},{6,14},{7,15},{8,16},{9,17... | collective-permute-start | bytes 884744 | tf_op jit(solution)/shard_map/ppermute | solution.py:31
  70.5 13.0 %collective-permute-start.16 = (bf16[4,288,128]{2,1,0:T(8,128)(2,1)S(1)}, bf16[4,288,128]{2,1,0:T(8,128)(2,1)S(1)}, u32[]{:S(2)}, u32[]{:S(2)}) collective-permute-start(bf16[4,288,128]{2,1,0:T(8,128)(2,1)S(1)} %get-tuple-element.100), channel_id=1, source_target_pairs={{0,16},{1,17},{2,18},{3,19},{4,20},{5,21},{6,22},{7,23},{8,24},{9,... | collective-permute-start | bytes 884744 | tf_op jit(solution)/shard_map/ppermute | solution.py:31
  72.3 11.3 %collective-permute-start.18 = (bf16[4,288,128]{2,1,0:T(8,128)(2,1)S(1)}, bf16[4,288,128]{2,1,0:T(8,128)(2,1)S(1)}, u32[]{:S(2)}, u32[]{:S(2)}) collective-permute-start(bf16[4,288,128]{2,1,0:T(8,128)(2,1)S(1)} %get-tuple-element.103), channel_id=1, source_target_pairs={{0,24},{1,25},{2,26},{3,27},{4,28},{5,29},{6,30},{7,31},{8,0},{9,1... | collective-permute-start | bytes 884744 | tf_op jit(solution)/shard_map/ppermute | solution.py:31
  73.9 12.9 %collective-permute-start.9 = (bf16[4,288,128]{2,1,0:T(8,128)(2,1)S(1)}, bf16[4,288,128]{2,1,0:T(8,128)(2,1)S(1)}, u32[]{:S(2)}, u32[]{:S(2)}) collective-permute-start(bf16[4,288,128]{2,1,0:T(8,128)(2,1)S(1)} %get-tuple-element.82), channel_id=1, source_target_pairs={{0,1},{1,2},{2,3},{3,4},{4,5},{5,6},{6,7},{7,0},{8,9},{9,10},{10,1... | collective-permute-start | bytes 884744 | tf_op jit(solution)/shard_map/ppermute | solution.py:25
  80.0 24.7 %collective-permute-start.11 = (bf16[4,288,128]{2,1,0:T(8,128)(2,1)}, bf16[4,288,128]{2,1,0:T(8,128)(2,1)}, u32[]{:S(2)}, u32[]{:S(2)}) collective-permute-start(bf16[4,288,128]{2,1,0:T(8,128)(2,1)} %get-tuple-element.85), channel_id=1, source_target_pairs={{0,7},{1,0},{2,1},{3,2},{4,3},{5,4},{6,5},{7,6},{8,15},{9,8},{10,9... | collective-permute-start | bytes 884744 | tf_op jit(solution)/shard_map/ppermute | solution.py:25
  80.3 24.4 %collective-permute-start.13 = (bf16[4,288,128]{2,1,0:T(8,128)(2,1)}, bf16[4,288,128]{2,1,0:T(8,128)(2,1)}, u32[]{:S(2)}, u32[]{:S(2)}) collective-permute-start(bf16[4,288,128]{2,1,0:T(8,128)(2,1)} %get-tuple-element.88), channel_id=1, source_target_pairs={{0,2},{1,7},{2,4},{3,1},{4,6},{5,3},{6,0},{7,5},{8,10},{9,15},{10,... | collective-permute-start | bytes 884744 | tf_op jit(solution)/shard_map/ppermute | solution.py:25
  83.5 21.2 %collective-permute-start.15 = (bf16[4,288,128]{2,1,0:T(8,128)(2,1)}, bf16[4,288,128]{2,1,0:T(8,128)(2,1)}, u32[]{:S(2)}, u32[]{:S(2)}) collective-permute-start(bf16[4,288,128]{2,1,0:T(8,128)(2,1)} %get-tuple-element.98), channel_id=1, source_target_pairs={{0,8},{1,9},{2,10},{3,11},{4,12},{5,13},{6,14},{7,15},{8,16},{9,17... | collective-permute-start | bytes 884744 | tf_op jit(solution)/shard_map/ppermute | solution.py:31
  83.6 21.1 %collective-permute-start.17 = (bf16[4,288,128]{2,1,0:T(8,128)(2,1)}, bf16[4,288,128]{2,1,0:T(8,128)(2,1)}, u32[]{:S(2)}, u32[]{:S(2)}) collective-permute-start(bf16[4,288,128]{2,1,0:T(8,128)(2,1)} %get-tuple-element.101), channel_id=1, source_target_pairs={{0,16},{1,17},{2,18},{3,19},{4,20},{5,21},{6,22},{7,23},{8,24},{9,... | collective-permute-start | bytes 884744 | tf_op jit(solution)/shard_map/ppermute | solution.py:31
  86.9 8.5 %copy-start.11 = (bf16[4,288,128]{2,1,0:T(8,128)(2,1)}, bf16[4,288,128]{2,1,0:T(8,128)(2,1)S(1)}, u32[]{:S(2)}) copy-start(bf16[4,288,128]{2,1,0:T(8,128)(2,1)S(1)} %collective-permute-done.9.rest_1_) | copy-start | bytes 884740
  86.9 17.8 %collective-permute-start.19 = (bf16[4,288,128]{2,1,0:T(8,128)(2,1)}, bf16[4,288,128]{2,1,0:T(8,128)(2,1)}, u32[]{:S(2)}, u32[]{:S(2)}) collective-permute-start(bf16[4,288,128]{2,1,0:T(8,128)(2,1)} %get-tuple-element.104), channel_id=1, source_target_pairs={{0,24},{1,25},{2,26},{3,27},{4,28},{5,29},{6,30},{7,31},{8,0},{9,1... | collective-permute-start | bytes 884744 | tf_op jit(solution)/shard_map/ppermute | solution.py:31
  95.4 20.2 %all-to-all-start.2 = ((bf16[8,64,640]{2,1,0:T(8,128)(2,1)}), bf16[8,64,640]{2,1,0:T(8,128)(2,1)}, u32[]{:S(2)}, u32[]{:S(2)}) async-start(bf16[8,64,640]{2,1,0:T(8,128)(2,1)} %bitcast.18), calls=%async_computation.2 | async-start | bytes 1310720 | tf_op jit(solution)/shard_map/all_to_all | solution.py:233
  104.7 1.0 copy-start.8
  105.7 1.0 copy-start.10
  106.7 1.0 copy-start.12
  115.6 18.5 %all-to-all-start.1 = ((bf16[8,64,640]{2,1,0:T(8,128)(2,1)}), bf16[8,64,640]{2,1,0:T(8,128)(2,1)S(1)}, u32[]{:S(2)}, u32[]{:S(2)}) async-start(bf16[8,64,640]{2,1,0:T(8,128)(2,1)} %bitcast.15), calls=%async_computation.1 | async-start | bytes 1310720 | tf_op jit(solution)/shard_map/all_to_all | solution.py:242
  122.2 11.9 %collective-permute-start.20 = (bf16[2,64,640]{2,1,0:T(8,128)(2,1)S(1)}, bf16[2,64,640]{2,1,0:T(8,128)(2,1)S(1)}, u32[]{:S(2)}, u32[]{:S(2)}) collective-permute-start(bf16[2,64,640]{2,1,0:T(8,128)(2,1)S(1)} %pad_maximum_fusion.3), channel_id=1, source_target_pairs={{0,4},{1,5},{2,6},{3,7},{4,0},{5,1},{6,2},{7,3},{8,12},{9,13},{10,... | collective-permute-start | bytes 491528 | tf_op jit(solution)/shard_map/ppermute | solution.py:35

commit v4 on v3

--- a/solution.py
+++ b/solution.py
@@ -40,7 +40,7 @@
 
 
 def lookup(slots, values, want):
-    return jnp.max(jnp.where(slots == want[..., None], values, 0), axis=-1)
+    return jnp.max(jnp.where(slots == jnp.expand_dims(want, -1), values, 0), axis=-1)
 
 
 def pick_kernel(idx_ref, k_ref, *outs):
@@ -57,7 +57,7 @@
         pick_kernel,
         in_specs=[pl.BlockSpec(memory_space=pltpu.SMEM), vm],
         out_specs=[vm] * 8,
-        out_shape=[pltpu.VMEM((2, 4, *block), k.dtype)] * 8,
+        out_shape=[pltpu.HBM((2, 4, *block), k.dtype)] * 8,
         compiler_params=pltpu.CompilerParams(vmem_limit_bytes=12 * 1024 * 1024),
         cost_estimate=pl.CostEstimate(flops=0, bytes_accessed=2 * 64 * block[0] * block[1] * 2, transcendentals=0),
     )(idx, k)
@@ -78,7 +78,7 @@
         regroup_kernel,
         in_specs=[vm] * 4,
         out_specs=[vm] * 8,
-        out_shape=[pltpu.VMEM(shape, parts[0].dtype)] * 8,
+        out_shape=[pltpu.VMEM(shape, parts[0].dtype)] * 4 + [pltpu.HBM(shape, parts[0].dtype)] * 4,
         compiler_params=pltpu.CompilerParams(vmem_limit_bytes=8 * 1024 * 1024),
         cost_estimate=pl.CostEstimate(flops=0, bytes_accessed=2 * 8 * size * 2, transcendentals=0),
     )(*parts)
@@ -89,7 +89,7 @@
     rest = rest[8:]
     if fresh:
         new_ref, rest = rest[0], rest[1:]
-    o_ref, kt, s_ref = rest
+    o_ref, kt, s_ref = rest[:3]
     half = mine[0].shape[1]
     latent = o_ref.shape[1] - LANES
     rows = q_ref.shape[0]
@@ -98,12 +98,26 @@
     at_recv = pl.ds(pl.multiple_of((1 - role) * half, 32), half)
     chunk = 4 * LANES
     lane = lax.broadcasted_iota(jnp.int32, (1, LANES), 1)
+    nt = (((1,), (1,)), ((), ()))
     high = jnp.full((rows, LANES), NEG, jnp.float32)
+    copies = []
+    if fresh:
+        sems = rest[3]
+        for j in range(4):
+            for c in range(4):
+                cols, n = pl.ds(j * chunk + c * LANES, LANES), 8 * j + 2 * c
+                copies.append(pltpu.make_async_copy(mine[c].at[j], kt.at[at_mine, cols], sems.at[n]))
+                copies.append(pltpu.make_async_copy(recv[j].at[c], kt.at[at_recv, cols], sems.at[n + 1]))
+        for copy in copies:
+            copy.start()
     for j in range(4):
-        for c in range(4):
-            cols = slice(j * chunk + c * LANES, j * chunk + (c + 1) * LANES)
-            kt[at_mine, cols] = mine[c][j]
-            kt[at_recv, cols] = recv[j][c]
+        for copy in copies[8 * j:8 * j + 8]:
+            copy.wait()
+        if not fresh:
+            for c in range(4):
+                cols = slice(j * chunk + c * LANES, j * chunk + (c + 1) * LANES)
+                kt[at_mine, cols] = mine[c][j]
+                kt[at_recv, cols] = recv[j][c]
         s = jnp.dot(q_ref[...], kt[:, j * chunk:(j + 1) * chunk], preferred_element_type=jnp.float32)
         for c in range(4):
             t = s[:, c * LANES:(c + 1) * LANES] * scale
@@ -111,7 +125,7 @@
             s_ref[:, j * chunk + c * LANES:j * chunk + (c + 1) * LANES] = t
             high = jnp.maximum(high, t)
     if fresh:
-        t = jnp.dot(q_ref[...], new_ref[...], preferred_element_type=jnp.float32) * scale
+        t = lax.dot_general(q_ref[...], new_ref[...], nt, preferred_element_type=jnp.float32) * scale
         step = (lax.broadcasted_iota(jnp.int32, (rows, LANES), 0) // 16) % 4
         u = lax.broadcasted_iota(jnp.int32, (rows, LANES), 1)
         f = jnp.where((u <= step) & (scal_ref[17] == 0), t, NEG)
@@ -119,7 +133,6 @@
     m = jnp.maximum(jnp.max(high, axis=1, keepdims=True), -1e29)
     total = jnp.zeros((rows, LANES), jnp.float32)
     acc = jnp.zeros((rows, latent), jnp.float32)
-    nt = (((1,), (1,)), ((), ()))
     for j in range(4):
         w = jnp.exp(s_ref[:, j * chunk:(j + 1) * chunk] - m)
         for c in range(4):
@@ -129,7 +142,7 @@
     if fresh:
         w = jnp.exp(f - m)
         total = total + w
-        acc = acc + lax.dot_general(w.astype(jnp.bfloat16), new_ref[:latent, :], nt, preferred_element_type=jnp.float32)
+        acc = acc + jnp.dot(w.astype(jnp.bfloat16), new_ref[:, :latent], preferred_element_type=jnp.float32)
     norm = jnp.sum(total, axis=1, keepdims=True)
     some = norm > 0.0
     safe = jnp.where(some, norm, 1.0)
@@ -149,14 +162,17 @@
     rows, width = q.shape
     fresh = new is not None
     vm = pl.BlockSpec(memory_space=pltpu.VMEM)
+    if fresh:
+        mine, recv = [[pltpu.with_memory_space_constraint(a, pltpu.HBM) for a in side] for side in (mine, recv)]
     args = [q, *mine, *recv] + ([new] if fresh else [])
     positions = 16 * LANES
     return pl.pallas_call(
         functools.partial(attend_kernel, fresh, scale),
-        in_specs=[pl.BlockSpec(memory_space=pltpu.SMEM)] + [vm] * len(args),
+        in_specs=[pl.BlockSpec(memory_space=pltpu.SMEM), vm] + [pl.BlockSpec(memory_space=pltpu.HBM) if fresh else vm] * 8 + [vm] * fresh,
         out_specs=vm,
-        out_shape=jax.ShapeDtypeStruct((rows, latent + LANES), jnp.bfloat16),
-        scratch_shapes=[pltpu.VMEM((width, positions), jnp.bfloat16), pltpu.VMEM((rows, positions), jnp.float32)],
+        out_shape=pltpu.HBM((rows, latent + LANES), jnp.bfloat16),
+        scratch_shapes=[pltpu.VMEM((width, positions), jnp.bfloat16), pltpu.VMEM((rows, positions), jnp.float32)]
+        + [pltpu.SemaphoreType.DMA((32,))] * fresh,
         compiler_params=pltpu.CompilerParams(vmem_limit_bytes=20 * 1024 * 1024),
         cost_estimate=pl.CostEstimate(flops=16 * rows * positions * (width + latent),
                                       bytes_accessed=positions * width * 2 + rows * (width + latent) * 2,
@@ -173,6 +189,34 @@
     return rows, jnp.squeeze(top, axis) + jnp.log(norm)
 
 
+def merge_kernel(parts_ref, o_ref):
+    slots, rows, width = o_ref.shape
+    latent = width - LANES
+    count = parts_ref.shape[0] // slots
+    lane = lax.broadcasted_iota(jnp.int32, (rows, LANES), 1)
+    for s in range(slots):
+        parts = [parts_ref[s * count + i] for i in range(count)]
+        lse = [jnp.sum(jnp.where(lane < 3, p[:, latent:].astype(jnp.float32), 0.0), axis=1, keepdims=True) for p in parts]
+        top = functools.reduce(jnp.maximum, lse)
+        w = [jnp.exp(v - top) for v in lse]
+        norm = functools.reduce(jnp.add, w)
+        total = functools.reduce(jnp.add, [p[:, :latent].astype(jnp.float32) * v for p, v in zip(parts, w)])
+        o_ref[s, :, :latent] = (total / norm).astype(jnp.bfloat16)
+        o_ref[s, :, latent:] = pack_columns(top + jnp.log(norm), lane)
+
+
+def merge_slots(parts, slots):
+    vm = pl.BlockSpec(memory_space=pltpu.VMEM)
+    return pl.pallas_call(
+        merge_kernel,
+        in_specs=[vm],
+        out_specs=vm,
+        out_shape=jax.ShapeDtypeStruct((slots, *parts.shape[1:]), parts.dtype),
+        compiler_params=pltpu.CompilerParams(vmem_limit_bytes=8 * 1024 * 1024),
+        cost_estimate=pl.CostEstimate(flops=4 * parts.size, bytes_accessed=2 * parts.size, transcendentals=1024),
+    )(parts)
+
+
 def after(v, dep):
     return lax.optimization_barrier((v, dep))[0]
 
@@ -191,19 +235,17 @@
     scale = (nope_dim + rope_dim) ** -0.5
     role, ctx, req = lax.axis_index("role"), lax.axis_index("ctx"), lax.axis_index("req")
     x, z = req // NZ, req % NZ
-    total = request_decode_slot.shape[0]
-    ids = jnp.arange(total, dtype=jnp.int32)
-    dx = jnp.arange(NX, dtype=jnp.int32)[:, None]
-    cls = jnp.arange(NC, dtype=jnp.int32)
-    move = jnp.where(cls == 1, 1, jnp.where(cls == 2, -1, jnp.where(cls == 3, jnp.where(z % 2 == 0, 2, -2), 0)))[None, :]
+    ids = jnp.arange(request_decode_slot.shape[0], dtype=jnp.int32)
     blocks = jnp.swapaxes(cache, 1, 2)
 
-    far = jnp.array([4, 0], jnp.int32)[:, None, None]
-    owner = (x + dx) % NX * NZ + (z + move + far + NZ) % NZ
-    take_x = lookup(request_decode_slot, ids, 2 * owner + role)
-    take_z = lookup(request_decode_slot, ids, 2 * owner + 1 - role)
-    index = jnp.concatenate([jnp.moveaxis(take_z, 2, 0).reshape(-1), jnp.moveaxis(take_x, 1, 0).reshape(-1)])
-    picked = pick(blocks, index)
+    def move(c):
+        return jnp.where(c == 1, 1, jnp.where(c == 2, -1, jnp.where(c == 3, 2 - 4 * (z % 2), 0)))
+
+    outer, inner, far = ids // 8, ids % 4, 4 - ids // 4 % 2 * 4
+    z_first = outer < NC
+    dx, cls = jnp.where(z_first, inner, outer - NC), jnp.where(z_first, outer, inner)
+    owner = (x + dx) % NX * NZ + (z + move(cls) + far + NZ) % NZ
+    picked = pick(blocks, lookup(request_decode_slot, ids, 2 * owner + jnp.where(z_first, 1 - role, role)))
     queries = q_nope.reshape(req_dev, steps, heads_dev, nope_dim)
     absorbed = jnp.einsum("bshd,hdk->bshk", queries, w_key, preferred_element_type=jnp.float32).astype(jnp.bfloat16)
     own = jnp.concatenate([absorbed, q_rope.reshape(req_dev, steps, heads_dev, rope_dim)], axis=3)
@@ -221,24 +263,23 @@
     every = jnp.moveaxis(every, 1, 0).reshape(2, -1, latent + rope_dim)
     mine_f, mine_n = second(got_x, move_z)
     recv_f, recv_n = second(got_z, move_x)
-    source = (x - dx + NX) % NX * NZ + (z - move + NZ) % NZ
-    base = ctx * (NX * NZ * LANES) + source * LANES
+    step = jnp.arange(NX * NC, dtype=jnp.int32)
+    source = (x - step // NC + NX) % NX * NZ + (z - move(step % NC) + NZ) % NZ
+    base = (ctx * (NX * NZ) + source) * LANES
 
     def scalars(far):
-        want = 2 * (x * NZ + (z + far) % NZ) + role
-        length = lookup(request_decode_slot, lengths, want)
-        return jnp.concatenate([(length - base).reshape(-1), role[None], ctx[None]]).astype(jnp.int32)
+        length = lookup(request_decode_slot, lengths, 2 * (x * NZ + (z + far) % NZ) + role)
+        return jnp.concatenate([length - base, role[None], ctx[None]]).astype(jnp.int32)
 
     part_f = attend(scalars(4), every[1], mine_f, recv_f, None, latent, scale)
     part_f = lax.all_to_all(part_f.reshape(heads, -1, latent + LANES), ("role", "ctx"), 0, 0, tiled=True)
-    rows_f, lse_f = merge(part_f.reshape(2, -1, *part_f.shape[1:]), latent, 1)
-    packed = jnp.concatenate(
-        [rows_f.astype(jnp.bfloat16), pack_columns(lse_f, lax.broadcasted_iota(jnp.int32, (*lse_f.shape[:2], LANES), 2))], axis=-1)
-    packed = move_far(packed)
+    merged_f = merge_slots(part_f, req_dev)
+    packed = move_far(merged_f)
 
     new = jnp.where(role == 0, new_latent[0], new_latent[1])
-    new = jnp.pad(new.T, ((0, 0), (0, LANES - steps)))
+    new = jnp.pad(new, ((0, LANES - steps), (0, 0)))
     part_n = attend(scalars(0), every[0], mine_n, recv_n, new, latent, scale)
+    part_n = after(part_n, merged_f)
     part_n = lax.all_to_all(part_n.reshape(heads, -1, latent + LANES), ("role", "ctx"), 0, 0, tiled=True)
     parts = jnp.concatenate([part_n.reshape(2, -1, *part_n.shape[1:]), packed[:, None]], axis=1)
     merged, _ = merge(parts, latent, 1)

time: 138 us -> 136 us (0.986)
  local copies, waits for them, and re-layouts: 17.2 us -> 9.97 us
  waiting for transfers between devices: 26.2 us -> 30.4 us
  other arithmetic: 7.25 us -> 3.16 us
  starting transfers between devices: 64.1 us -> 66.8 us
  Pallas kernels: 19.3 us -> 21.3 us
    unnamed x38 -> x18, local copies, waits for them, and re-layouts: 11.3 us -> 4.94 us
    ppermute x10, waiting for transfers between devices: 14.5 us -> 18.8 us  [move_z(): return lax.ppermute(a, ('role', 'req'), pairs)]
    ppermute x2, starting transfers between devices: 12.1 us -> 14.7 us  [move_far(): lax.ppermute(a, 'req', [(x * NZ + z, x * NZ + (z + 4) % NZ) for x in rang...]
    ppermute x9, waiting for transfers between devices: 3.17 us -> 1.32 us  [move_x(): lax.ppermute(a, 'req', [(x * NZ + z, (x + dx) % NX * NZ + z) for x in ran...]
    all_to_all x1, waiting for transfers between devices: 0.85 us -> 2.35 us  [shards(): lax.all_to_all(part_f.reshape(heads, -1, latent + LANES), ('role', 'ctx')...]
    ppermute x10, starting transfers between devices: 17.3 us -> 18.7 us  [move_z(): return lax.ppermute(a, ('role', 'req'), pairs)]
  transfers between devices with their start and end apart: 24 -> 24, of which waited for: 10 -> 7; matrix products, arithmetic and copies ran while one was open for 8% -> 4% of each run, Pallas kernels for 12% -> 14%
where the time goes in v4:
time: 136 us; the launch traced here: 135 us
  starting transfers between devices  66.8 us (49%)
  waiting for transfers between devices  30.4 us (22%)
  Pallas kernels  21.3 us (16%)
  local copies, waits for them, and re-layouts  9.97 us (7%)
  matrix products  3.16 us (2%)
  other arithmetic  3.16 us (2%)
    ppermute x10, waiting for transfers between devices, move_z(): return lax.ppermute(a, ('role', 'req'), pairs)  18.8 us
    ppermute x10, starting transfers between devices, move_z(): return lax.ppermute(a, ('role', 'req'), pairs)  18.7 us
    ppermute x9, starting transfers between devices, move_x(): lax.ppermute(a, 'req', [(x * NZ + z, (x + dx) % NX * NZ + z) for x in ran...  16.2 us
    ppermute x2, starting transfers between devices, move_far(): lax.ppermute(a, 'req', [(x * NZ + z, x * NZ + (z + 4) % NZ) for x in rang...  14.7 us
    pallas_call x2, Pallas kernels, attend(): pl.pallas_call(functools.partial(attend_kernel, fresh, scale), in_specs=[...  13.1 us
    all_to_all x1, starting transfers between devices, shards(): lax.all_to_all(part_f.reshape(heads, -1, latent + LANES), ('role', 'ctx')...  8.65 us
    ppermute x2, waiting for transfers between devices, move_far(): lax.ppermute(a, 'req', [(x * NZ + z, x * NZ + (z + 4) % NZ) for x in rang...  8 us
    unnamed x18, local copies, waits for them, and re-layouts  4.94 us
  transfers between devices with their start and end apart: 24, of which 7 were waited for; matrix products, arithmetic and copies ran while one was open for 4% of the time, Pallas kernels for 14%

profile of v4, /device:TPU:1, one launch (start us, length us, event | category | flops | bytes accessed | tf_op | source)
XLA Modules:
  0.0 135.0 jit_solution(17380408464879053015)
XLA Ops:
  0.0 1.0 reshape.132
  1.0 0.6 copy-done
  1.6 1.1 fusion.7
  2.8 7.8 %collective-permute-start = (bf16[2,4,16,576]{3,1,0,2:T(4,128)(2,1)S(1)}, bf16[2,4,16,576]{3,1,0,2:T(4,128)(2,1)S(1)}, u32[]{:S(2)}, u32[]{:S(2)}) collective-permute-start(bf16[2,4,16,576]{3,1,0,2:T(4,128)(2,1)S(1)} %pad_maximum_fusion.2), channel_id=1, source_target_pairs={{0,4},{1,5},{2,6},{3,7},{4,0},{5,1},{6,2},{7,3},{8,12},{9,13},{10,... | collective-permute-start | bytes 442376 | tf_op jit(solution)/shard_map/ppermute | solution.py:35
  10.9 2.3 %copy-done.1 = bf16[64,128,288]{1,2,0:T(8,128)(2,1)S(1)} copy-done((bf16[64,128,288]{1,2,0:T(8,128)(2,1)S(1)}, bf16[64,128,288]{1,2,0:T(8,128)(2,1)}, u32[]{:S(2)}) %copy-start.1) | copy-done | bytes 4718616
  13.2 3.1 %shard_map.82 = (bf16[2,4,288,128]{3,2,1,0:T(8,128)(2,1)}, bf16[2,4,288,128]{3,2,1,0:T(8,128)(2,1)}, bf16[2,4,288,128]{3,2,1,0:T(8,128)(2,1)}, bf16[2,4,288,128]...) custom-call(s32[64]{0:T(128)S(1)} %select_reduce_fusion.idx_ref, ...), custom_call_target="tpu_custom_call" | custom-call | bytes 9437184 | tf_op jit(solution)/shard_map/pallas_call | solution.py:56
  16.3 3.4 %collective-permute-start.1 = (bf16[2,4,288,128]{3,2,1,0:T(8,128)(2,1)}, bf16[2,4,288,128]{3,2,1,0:T(8,128)(2,1)S(1)}, u32[]{:S(2)}, u32[]{:S(2)}) collective-permute-start(bf16[2,4,288,128]{3,2,1,0:T(8,128)(2,1)} %get-tuple-element.64), channel_id=1, source_target_pairs={{0,129},{1,130},{2,131},{3,132},{4,133},{5,134},{6,135},{7,128},{8... | collective-permute-start | bytes 1769480 | tf_op jit(solution)/shard_map/ppermute | solution.py:25
  19.7 1.2 collective-permute-start.2
  21.2 1.2 broadcast_in_dim.71
  22.4 4.7 %all-to-all-start = ((bf16[8,2,4,16,576]{4,3,2,1,0:T(8,128)(2,1)}), bf16[8,2,4,16,576]{4,3,2,1,0:T(8,128)(2,1)}, u32[]{:S(2)}, u32[]{:S(2)}) async-start(bf16[8,2,4,16,576]{4,3,2,1,0:T(8,128)(2,1)} %bitcast.57), calls=%async_computation | async-start | bytes 2621440 | tf_op jit(solution)/shard_map/all_to_all | solution.py:257
  27.2 2.7 %collective-permute-start.3 = (bf16[2,4,288,128]{3,2,1,0:T(8,128)(2,1)}, bf16[2,4,288,128]{3,2,1,0:T(8,128)(2,1)S(1)}, u32[]{:S(2)}, u32[]{:S(2)}) collective-permute-start(bf16[2,4,288,128]{3,2,1,0:T(8,128)(2,1)} %get-tuple-element.66), channel_id=1, source_target_pairs={{0,135},{1,128},{2,129},{3,130},{4,131},{5,132},{6,133},{7,134},{8... | collective-permute-start | bytes 1769480 | tf_op jit(solution)/shard_map/ppermute | solution.py:25
  29.8 1.5 %collective-permute-start.4 = (bf16[2,4,288,128]{3,2,1,0:T(8,128)(2,1)}, bf16[2,4,288,128]{3,2,1,0:T(8,128)(2,1)}, u32[]{:S(2)}, u32[]{:S(2)}) collective-permute-start(bf16[2,4,288,128]{3,2,1,0:T(8,128)(2,1)} %get-tuple-element.67), channel_id=1, source_target_pairs={{0,24},{1,25},{2,26},{3,27},{4,28},{5,29},{6,30},{7,31},{8,0},{9,1... | collective-permute-start | bytes 1769480 | tf_op jit(solution)/shard_map/ppermute | solution.py:31
  31.3 0.5 collective-permute-start.5
  31.8 4.1 %collective-permute-done.1.refs_1_ = bf16[2,4,288,128]{3,2,1,0:T(8,128)(2,1)S(1)} collective-permute-done((bf16[2,4,288,128]{3,2,1,0:T(8,128)(2,1)}, bf16[2,4,288,128]{3,2,1,0:T(8,128)(2,1)S(1)}, u32[]{:S(2)}, u32[]{:S(2)}) %collective-permute-start.1) | collective-permute-done | bytes 589856 | tf_op jit(solution)/shard_map/ppermute | solution.py:25
  35.8 2.7 %collective-permute-start.6 = (bf16[2,4,288,128]{3,2,1,0:T(8,128)(2,1)}, bf16[2,4,288,128]{3,2,1,0:T(8,128)(2,1)}, u32[]{:S(2)}, u32[]{:S(2)}) collective-permute-start(bf16[2,4,288,128]{3,2,1,0:T(8,128)(2,1)} %get-tuple-element.69), channel_id=1, source_target_pairs={{0,16},{1,17},{2,18},{3,19},{4,20},{5,21},{6,22},{7,23},{8,24},{9,... | collective-permute-start | bytes 1769480 | tf_op jit(solution)/shard_map/ppermute | solution.py:31
  38.6 0.7 fusion.36
  39.3 0.6 broadcast_subtract_fusion
  39.9 0.6 broadcast_subtract_fusion.1
  40.5 14.6 %collective-permute-done.3.refs_2_ = bf16[2,4,288,128]{3,2,1,0:T(8,128)(2,1)S(1)} collective-permute-done((bf16[2,4,288,128]{3,2,1,0:T(8,128)(2,1)}, bf16[2,4,288,128]{3,2,1,0:T(8,128)(2,1)S(1)}, u32[]{:S(2)}, u32[]{:S(2)}) %collective-permute-start.3) | collective-permute-done | bytes 589856 | tf_op jit(solution)/shard_map/ppermute | solution.py:25
  55.2 1.1 copy-done.2
  56.2 2.5 %shard_map.83 = (bf16[4,288,128]{2,1,0:T(8,128)(2,1)S(1)}, bf16[4,288,128]{2,1,0:T(8,128)(2,1)S(1)}, bf16[4,288,128]{2,1,0:T(8,128)(2,1)S(1)}, bf16[4,288,128]{2...) custom-call(bf16[2,4,288,128]{3,2,1,0:T(8,128)(2,1)S(1)} %copy-done., ...), custom_call_target="tpu_custom_call" | custom-call | bytes 4718592 | tf_op jit(solution)/shard_map/pallas_call | solution.py:77
  58.7 3.4 %collective-permute-start.8 = (bf16[4,288,128]{2,1,0:T(8,128)(2,1)S(1)}, bf16[4,288,128]{2,1,0:T(8,128)(2,1)S(1)}, u32[]{:S(2)}, u32[]{:S(2)}) collective-permute-start(bf16[4,288,128]{2,1,0:T(8,128)(2,1)S(1)} %get-tuple-element.82), channel_id=1, source_target_pairs={{0,1},{1,2},{2,3},{3,4},{4,5},{5,6},{6,7},{7,0},{8,9},{9,10},{10,1... | collective-permute-start | bytes 884744 | tf_op jit(solution)/shard_map/ppermute | solution.py:25
  62.1 0.5 collective-permute-start.10
  62.7 2.1 %collective-permute-start.12 = (bf16[4,288,128]{2,1,0:T(8,128)(2,1)S(1)}, bf16[4,288,128]{2,1,0:T(8,128)(2,1)S(1)}, u32[]{:S(2)}, u32[]{:S(2)}) collective-permute-start(bf16[4,288,128]{2,1,0:T(8,128)(2,1)S(1)} %get-tuple-element.88), channel_id=1, source_target_pairs={{0,2},{1,7},{2,4},{3,1},{4,6},{5,3},{6,0},{7,5},{8,10},{9,15},{10,... | collective-permute-start | bytes 884744 | tf_op jit(solution)/shard_map/ppermute | solution.py:25
  64.7 2.3 %shard_map.84 = (bf16[4,288,128]{2,1,0:T(8,128)(2,1)S(1)}, bf16[4,288,128]{2,1,0:T(8,128)(2,1)S(1)}, bf16[4,288,128]{2,1,0:T(8,128)(2,1)S(1)}, bf16[4,288,128]{2...) custom-call(bf16[2,4,288,128]{3,2,1,0:T(8,128)(2,1)} %collective-per, ...), custom_call_target="tpu_custom_call" | custom-call | bytes 4718592 | tf_op jit(solution)/shard_map/pallas_call | solution.py:77
  67.1 1.2 collective-permute-start.14
  68.3 1.6 %collective-permute-start.16 = (bf16[4,288,128]{2,1,0:T(8,128)(2,1)S(1)}, bf16[4,288,128]{2,1,0:T(8,128)(2,1)S(1)}, u32[]{:S(2)}, u32[]{:S(2)}) collective-permute-start(bf16[4,288,128]{2,1,0:T(8,128)(2,1)S(1)} %get-tuple-element.101), channel_id=1, source_target_pairs={{0,16},{1,17},{2,18},{3,19},{4,20},{5,21},{6,22},{7,23},{8,24},{9,... | collective-permute-start | bytes 884744 | tf_op jit(solution)/shard_map/ppermute | solution.py:31
  69.9 2.0 %collective-permute-start.18 = (bf16[4,288,128]{2,1,0:T(8,128)(2,1)S(1)}, bf16[4,288,128]{2,1,0:T(8,128)(2,1)S(1)}, u32[]{:S(2)}, u32[]{:S(2)}) collective-permute-start(bf16[4,288,128]{2,1,0:T(8,128)(2,1)S(1)} %get-tuple-element.104), channel_id=1, source_target_pairs={{0,24},{1,25},{2,26},{3,27},{4,28},{5,29},{6,30},{7,31},{8,0},{9,1... | collective-permute-start | bytes 884744 | tf_op jit(solution)/shard_map/ppermute | solution.py:31
  71.9 0.3 collective-permute-start.9
  72.3 0.7 pad.4.rest_8_
  72.9 1.4 %fusion.45 = (bf16[1,8,4,16,576]{4,3,2,0,1:T(8,128)(2,1)S(1)}, bf16[1,8,4,16,576]{4,3,2,0,1:T(8,128)(2,1)S(1)}) fusion(bf16[2,8,4,16,576]{4,3,2,0,1:T(8,128)(2,1)} %bitcast.9), kind=kLoop, calls=%fused_computation.90 | loop fusion | bytes 2359296 | tf_op jit(solution)/shard_map/slice | solution.py:274
  74.4 4.2 %collective-permute-start.11 = (bf16[4,288,128]{2,1,0:T(8,128)(2,1)}, bf16[4,288,128]{2,1,0:T(8,128)(2,1)}, u32[]{:S(2)}, u32[]{:S(2)}) collective-permute-start(bf16[4,288,128]{2,1,0:T(8,128)(2,1)} %get-tuple-element.86), channel_id=1, source_target_pairs={{0,7},{1,0},{2,1},{3,2},{4,3},{5,4},{6,5},{7,6},{8,15},{9,8},{10,9... | collective-permute-start | bytes 884744 | tf_op jit(solution)/shard_map/ppermute | solution.py:25
  78.6 1.7 %collective-permute-start.13 = (bf16[4,288,128]{2,1,0:T(8,128)(2,1)}, bf16[4,288,128]{2,1,0:T(8,128)(2,1)}, u32[]{:S(2)}, u32[]{:S(2)}) collective-permute-start(bf16[4,288,128]{2,1,0:T(8,128)(2,1)} %get-tuple-element.89), channel_id=1, source_target_pairs={{0,2},{1,7},{2,4},{3,1},{4,6},{5,3},{6,0},{7,5},{8,10},{9,15},{10,... | collective-permute-start | bytes 884744 | tf_op jit(solution)/shard_map/ppermute | solution.py:25
  80.3 0.3 collective-permute-done.16.rest_6_
  80.6 1.0 collective-permute-done.18.rest_7_
  81.6 4.0 %collective-permute-start.17 = (bf16[4,288,128]{2,1,0:T(8,128)(2,1)}, bf16[4,288,128]{2,1,0:T(8,128)(2,1)}, u32[]{:S(2)}, u32[]{:S(2)}) collective-permute-start(bf16[4,288,128]{2,1,0:T(8,128)(2,1)} %get-tuple-element.102), channel_id=1, source_target_pairs={{0,16},{1,17},{2,18},{3,19},{4,20},{5,21},{6,22},{7,23},{8,24},{9,... | collective-permute-start | bytes 884744 | tf_op jit(solution)/shard_map/ppermute | solution.py:31
  85.6 2.0 %collective-permute-start.19 = (bf16[4,288,128]{2,1,0:T(8,128)(2,1)}, bf16[4,288,128]{2,1,0:T(8,128)(2,1)}, u32[]{:S(2)}, u32[]{:S(2)}) collective-permute-start(bf16[4,288,128]{2,1,0:T(8,128)(2,1)} %get-tuple-element.105), channel_id=1, source_target_pairs={{0,24},{1,25},{2,26},{3,27},{4,28},{5,29},{6,30},{7,31},{8,0},{9,1... | collective-permute-start | bytes 884744 | tf_op jit(solution)/shard_map/ppermute | solution.py:31
  87.6 5.6 %shard_map.86 = bf16[512,640]{1,0:T(8,128)(2,1)} custom-call(s32[18]{0:T(128)S(1)} %add_add_fusion.1.scal_ref, bf16[512,576]{1,0:T(8,128)(2,1)S(1)} %bitcast.54, bf16[4,288,128]{2,1,0:T(8,128)(2,1)S(1)} %get-tuple-element.79.rest_0_, bf16[4,288,128]{2,1,0:T(8,128)(2,1)S(1)} %collective-permute-done.8.rest_1_, ...), custom_call_target="tpu_custom_call" | custom-call | flops 18253611008 | bytes 3473408 | tf_op jit(solution)/shard_map/pallas_call | solution.py:169
  93.3 8.6 %all-to-all-start.1 = ((bf16[8,64,640]{2,1,0:T(8,128)(2,1)}), bf16[8,64,640]{2,1,0:T(8,128)(2,1)S(1)}, u32[]{:S(2)}, u32[]{:S(2)}) async-start(bf16[8,64,640]{2,1,0:T(8,128)(2,1)} %bitcast.60), calls=%async_computation.1 | async-start | bytes 1310720 | tf_op jit(solution)/shard_map/all_to_all | solution.py:275
  102.0 0.9 copy-done.3
  102.9 7.5 %shard_map.85 = bf16[512,640]{1,0:T(8,128)(2,1)} custom-call(s32[18]{0:T(128)S(1)} %add_add_fusion.scal_ref, bf16[512,576]{1,0:T(8,128)(2,1)S(1)} %bitcast.53, bf16[4,288,128]{2,1,0:T(8,128)(2,1)} %get-tuple-element.80.rest_0_, bf16[4,288,128]{2,1,0:T(8,128)(2,1)} %copy-done.8, bf16[4,288,128]{2,1,0:T(8,128)(2,1)} %collective-permute-done.11.rest_2_, ...), custom_call_target="tpu_custom_call" | custom-call | flops 18253611008 | bytes 3473408 | tf_op jit(solution)/shard_map/pallas_call | solution.py:169
  110.3 2.4 %all-to-all-done.1.parts_ref = bf16[8,64,640]{2,1,0:T(8,128)(2,1)S(1)} async-done(((bf16[8,64,640]{2,1,0:T(8,128)(2,1)}), bf16[8,64,640]{2,1,0:T(8,128)(2,1)S(1)}, u32[]{:S(2)}, u32[]{:S(2)}) %all-to-all-start.1) | async-done | bytes 655392 | tf_op jit(solution)/shard_map/all_to_all | solution.py:275
  112.7 0.3 shard_map.87
  113.0 3.8 %all-to-all-start.2 = ((bf16[8,64,640]{2,1,0:T(8,128)(2,1)}), bf16[8,64,640]{2,1,0:T(8,128)(2,1)S(1)}, u32[]{:S(2)}, u32[]{:S(2)}) async-start(bf16[8,64,640]{2,1,0:T(8,128)(2,1)} %bitcast.61), calls=%async_computation.2 | async-start | bytes 1310720 | tf_op jit(solution)/shard_map/all_to_all | solution.py:283
  116.8 6.9 %collective-permute-start.20 = (bf16[2,64,640]{2,1,0:T(8,128)(2,1)S(1)}, bf16[2,64,640]{2,1,0:T(8,128)(2,1)S(1)}, u32[]{:S(2)}, u32[]{:S(2)}) collective-permute-start(bf16[2,64,640]{2,1,0:T(8,128)(2,1)S(1)} %shard_map.87), channel_id=1, source_target_pairs={{0,4},{1,5},{2,6},{3,7},{4,0},{5,1},{6,2},{7,3},{8,12},{9,13},{10,... | collective-permute-start | bytes 491528 | tf_op jit(solution)/shard_map/ppermute | solution.py:35
  123.7 8.0 %collective-permute-done.20 = bf16[2,64,640]{2,1,0:T(8,128)(2,1)S(1)} collective-permute-done((bf16[2,64,640]{2,1,0:T(8,128)(2,1)S(1)}, bf16[2,64,640]{2,1,0:T(8,128)(2,1)S(1)}, u32[]{:S(2)}, u32[]{:S(2)}) %collective-permute-start.20) | collective-permute-done | bytes 163872 | tf_op jit(solution)/shard_map/ppermute | solution.py:35
  132.3 2.0 %fusion.13 = bf16[16,2,1,4,128]{4,3,2,1,0:T(4,128)(2,1)S(1)} fusion(bf16[16,512,128]{2,1,0:T(8,128)(2,1)} %param.15, bf16[2,4,16,512]{3,2,1,0:T(8,128)(2,1)S(1)} %divide_convert_fusion), kind=kOutput, calls=%fused_computation.8 | convolution fusion | flops 16793600 | bytes 2260992 | tf_op jit(solution)/shard_map/bshk,hkv->bshv/dot_general | solution.py:287
  134.4 0.6 copy.42
  (48 shorter events, 1.5 us)
Async XLA Ops:
  0.0 1.6 %copy-start = (bf16[16,128,512]{2,1,0:T(8,128)(2,1)S(1)}, bf16[16,128,512]{2,1,0:T(8,128)(2,1)}, u32[]{:S(2)}) copy-start(bf16[16,128,512]{2,1,0:T(8,128)(2,1)} %param.14) | copy-start | bytes 6291460
  0.0 10.7 %copy-start.6 = (s32[64]{0:T(128)S(1)}, s32[64]{0:T(128)}, u32[]{:S(2)}) copy-start(s32[64]{0:T(128)} %param.10) | copy-start | bytes 772
  2.8 13.5 %collective-permute-start = (bf16[2,4,16,576]{3,1,0,2:T(4,128)(2,1)S(1)}, bf16[2,4,16,576]{3,1,0,2:T(4,128)(2,1)S(1)}, u32[]{:S(2)}, u32[]{:S(2)}) collective-permute-start(bf16[2,4,16,576]{3,1,0,2:T(4,128)(2,1)S(1)} %pad_maximum_fusion.2), channel_id=1, source_target_pairs={{0,4},{1,5},{2,6},{3,7},{4,0},{5,1},{6,2},{7,3},{8,12},{9,13},{10,... | collective-permute-start | bytes 442376 | tf_op jit(solution)/shard_map/ppermute | solution.py:35
  10.9 2.3 %copy-start.1 = (bf16[64,128,288]{1,2,0:T(8,128)(2,1)S(1)}, bf16[64,128,288]{1,2,0:T(8,128)(2,1)}, u32[]{:S(2)}) copy-start(bf16[64,128,288]{1,2,0:T(8,128)(2,1)} %param.8) | copy-start | bytes 14155780
  16.3 19.5 %collective-permute-start.1 = (bf16[2,4,288,128]{3,2,1,0:T(8,128)(2,1)}, bf16[2,4,288,128]{3,2,1,0:T(8,128)(2,1)S(1)}, u32[]{:S(2)}, u32[]{:S(2)}) collective-permute-start(bf16[2,4,288,128]{3,2,1,0:T(8,128)(2,1)} %get-tuple-element.64), channel_id=1, source_target_pairs={{0,129},{1,130},{2,131},{3,132},{4,133},{5,134},{6,135},{7,128},{8... | collective-permute-start | bytes 1769480 | tf_op jit(solution)/shard_map/ppermute | solution.py:25
  19.7 18.9 %collective-permute-start.2 = (bf16[2,4,288,128]{3,2,1,0:T(8,128)(2,1)}, bf16[2,4,288,128]{3,2,1,0:T(8,128)(2,1)}, u32[]{:S(2)}, u32[]{:S(2)}) collective-permute-start(bf16[2,4,288,128]{3,2,1,0:T(8,128)(2,1)} %get-tuple-element.65), channel_id=1, source_target_pairs={{0,8},{1,9},{2,10},{3,11},{4,12},{5,13},{6,14},{7,15},{8,16},{9,17... | collective-permute-start | bytes 1769480 | tf_op jit(solution)/shard_map/ppermute | solution.py:31
  21.2 17.4 %copy-start.5 = (s32[64]{0:T(128)S(1)}, s32[64]{0:T(128)}, u32[]{:S(2)}) copy-start(s32[64]{0:T(128)} %param.9) | copy-start | bytes 772
  22.4 40.2 %copy-start.4 = (bf16[2,4,576]{2,1,0:T(4,128)(2,1)S(1)}, bf16[2,4,576]{2,1,0:T(4,128)(2,1)}, u32[]{:S(2)}) copy-start(bf16[2,4,576]{2,1,0:T(4,128)(2,1)} %param.13) | copy-start | bytes 27652
  22.4 32.7 %all-to-all-start = ((bf16[8,2,4,16,576]{4,3,2,1,0:T(8,128)(2,1)}), bf16[8,2,4,16,576]{4,3,2,1,0:T(8,128)(2,1)}, u32[]{:S(2)}, u32[]{:S(2)}) async-start(bf16[8,2,4,16,576]{4,3,2,1,0:T(8,128)(2,1)} %bitcast.57), calls=%async_computation | async-start | bytes 2621440 | tf_op jit(solution)/shard_map/all_to_all | solution.py:257
  27.2 28.0 %collective-permute-start.3 = (bf16[2,4,288,128]{3,2,1,0:T(8,128)(2,1)}, bf16[2,4,288,128]{3,2,1,0:T(8,128)(2,1)S(1)}, u32[]{:S(2)}, u32[]{:S(2)}) collective-permute-start(bf16[2,4,288,128]{3,2,1,0:T(8,128)(2,1)} %get-tuple-element.66), channel_id=1, source_target_pairs={{0,135},{1,128},{2,129},{3,130},{4,131},{5,132},{6,133},{7,134},{8... | collective-permute-start | bytes 1769480 | tf_op jit(solution)/shard_map/ppermute | solution.py:25
  29.8 25.3 %collective-permute-start.4 = (bf16[2,4,288,128]{3,2,1,0:T(8,128)(2,1)}, bf16[2,4,288,128]{3,2,1,0:T(8,128)(2,1)}, u32[]{:S(2)}, u32[]{:S(2)}) collective-permute-start(bf16[2,4,288,128]{3,2,1,0:T(8,128)(2,1)} %get-tuple-element.67), channel_id=1, source_target_pairs={{0,24},{1,25},{2,26},{3,27},{4,28},{5,29},{6,30},{7,31},{8,0},{9,1... | collective-permute-start | bytes 1769480 | tf_op jit(solution)/shard_map/ppermute | solution.py:31
  31.3 23.9 %collective-permute-start.5 = (bf16[2,4,288,128]{3,2,1,0:T(8,128)(2,1)}, bf16[2,4,288,128]{3,2,1,0:T(8,128)(2,1)}, u32[]{:S(2)}, u32[]{:S(2)}) collective-permute-start(bf16[2,4,288,128]{3,2,1,0:T(8,128)(2,1)} %get-tuple-element.68), channel_id=1, source_target_pairs={{0,130},{1,135},{2,132},{3,129},{4,134},{5,131},{6,128},{7,133},{8... | collective-permute-start | bytes 1769480 | tf_op jit(solution)/shard_map/ppermute | solution.py:25
  35.8 19.3 %collective-permute-start.6 = (bf16[2,4,288,128]{3,2,1,0:T(8,128)(2,1)}, bf16[2,4,288,128]{3,2,1,0:T(8,128)(2,1)}, u32[]{:S(2)}, u32[]{:S(2)}) collective-permute-start(bf16[2,4,288,128]{3,2,1,0:T(8,128)(2,1)} %get-tuple-element.69), channel_id=1, source_target_pairs={{0,16},{1,17},{2,18},{3,19},{4,20},{5,21},{6,22},{7,23},{8,24},{9,... | collective-permute-start | bytes 1769480 | tf_op jit(solution)/shard_map/ppermute | solution.py:31
  38.6 16.6 %collective-permute-start.7 = (bf16[2,4,288,128]{3,2,1,0:T(8,128)(2,1)}, bf16[2,4,288,128]{3,2,1,0:T(8,128)(2,1)}, u32[]{:S(2)}, u32[]{:S(2)}) collective-permute-start(bf16[2,4,288,128]{3,2,1,0:T(8,128)(2,1)} %get-tuple-element.70), channel_id=1, source_target_pairs={{0,128},{1,129},{2,130},{3,131},{4,132},{5,133},{6,134},{7,135},{8... | collective-permute-start | bytes 1769480 | tf_op jit(solution)/shard_map/ppermute | solution.py:25
  55.2 1.1 copy-start.2
  58.7 13.2 %copy-start.7 = (bf16[4,288,128]{2,1,0:T(8,128)(2,1)S(1)}, bf16[4,288,128]{2,1,0:T(8,128)(2,1)}, u32[]{:S(2)}) copy-start(bf16[4,288,128]{2,1,0:T(8,128)(2,1)} %get-tuple-element.83) | copy-start | bytes 884740
  58.7 11.2 %collective-permute-start.8 = (bf16[4,288,128]{2,1,0:T(8,128)(2,1)S(1)}, bf16[4,288,128]{2,1,0:T(8,128)(2,1)S(1)}, u32[]{:S(2)}, u32[]{:S(2)}) collective-permute-start(bf16[4,288,128]{2,1,0:T(8,128)(2,1)S(1)} %get-tuple-element.82), channel_id=1, source_target_pairs={{0,1},{1,2},{2,3},{3,4},{4,5},{5,6},{6,7},{7,0},{8,9},{9,10},{10,1... | collective-permute-start | bytes 884744 | tf_op jit(solution)/shard_map/ppermute | solution.py:25
  62.1 9.8 %collective-permute-start.10 = (bf16[4,288,128]{2,1,0:T(8,128)(2,1)S(1)}, bf16[4,288,128]{2,1,0:T(8,128)(2,1)S(1)}, u32[]{:S(2)}, u32[]{:S(2)}) collective-permute-start(bf16[4,288,128]{2,1,0:T(8,128)(2,1)S(1)} %get-tuple-element.85), channel_id=1, source_target_pairs={{0,7},{1,0},{2,1},{3,2},{4,3},{5,4},{6,5},{7,6},{8,15},{9,8},{10,9... | collective-permute-start | bytes 884744 | tf_op jit(solution)/shard_map/ppermute | solution.py:25
  62.7 11.8 %collective-permute-start.12 = (bf16[4,288,128]{2,1,0:T(8,128)(2,1)S(1)}, bf16[4,288,128]{2,1,0:T(8,128)(2,1)S(1)}, u32[]{:S(2)}, u32[]{:S(2)}) collective-permute-start(bf16[4,288,128]{2,1,0:T(8,128)(2,1)S(1)} %get-tuple-element.88), channel_id=1, source_target_pairs={{0,2},{1,7},{2,4},{3,1},{4,6},{5,3},{6,0},{7,5},{8,10},{9,15},{10,... | collective-permute-start | bytes 884744 | tf_op jit(solution)/shard_map/ppermute | solution.py:25
  67.1 11.5 %collective-permute-start.14 = (bf16[4,288,128]{2,1,0:T(8,128)(2,1)S(1)}, bf16[4,288,128]{2,1,0:T(8,128)(2,1)S(1)}, u32[]{:S(2)}, u32[]{:S(2)}) collective-permute-start(bf16[4,288,128]{2,1,0:T(8,128)(2,1)S(1)} %get-tuple-element.98), channel_id=1, source_target_pairs={{0,8},{1,9},{2,10},{3,11},{4,12},{5,13},{6,14},{7,15},{8,16},{9,17... | collective-permute-start | bytes 884744 | tf_op jit(solution)/shard_map/ppermute | solution.py:31
  68.3 12.4 %collective-permute-start.16 = (bf16[4,288,128]{2,1,0:T(8,128)(2,1)S(1)}, bf16[4,288,128]{2,1,0:T(8,128)(2,1)S(1)}, u32[]{:S(2)}, u32[]{:S(2)}) collective-permute-start(bf16[4,288,128]{2,1,0:T(8,128)(2,1)S(1)} %get-tuple-element.101), channel_id=1, source_target_pairs={{0,16},{1,17},{2,18},{3,19},{4,20},{5,21},{6,22},{7,23},{8,24},{9,... | collective-permute-start | bytes 884744 | tf_op jit(solution)/shard_map/ppermute | solution.py:31
  69.9 11.7 %collective-permute-start.18 = (bf16[4,288,128]{2,1,0:T(8,128)(2,1)S(1)}, bf16[4,288,128]{2,1,0:T(8,128)(2,1)S(1)}, u32[]{:S(2)}, u32[]{:S(2)}) collective-permute-start(bf16[4,288,128]{2,1,0:T(8,128)(2,1)S(1)} %get-tuple-element.104), channel_id=1, source_target_pairs={{0,24},{1,25},{2,26},{3,27},{4,28},{5,29},{6,30},{7,31},{8,0},{9,1... | collective-permute-start | bytes 884744 | tf_op jit(solution)/shard_map/ppermute | solution.py:31
  71.9 13.8 %collective-permute-start.9 = (bf16[4,288,128]{2,1,0:T(8,128)(2,1)S(1)}, bf16[4,288,128]{2,1,0:T(8,128)(2,1)S(1)}, u32[]{:S(2)}, u32[]{:S(2)}) collective-permute-start(bf16[4,288,128]{2,1,0:T(8,128)(2,1)S(1)} %copy-done.7), channel_id=1, source_target_pairs={{0,1},{1,2},{2,3},{3,4},{4,5},{5,6},{6,7},{7,0},{8,9},{9,10},{10,1... | collective-permute-start | bytes 884744 | tf_op jit(solution)/shard_map/ppermute | solution.py:25
  74.4 27.5 %collective-permute-start.11 = (bf16[4,288,128]{2,1,0:T(8,128)(2,1)}, bf16[4,288,128]{2,1,0:T(8,128)(2,1)}, u32[]{:S(2)}, u32[]{:S(2)}) collective-permute-start(bf16[4,288,128]{2,1,0:T(8,128)(2,1)} %get-tuple-element.86), channel_id=1, source_target_pairs={{0,7},{1,0},{2,1},{3,2},{4,3},{5,4},{6,5},{7,6},{8,15},{9,8},{10,9... | collective-permute-start | bytes 884744 | tf_op jit(solution)/shard_map/ppermute | solution.py:25
  78.6 23.3 %collective-permute-start.13 = (bf16[4,288,128]{2,1,0:T(8,128)(2,1)}, bf16[4,288,128]{2,1,0:T(8,128)(2,1)}, u32[]{:S(2)}, u32[]{:S(2)}) collective-permute-start(bf16[4,288,128]{2,1,0:T(8,128)(2,1)} %get-tuple-element.89), channel_id=1, source_target_pairs={{0,2},{1,7},{2,4},{3,1},{4,6},{5,3},{6,0},{7,5},{8,10},{9,15},{10,... | collective-permute-start | bytes 884744 | tf_op jit(solution)/shard_map/ppermute | solution.py:25
  80.6 21.3 %collective-permute-start.15 = (bf16[4,288,128]{2,1,0:T(8,128)(2,1)}, bf16[4,288,128]{2,1,0:T(8,128)(2,1)}, u32[]{:S(2)}, u32[]{:S(2)}) collective-permute-start(bf16[4,288,128]{2,1,0:T(8,128)(2,1)} %get-tuple-element.99), channel_id=1, source_target_pairs={{0,8},{1,9},{2,10},{3,11},{4,12},{5,13},{6,14},{7,15},{8,16},{9,17... | collective-permute-start | bytes 884744 | tf_op jit(solution)/shard_map/ppermute | solution.py:31
  81.6 20.3 %collective-permute-start.17 = (bf16[4,288,128]{2,1,0:T(8,128)(2,1)}, bf16[4,288,128]{2,1,0:T(8,128)(2,1)}, u32[]{:S(2)}, u32[]{:S(2)}) collective-permute-start(bf16[4,288,128]{2,1,0:T(8,128)(2,1)} %get-tuple-element.102), channel_id=1, source_target_pairs={{0,16},{1,17},{2,18},{3,19},{4,20},{5,21},{6,22},{7,23},{8,24},{9,... | collective-permute-start | bytes 884744 | tf_op jit(solution)/shard_map/ppermute | solution.py:31
  85.6 7.6 %copy-start.8 = (bf16[4,288,128]{2,1,0:T(8,128)(2,1)}, bf16[4,288,128]{2,1,0:T(8,128)(2,1)S(1)}, u32[]{:S(2)}) copy-start(bf16[4,288,128]{2,1,0:T(8,128)(2,1)S(1)} %collective-permute-done.9.rest_1_) | copy-start | bytes 884740
  85.6 16.3 %collective-permute-start.19 = (bf16[4,288,128]{2,1,0:T(8,128)(2,1)}, bf16[4,288,128]{2,1,0:T(8,128)(2,1)}, u32[]{:S(2)}, u32[]{:S(2)}) collective-permute-start(bf16[4,288,128]{2,1,0:T(8,128)(2,1)} %get-tuple-element.105), channel_id=1, source_target_pairs={{0,24},{1,25},{2,26},{3,27},{4,28},{5,29},{6,30},{7,31},{8,0},{9,1... | collective-permute-start | bytes 884744 | tf_op jit(solution)/shard_map/ppermute | solution.py:31
  93.3 19.4 %all-to-all-start.1 = ((bf16[8,64,640]{2,1,0:T(8,128)(2,1)}), bf16[8,64,640]{2,1,0:T(8,128)(2,1)S(1)}, u32[]{:S(2)}, u32[]{:S(2)}) async-start(bf16[8,64,640]{2,1,0:T(8,128)(2,1)} %bitcast.60), calls=%async_computation.1 | async-start | bytes 1310720 | tf_op jit(solution)/shard_map/all_to_all | solution.py:275
  102.0 0.9 copy-start.3
  113.0 18.7 %all-to-all-start.2 = ((bf16[8,64,640]{2,1,0:T(8,128)(2,1)}), bf16[8,64,640]{2,1,0:T(8,128)(2,1)S(1)}, u32[]{:S(2)}, u32[]{:S(2)}) async-start(bf16[8,64,640]{2,1,0:T(8,128)(2,1)} %bitcast.61), calls=%async_computation.2 | async-start | bytes 1310720 | tf_op jit(solution)/shard_map/all_to_all | solution.py:283
  116.8 14.9 %collective-permute-start.20 = (bf16[2,64,640]{2,1,0:T(8,128)(2,1)S(1)}, bf16[2,64,640]{2,1,0:T(8,128)(2,1)S(1)}, u32[]{:S(2)}, u32[]{:S(2)}) collective-permute-start(bf16[2,64,640]{2,1,0:T(8,128)(2,1)S(1)} %shard_map.87), channel_id=1, source_target_pairs={{0,4},{1,5},{2,6},{3,7},{4,0},{5,1},{6,2},{7,3},{8,12},{9,13},{10,... | collective-permute-start | bytes 491528 | tf_op jit(solution)/shard_map/ppermute | solution.py:35

commit v5 on v4

--- a/solution.py
+++ b/solution.py
@@ -81,7 +81,7 @@
         out_shape=[pltpu.VMEM(shape, parts[0].dtype)] * 4 + [pltpu.HBM(shape, parts[0].dtype)] * 4,
         compiler_params=pltpu.CompilerParams(vmem_limit_bytes=8 * 1024 * 1024),
         cost_estimate=pl.CostEstimate(flops=0, bytes_accessed=2 * 8 * size * 2, transcendentals=0),
-    )(*parts)
+    )(*[pltpu.with_memory_space_constraint(p, pltpu.HBM) for p in parts])
 
 
 def attend_kernel(fresh, scale, scal_ref, q_ref, *rest):
@@ -102,7 +102,10 @@
     high = jnp.full((rows, LANES), NEG, jnp.float32)
     copies = []
     if fresh:
-        sems = rest[3]
+        sems, q_vm = rest[3:]
+        copies_q = pltpu.make_async_copy(q_ref, q_vm, sems.at[32])
+        copies_q.start()
+        q_ref = q_vm
         for j in range(4):
             for c in range(4):
                 cols, n = pl.ds(j * chunk + c * LANES, LANES), 8 * j + 2 * c
@@ -110,6 +113,7 @@
                 copies.append(pltpu.make_async_copy(recv[j].at[c], kt.at[at_recv, cols], sems.at[n + 1]))
         for copy in copies:
             copy.start()
+        copies_q.wait()
     for j in range(4):
         for copy in copies[8 * j:8 * j + 8]:
             copy.wait()
@@ -163,16 +167,17 @@
     fresh = new is not None
     vm = pl.BlockSpec(memory_space=pltpu.VMEM)
     if fresh:
+        q = pltpu.with_memory_space_constraint(q, pltpu.HBM)
         mine, recv = [[pltpu.with_memory_space_constraint(a, pltpu.HBM) for a in side] for side in (mine, recv)]
     args = [q, *mine, *recv] + ([new] if fresh else [])
     positions = 16 * LANES
     return pl.pallas_call(
         functools.partial(attend_kernel, fresh, scale),
-        in_specs=[pl.BlockSpec(memory_space=pltpu.SMEM), vm] + [pl.BlockSpec(memory_space=pltpu.HBM) if fresh else vm] * 8 + [vm] * fresh,
+        in_specs=[pl.BlockSpec(memory_space=pltpu.SMEM)] + [pl.BlockSpec(memory_space=pltpu.HBM) if fresh else vm] * 9 + [vm] * fresh,
         out_specs=vm,
         out_shape=pltpu.HBM((rows, latent + LANES), jnp.bfloat16),
         scratch_shapes=[pltpu.VMEM((width, positions), jnp.bfloat16), pltpu.VMEM((rows, positions), jnp.float32)]
-        + [pltpu.SemaphoreType.DMA((32,))] * fresh,
+        + [pltpu.SemaphoreType.DMA((33,)), pltpu.VMEM((rows, width), jnp.bfloat16)] * fresh,
         compiler_params=pltpu.CompilerParams(vmem_limit_bytes=20 * 1024 * 1024),
         cost_estimate=pl.CostEstimate(flops=16 * rows * positions * (width + latent),
                                       bytes_accessed=positions * width * 2 + rows * (width + latent) * 2,

time: 136 us -> 135 us (level)
    unnamed x18 -> x22, local copies, waits for them, and re-layouts: 4.94 us -> 3.68 us
  transfers between devices with their start and end apart: 24 -> 24, of which waited for: 7 -> 6; matrix products, arithmetic and copies ran while one was open for 4% -> 5% of each run, Pallas kernels for 14% -> 14%
where the time goes in v5:
time: 135 us; the launch traced here: 134 us
  starting transfers between devices  65.6 us (49%)
  waiting for transfers between devices  30.8 us (23%)
  Pallas kernels  22.1 us (16%)
  local copies, waits for them, and re-layouts  8.94 us (7%)
  matrix products  3.17 us (2%)
  other arithmetic  3.13 us (2%)
    ppermute x10, waiting for transfers between devices, move_z(): return lax.ppermute(a, ('role', 'req'), pairs)  18.7 us
    ppermute x10, starting transfers between devices, move_z(): return lax.ppermute(a, ('role', 'req'), pairs)  18.3 us
    ppermute x9, starting transfers between devices, move_x(): lax.ppermute(a, 'req', [(x * NZ + z, (x + dx) % NX * NZ + z) for x in ran...  15.8 us
    ppermute x2, starting transfers between devices, move_far(): lax.ppermute(a, 'req', [(x * NZ + z, x * NZ + (z + 4) % NZ) for x in rang...  14.5 us
    pallas_call x2, Pallas kernels, attend(): pl.pallas_call(functools.partial(attend_kernel, fresh, scale), in_specs=[...  13.2 us
    all_to_all x1, starting transfers between devices, shards(): lax.all_to_all(part_f.reshape(heads, -1, latent + LANES), ('role', 'ctx')...  8.48 us
    ppermute x2, waiting for transfers between devices, move_far(): lax.ppermute(a, 'req', [(x * NZ + z, x * NZ + (z + 4) % NZ) for x in rang...  8.01 us
    pallas_call x2, Pallas kernels, regroup(): pl.pallas_call(regroup_kernel, in_specs=[vm] * 4, out_specs=[vm] * 8, out...  5.48 us
  transfers between devices with their start and end apart: 24, of which 6 were waited for; matrix products, arithmetic and copies ran while one was open for 5% of the time, Pallas kernels for 14%

profile of v5, /device:TPU:1, one launch (start us, length us, event | category | flops | bytes accessed | tf_op | source)
XLA Modules:
  0.0 133.9 jit_solution(8521948673457896256)
XLA Ops:
  0.0 1.0 reshape.132
  1.0 0.6 copy-done
  1.6 1.1 fusion.7
  2.8 7.8 %collective-permute-start = (bf16[2,4,16,576]{3,1,0,2:T(4,128)(2,1)S(1)}, bf16[2,4,16,576]{3,1,0,2:T(4,128)(2,1)S(1)}, u32[]{:S(2)}, u32[]{:S(2)}) collective-permute-start(bf16[2,4,16,576]{3,1,0,2:T(4,128)(2,1)S(1)} %pad_maximum_fusion.2), channel_id=1, source_target_pairs={{0,4},{1,5},{2,6},{3,7},{4,0},{5,1},{6,2},{7,3},{8,12},{9,13},{10,... | collective-permute-start | bytes 442376 | tf_op jit(solution)/shard_map/ppermute | solution.py:35
  10.9 2.3 %copy-done.1 = bf16[64,128,288]{1,2,0:T(8,128)(2,1)S(1)} copy-done((bf16[64,128,288]{1,2,0:T(8,128)(2,1)S(1)}, bf16[64,128,288]{1,2,0:T(8,128)(2,1)}, u32[]{:S(2)}) %copy-start.1) | copy-done | bytes 4718616
  13.2 3.1 %shard_map.82 = (bf16[2,4,288,128]{3,2,1,0:T(8,128)(2,1)}, bf16[2,4,288,128]{3,2,1,0:T(8,128)(2,1)}, bf16[2,4,288,128]{3,2,1,0:T(8,128)(2,1)}, bf16[2,4,288,128]...) custom-call(s32[64]{0:T(128)S(1)} %select_reduce_fusion.idx_ref, ...), custom_call_target="tpu_custom_call" | custom-call | bytes 9437184 | tf_op jit(solution)/shard_map/pallas_call | solution.py:56
  16.4 3.4 %collective-permute-start.1 = (bf16[2,4,288,128]{3,2,1,0:T(8,128)(2,1)}, bf16[2,4,288,128]{3,2,1,0:T(8,128)(2,1)S(1)}, u32[]{:S(2)}, u32[]{:S(2)}) collective-permute-start(bf16[2,4,288,128]{3,2,1,0:T(8,128)(2,1)} %get-tuple-element.64), channel_id=1, source_target_pairs={{0,129},{1,130},{2,131},{3,132},{4,133},{5,134},{6,135},{7,128},{8... | collective-permute-start | bytes 1769480 | tf_op jit(solution)/shard_map/ppermute | solution.py:25
  19.7 1.2 collective-permute-start.2
  20.9 0.2 pad_maximum_fusion
  21.2 1.2 broadcast_in_dim.71
  22.5 4.7 %all-to-all-start = ((bf16[8,2,4,16,576]{4,3,2,1,0:T(8,128)(2,1)}), bf16[8,2,4,16,576]{4,3,2,1,0:T(8,128)(2,1)}, u32[]{:S(2)}, u32[]{:S(2)}) async-start(bf16[8,2,4,16,576]{4,3,2,1,0:T(8,128)(2,1)} %bitcast.8), calls=%async_computation | async-start | bytes 2621440 | tf_op jit(solution)/shard_map/all_to_all | solution.py:262
  27.2 2.7 %collective-permute-start.3 = (bf16[2,4,288,128]{3,2,1,0:T(8,128)(2,1)}, bf16[2,4,288,128]{3,2,1,0:T(8,128)(2,1)S(1)}, u32[]{:S(2)}, u32[]{:S(2)}) collective-permute-start(bf16[2,4,288,128]{3,2,1,0:T(8,128)(2,1)} %get-tuple-element.66), channel_id=1, source_target_pairs={{0,135},{1,128},{2,129},{3,130},{4,131},{5,132},{6,133},{7,134},{8... | collective-permute-start | bytes 1769480 | tf_op jit(solution)/shard_map/ppermute | solution.py:25
  29.8 1.5 %collective-permute-start.4 = (bf16[2,4,288,128]{3,2,1,0:T(8,128)(2,1)}, bf16[2,4,288,128]{3,2,1,0:T(8,128)(2,1)}, u32[]{:S(2)}, u32[]{:S(2)}) collective-permute-start(bf16[2,4,288,128]{3,2,1,0:T(8,128)(2,1)} %get-tuple-element.67), channel_id=1, source_target_pairs={{0,24},{1,25},{2,26},{3,27},{4,28},{5,29},{6,30},{7,31},{8,0},{9,1... | collective-permute-start | bytes 1769480 | tf_op jit(solution)/shard_map/ppermute | solution.py:31
  31.3 0.5 collective-permute-start.5
  31.8 4.1 %collective-permute-done.1.refs_1_ = bf16[2,4,288,128]{3,2,1,0:T(8,128)(2,1)S(1)} collective-permute-done((bf16[2,4,288,128]{3,2,1,0:T(8,128)(2,1)}, bf16[2,4,288,128]{3,2,1,0:T(8,128)(2,1)S(1)}, u32[]{:S(2)}, u32[]{:S(2)}) %collective-permute-start.1) | collective-permute-done | bytes 589856 | tf_op jit(solution)/shard_map/ppermute | solution.py:25
  35.8 2.7 %collective-permute-start.6 = (bf16[2,4,288,128]{3,2,1,0:T(8,128)(2,1)}, bf16[2,4,288,128]{3,2,1,0:T(8,128)(2,1)}, u32[]{:S(2)}, u32[]{:S(2)}) collective-permute-start(bf16[2,4,288,128]{3,2,1,0:T(8,128)(2,1)} %get-tuple-element.69), channel_id=1, source_target_pairs={{0,16},{1,17},{2,18},{3,19},{4,20},{5,21},{6,22},{7,23},{8,24},{9,... | collective-permute-start | bytes 1769480 | tf_op jit(solution)/shard_map/ppermute | solution.py:31
  38.6 0.7 fusion.36
  39.2 0.7 broadcast_subtract_fusion
  39.9 0.6 broadcast_subtract_fusion.1
  40.5 14.6 %collective-permute-done.3.refs_2_ = bf16[2,4,288,128]{3,2,1,0:T(8,128)(2,1)S(1)} collective-permute-done((bf16[2,4,288,128]{3,2,1,0:T(8,128)(2,1)}, bf16[2,4,288,128]{3,2,1,0:T(8,128)(2,1)S(1)}, u32[]{:S(2)}, u32[]{:S(2)}) %collective-permute-start.3) | collective-permute-done | bytes 589856 | tf_op jit(solution)/shard_map/ppermute | solution.py:25
  55.2 2.8 %shard_map.83 = (bf16[4,288,128]{2,1,0:T(8,128)(2,1)S(1)}, bf16[4,288,128]{2,1,0:T(8,128)(2,1)S(1)}, bf16[4,288,128]{2,1,0:T(8,128)(2,1)S(1)}, bf16[4,288,128]{2...) custom-call(bf16[2,4,288,128]{3,2,1,0:T(8,128)(2,1)} %get-tuple-elem, ...), custom_call_target="tpu_custom_call" | custom-call | bytes 4718592 | tf_op jit(solution)/shard_map/pallas_call | solution.py:77
  58.0 3.2 %collective-permute-start.8 = (bf16[4,288,128]{2,1,0:T(8,128)(2,1)S(1)}, bf16[4,288,128]{2,1,0:T(8,128)(2,1)S(1)}, u32[]{:S(2)}, u32[]{:S(2)}) collective-permute-start(bf16[4,288,128]{2,1,0:T(8,128)(2,1)S(1)} %get-tuple-element.82), channel_id=1, source_target_pairs={{0,1},{1,2},{2,3},{3,4},{4,5},{5,6},{6,7},{7,0},{8,9},{9,10},{10,1... | collective-permute-start | bytes 884744 | tf_op jit(solution)/shard_map/ppermute | solution.py:25
  61.2 0.7 collective-permute-start.10
  62.0 1.9 %collective-permute-start.12 = (bf16[4,288,128]{2,1,0:T(8,128)(2,1)S(1)}, bf16[4,288,128]{2,1,0:T(8,128)(2,1)S(1)}, u32[]{:S(2)}, u32[]{:S(2)}) collective-permute-start(bf16[4,288,128]{2,1,0:T(8,128)(2,1)S(1)} %get-tuple-element.88), channel_id=1, source_target_pairs={{0,2},{1,7},{2,4},{3,1},{4,6},{5,3},{6,0},{7,5},{8,10},{9,15},{10,... | collective-permute-start | bytes 884744 | tf_op jit(solution)/shard_map/ppermute | solution.py:25
  63.9 2.6 %shard_map.84 = (bf16[4,288,128]{2,1,0:T(8,128)(2,1)S(1)}, bf16[4,288,128]{2,1,0:T(8,128)(2,1)S(1)}, bf16[4,288,128]{2,1,0:T(8,128)(2,1)S(1)}, bf16[4,288,128]{2...) custom-call(bf16[2,4,288,128]{3,2,1,0:T(8,128)(2,1)} %collective-per, ...), custom_call_target="tpu_custom_call" | custom-call | bytes 4718592 | tf_op jit(solution)/shard_map/pallas_call | solution.py:77
  66.5 1.2 collective-permute-start.14
  67.7 1.6 %collective-permute-start.16 = (bf16[4,288,128]{2,1,0:T(8,128)(2,1)S(1)}, bf16[4,288,128]{2,1,0:T(8,128)(2,1)S(1)}, u32[]{:S(2)}, u32[]{:S(2)}) collective-permute-start(bf16[4,288,128]{2,1,0:T(8,128)(2,1)S(1)} %get-tuple-element.101), channel_id=1, source_target_pairs={{0,16},{1,17},{2,18},{3,19},{4,20},{5,21},{6,22},{7,23},{8,24},{9,... | collective-permute-start | bytes 884744 | tf_op jit(solution)/shard_map/ppermute | solution.py:31
  69.4 1.7 %collective-permute-start.18 = (bf16[4,288,128]{2,1,0:T(8,128)(2,1)S(1)}, bf16[4,288,128]{2,1,0:T(8,128)(2,1)S(1)}, u32[]{:S(2)}, u32[]{:S(2)}) collective-permute-start(bf16[4,288,128]{2,1,0:T(8,128)(2,1)S(1)} %get-tuple-element.104), channel_id=1, source_target_pairs={{0,24},{1,25},{2,26},{3,27},{4,28},{5,29},{6,30},{7,31},{8,0},{9,1... | collective-permute-start | bytes 884744 | tf_op jit(solution)/shard_map/ppermute | solution.py:31
  71.0 0.8 collective-permute-start.9
  71.9 2.3 %fusion.45 = (bf16[1,8,4,16,576]{4,3,2,0,1:T(8,128)(2,1)S(1)}, bf16[1,8,4,16,576]{4,3,2,0,1:T(8,128)(2,1)}) fusion(bf16[2,8,4,16,576]{4,3,2,0,1:T(8,128)(2,1)} %bitcast.9), kind=kLoop, calls=%fused_computation.90 | loop fusion | bytes 2359296 | tf_op jit(solution)/shard_map/slice | solution.py:279
  74.2 3.5 %collective-permute-start.11 = (bf16[4,288,128]{2,1,0:T(8,128)(2,1)}, bf16[4,288,128]{2,1,0:T(8,128)(2,1)S(1)}, u32[]{:S(2)}, u32[]{:S(2)}) collective-permute-start(bf16[4,288,128]{2,1,0:T(8,128)(2,1)} %get-tuple-element.86), channel_id=1, source_target_pairs={{0,7},{1,0},{2,1},{3,2},{4,3},{5,4},{6,5},{7,6},{8,15},{9,8},{10,9... | collective-permute-start | bytes 884744 | tf_op jit(solution)/shard_map/ppermute | solution.py:25
  77.7 1.7 %collective-permute-start.13 = (bf16[4,288,128]{2,1,0:T(8,128)(2,1)}, bf16[4,288,128]{2,1,0:T(8,128)(2,1)}, u32[]{:S(2)}, u32[]{:S(2)}) collective-permute-start(bf16[4,288,128]{2,1,0:T(8,128)(2,1)} %get-tuple-element.89), channel_id=1, source_target_pairs={{0,2},{1,7},{2,4},{3,1},{4,6},{5,3},{6,0},{7,5},{8,10},{9,15},{10,... | collective-permute-start | bytes 884744 | tf_op jit(solution)/shard_map/ppermute | solution.py:25
  79.5 0.6 collective-permute-done.16.rest_6_
  80.1 1.0 collective-permute-done.18.rest_7_
  81.1 3.8 %collective-permute-start.17 = (bf16[4,288,128]{2,1,0:T(8,128)(2,1)}, bf16[4,288,128]{2,1,0:T(8,128)(2,1)}, u32[]{:S(2)}, u32[]{:S(2)}) collective-permute-start(bf16[4,288,128]{2,1,0:T(8,128)(2,1)} %get-tuple-element.102), channel_id=1, source_target_pairs={{0,16},{1,17},{2,18},{3,19},{4,20},{5,21},{6,22},{7,23},{8,24},{9,... | collective-permute-start | bytes 884744 | tf_op jit(solution)/shard_map/ppermute | solution.py:31
  84.9 2.1 %collective-permute-start.19 = (bf16[4,288,128]{2,1,0:T(8,128)(2,1)S(1)}, bf16[4,288,128]{2,1,0:T(8,128)(2,1)}, u32[]{:S(2)}, u32[]{:S(2)}) collective-permute-start(bf16[4,288,128]{2,1,0:T(8,128)(2,1)S(1)} %copy-done.7), channel_id=1, source_target_pairs={{0,24},{1,25},{2,26},{3,27},{4,28},{5,29},{6,30},{7,31},{8,0},{9,1... | collective-permute-start | bytes 884744 | tf_op jit(solution)/shard_map/ppermute | solution.py:31
  87.0 5.6 %shard_map.86 = bf16[512,640]{1,0:T(8,128)(2,1)} custom-call(s32[18]{0:T(128)S(1)} %add_add_fusion.1.scal_ref, bf16[512,576]{1,0:T(8,128)(2,1)S(1)} %bitcast.53, bf16[4,288,128]{2,1,0:T(8,128)(2,1)S(1)} %get-tuple-element.79.rest_0_, bf16[4,288,128]{2,1,0:T(8,128)(2,1)S(1)} %collective-permute-done.8.rest_1_, ...), custom_call_target="tpu_custom_call" | custom-call | flops 18253611008 | bytes 3473408 | tf_op jit(solution)/shard_map/pallas_call | solution.py:174
  92.6 8.5 %all-to-all-start.1 = ((bf16[8,64,640]{2,1,0:T(8,128)(2,1)}), bf16[8,64,640]{2,1,0:T(8,128)(2,1)S(1)}, u32[]{:S(2)}, u32[]{:S(2)}) async-start(bf16[8,64,640]{2,1,0:T(8,128)(2,1)} %bitcast.59), calls=%async_computation.1 | async-start | bytes 1310720 | tf_op jit(solution)/shard_map/all_to_all | solution.py:280
  101.1 0.7 copy-done.10
  101.8 7.6 %shard_map.85 = bf16[512,640]{1,0:T(8,128)(2,1)} custom-call(s32[18]{0:T(128)S(1)} %add_add_fusion.scal_ref, bf16[512,576]{1,0:T(8,128)(2,1)} %bitcast.57, bf16[4,288,128]{2,1,0:T(8,128)(2,1)} %get-tuple-element.80.rest_0_, bf16[4,288,128]{2,1,0:T(8,128)(2,1)} %copy-done.9, bf16[4,288,128]{2,1,0:T(8,128)(2,1)} %copy-done.10, ...), custom_call_target="tpu_custom_call" | custom-call | flops 18253611008 | bytes 3473408 | tf_op jit(solution)/shard_map/pallas_call | solution.py:174
  109.4 2.5 %all-to-all-done.1.parts_ref = bf16[8,64,640]{2,1,0:T(8,128)(2,1)S(1)} async-done(((bf16[8,64,640]{2,1,0:T(8,128)(2,1)}), bf16[8,64,640]{2,1,0:T(8,128)(2,1)S(1)}, u32[]{:S(2)}, u32[]{:S(2)}) %all-to-all-start.1) | async-done | bytes 655392 | tf_op jit(solution)/shard_map/all_to_all | solution.py:280
  111.8 0.3 shard_map.87
  112.1 3.8 %all-to-all-start.2 = ((bf16[8,64,640]{2,1,0:T(8,128)(2,1)}), bf16[8,64,640]{2,1,0:T(8,128)(2,1)S(1)}, u32[]{:S(2)}, u32[]{:S(2)}) async-start(bf16[8,64,640]{2,1,0:T(8,128)(2,1)} %bitcast.60), calls=%async_computation.2 | async-start | bytes 1310720 | tf_op jit(solution)/shard_map/all_to_all | solution.py:288
  116.0 6.7 %collective-permute-start.20 = (bf16[2,64,640]{2,1,0:T(8,128)(2,1)S(1)}, bf16[2,64,640]{2,1,0:T(8,128)(2,1)S(1)}, u32[]{:S(2)}, u32[]{:S(2)}) collective-permute-start(bf16[2,64,640]{2,1,0:T(8,128)(2,1)S(1)} %shard_map.87), channel_id=1, source_target_pairs={{0,4},{1,5},{2,6},{3,7},{4,0},{5,1},{6,2},{7,3},{8,12},{9,13},{10,... | collective-permute-start | bytes 491528 | tf_op jit(solution)/shard_map/ppermute | solution.py:35
  122.6 8.0 %collective-permute-done.20 = bf16[2,64,640]{2,1,0:T(8,128)(2,1)S(1)} collective-permute-done((bf16[2,64,640]{2,1,0:T(8,128)(2,1)S(1)}, bf16[2,64,640]{2,1,0:T(8,128)(2,1)S(1)}, u32[]{:S(2)}, u32[]{:S(2)}) %collective-permute-start.20) | collective-permute-done | bytes 163872 | tf_op jit(solution)/shard_map/ppermute | solution.py:35
  130.9 0.2 multiply_reduce_fusion
  131.3 2.0 %fusion.13 = bf16[16,2,1,4,128]{4,3,2,1,0:T(4,128)(2,1)S(1)} fusion(bf16[16,512,128]{2,1,0:T(8,128)(2,1)} %param.15, bf16[2,4,16,512]{3,2,1,0:T(8,128)(2,1)S(1)} %divide_convert_fusion), kind=kOutput, calls=%fused_computation.8 | convolution fusion | flops 16793600 | bytes 2260992 | tf_op jit(solution)/shard_map/bshk,hkv->bshv/dot_general | solution.py:292
  133.3 0.6 copy.42
  (52 shorter events, 1.0 us)
Async XLA Ops:
  0.0 1.6 %copy-start = (bf16[16,128,512]{2,1,0:T(8,128)(2,1)S(1)}, bf16[16,128,512]{2,1,0:T(8,128)(2,1)}, u32[]{:S(2)}) copy-start(bf16[16,128,512]{2,1,0:T(8,128)(2,1)} %param.14) | copy-start | bytes 6291460
  0.0 10.7 %copy-start.6 = (s32[64]{0:T(128)S(1)}, s32[64]{0:T(128)}, u32[]{:S(2)}) copy-start(s32[64]{0:T(128)} %param.10) | copy-start | bytes 772
  2.8 13.5 %collective-permute-start = (bf16[2,4,16,576]{3,1,0,2:T(4,128)(2,1)S(1)}, bf16[2,4,16,576]{3,1,0,2:T(4,128)(2,1)S(1)}, u32[]{:S(2)}, u32[]{:S(2)}) collective-permute-start(bf16[2,4,16,576]{3,1,0,2:T(4,128)(2,1)S(1)} %pad_maximum_fusion.2), channel_id=1, source_target_pairs={{0,4},{1,5},{2,6},{3,7},{4,0},{5,1},{6,2},{7,3},{8,12},{9,13},{10,... | collective-permute-start | bytes 442376 | tf_op jit(solution)/shard_map/ppermute | solution.py:35
  10.9 2.3 %copy-start.1 = (bf16[64,128,288]{1,2,0:T(8,128)(2,1)S(1)}, bf16[64,128,288]{1,2,0:T(8,128)(2,1)}, u32[]{:S(2)}) copy-start(bf16[64,128,288]{1,2,0:T(8,128)(2,1)} %param.8) | copy-start | bytes 14155780
  16.4 19.5 %collective-permute-start.1 = (bf16[2,4,288,128]{3,2,1,0:T(8,128)(2,1)}, bf16[2,4,288,128]{3,2,1,0:T(8,128)(2,1)S(1)}, u32[]{:S(2)}, u32[]{:S(2)}) collective-permute-start(bf16[2,4,288,128]{3,2,1,0:T(8,128)(2,1)} %get-tuple-element.64), channel_id=1, source_target_pairs={{0,129},{1,130},{2,131},{3,132},{4,133},{5,134},{6,135},{7,128},{8... | collective-permute-start | bytes 1769480 | tf_op jit(solution)/shard_map/ppermute | solution.py:25
  19.7 18.9 %collective-permute-start.2 = (bf16[2,4,288,128]{3,2,1,0:T(8,128)(2,1)}, bf16[2,4,288,128]{3,2,1,0:T(8,128)(2,1)}, u32[]{:S(2)}, u32[]{:S(2)}) collective-permute-start(bf16[2,4,288,128]{3,2,1,0:T(8,128)(2,1)} %get-tuple-element.65), channel_id=1, source_target_pairs={{0,8},{1,9},{2,10},{3,11},{4,12},{5,13},{6,14},{7,15},{8,16},{9,17... | collective-permute-start | bytes 1769480 | tf_op jit(solution)/shard_map/ppermute | solution.py:31
  21.2 17.4 %copy-start.5 = (s32[64]{0:T(128)S(1)}, s32[64]{0:T(128)}, u32[]{:S(2)}) copy-start(s32[64]{0:T(128)} %param.9) | copy-start | bytes 772
  22.5 39.5 %copy-start.4 = (bf16[2,4,576]{2,1,0:T(4,128)(2,1)S(1)}, bf16[2,4,576]{2,1,0:T(4,128)(2,1)}, u32[]{:S(2)}) copy-start(bf16[2,4,576]{2,1,0:T(4,128)(2,1)} %param.13) | copy-start | bytes 27652
  22.5 32.7 %all-to-all-start = ((bf16[8,2,4,16,576]{4,3,2,1,0:T(8,128)(2,1)}), bf16[8,2,4,16,576]{4,3,2,1,0:T(8,128)(2,1)}, u32[]{:S(2)}, u32[]{:S(2)}) async-start(bf16[8,2,4,16,576]{4,3,2,1,0:T(8,128)(2,1)} %bitcast.8), calls=%async_computation | async-start | bytes 2621440 | tf_op jit(solution)/shard_map/all_to_all | solution.py:262
  27.2 28.0 %collective-permute-start.3 = (bf16[2,4,288,128]{3,2,1,0:T(8,128)(2,1)}, bf16[2,4,288,128]{3,2,1,0:T(8,128)(2,1)S(1)}, u32[]{:S(2)}, u32[]{:S(2)}) collective-permute-start(bf16[2,4,288,128]{3,2,1,0:T(8,128)(2,1)} %get-tuple-element.66), channel_id=1, source_target_pairs={{0,135},{1,128},{2,129},{3,130},{4,131},{5,132},{6,133},{7,134},{8... | collective-permute-start | bytes 1769480 | tf_op jit(solution)/shard_map/ppermute | solution.py:25
  29.8 25.3 %collective-permute-start.4 = (bf16[2,4,288,128]{3,2,1,0:T(8,128)(2,1)}, bf16[2,4,288,128]{3,2,1,0:T(8,128)(2,1)}, u32[]{:S(2)}, u32[]{:S(2)}) collective-permute-start(bf16[2,4,288,128]{3,2,1,0:T(8,128)(2,1)} %get-tuple-element.67), channel_id=1, source_target_pairs={{0,24},{1,25},{2,26},{3,27},{4,28},{5,29},{6,30},{7,31},{8,0},{9,1... | collective-permute-start | bytes 1769480 | tf_op jit(solution)/shard_map/ppermute | solution.py:31
  31.3 23.9 %collective-permute-start.5 = (bf16[2,4,288,128]{3,2,1,0:T(8,128)(2,1)}, bf16[2,4,288,128]{3,2,1,0:T(8,128)(2,1)}, u32[]{:S(2)}, u32[]{:S(2)}) collective-permute-start(bf16[2,4,288,128]{3,2,1,0:T(8,128)(2,1)} %get-tuple-element.68), channel_id=1, source_target_pairs={{0,130},{1,135},{2,132},{3,129},{4,134},{5,131},{6,128},{7,133},{8... | collective-permute-start | bytes 1769480 | tf_op jit(solution)/shard_map/ppermute | solution.py:25
  35.8 28.0 %copy-start.2 = (bf16[2,4,288,128]{3,2,1,0:T(8,128)(2,1)}, bf16[2,4,288,128]{3,2,1,0:T(8,128)(2,1)S(1)}, u32[]{:S(2)}) copy-start(bf16[2,4,288,128]{3,2,1,0:T(8,128)(2,1)S(1)} %collective-permute-done.1.refs_1_) | copy-start | bytes 1769476
  35.8 19.3 %collective-permute-start.6 = (bf16[2,4,288,128]{3,2,1,0:T(8,128)(2,1)}, bf16[2,4,288,128]{3,2,1,0:T(8,128)(2,1)}, u32[]{:S(2)}, u32[]{:S(2)}) collective-permute-start(bf16[2,4,288,128]{3,2,1,0:T(8,128)(2,1)} %get-tuple-element.69), channel_id=1, source_target_pairs={{0,16},{1,17},{2,18},{3,19},{4,20},{5,21},{6,22},{7,23},{8,24},{9,... | collective-permute-start | bytes 1769480 | tf_op jit(solution)/shard_map/ppermute | solution.py:31
  38.6 16.6 %collective-permute-start.7 = (bf16[2,4,288,128]{3,2,1,0:T(8,128)(2,1)}, bf16[2,4,288,128]{3,2,1,0:T(8,128)(2,1)}, u32[]{:S(2)}, u32[]{:S(2)}) collective-permute-start(bf16[2,4,288,128]{3,2,1,0:T(8,128)(2,1)} %get-tuple-element.70), channel_id=1, source_target_pairs={{0,128},{1,129},{2,130},{3,131},{4,132},{5,133},{6,134},{7,135},{8... | collective-permute-start | bytes 1769480 | tf_op jit(solution)/shard_map/ppermute | solution.py:25
  55.2 8.7 %copy-start.3 = (bf16[2,4,288,128]{3,2,1,0:T(8,128)(2,1)}, bf16[2,4,288,128]{3,2,1,0:T(8,128)(2,1)S(1)}, u32[]{:S(2)}) copy-start(bf16[2,4,288,128]{3,2,1,0:T(8,128)(2,1)S(1)} %collective-permute-done.3.refs_2_) | copy-start | bytes 1769476
  58.0 13.0 %copy-start.8 = (bf16[4,288,128]{2,1,0:T(8,128)(2,1)S(1)}, bf16[4,288,128]{2,1,0:T(8,128)(2,1)}, u32[]{:S(2)}) copy-start(bf16[4,288,128]{2,1,0:T(8,128)(2,1)} %get-tuple-element.83) | copy-start | bytes 884740
  58.0 11.3 %collective-permute-start.8 = (bf16[4,288,128]{2,1,0:T(8,128)(2,1)S(1)}, bf16[4,288,128]{2,1,0:T(8,128)(2,1)S(1)}, u32[]{:S(2)}, u32[]{:S(2)}) collective-permute-start(bf16[4,288,128]{2,1,0:T(8,128)(2,1)S(1)} %get-tuple-element.82), channel_id=1, source_target_pairs={{0,1},{1,2},{2,3},{3,4},{4,5},{5,6},{6,7},{7,0},{8,9},{9,10},{10,1... | collective-permute-start | bytes 884744 | tf_op jit(solution)/shard_map/ppermute | solution.py:25
  61.2 9.8 %collective-permute-start.10 = (bf16[4,288,128]{2,1,0:T(8,128)(2,1)S(1)}, bf16[4,288,128]{2,1,0:T(8,128)(2,1)S(1)}, u32[]{:S(2)}, u32[]{:S(2)}) collective-permute-start(bf16[4,288,128]{2,1,0:T(8,128)(2,1)S(1)} %get-tuple-element.85), channel_id=1, source_target_pairs={{0,7},{1,0},{2,1},{3,2},{4,3},{5,4},{6,5},{7,6},{8,15},{9,8},{10,9... | collective-permute-start | bytes 884744 | tf_op jit(solution)/shard_map/ppermute | solution.py:25
  62.0 12.2 %collective-permute-start.12 = (bf16[4,288,128]{2,1,0:T(8,128)(2,1)S(1)}, bf16[4,288,128]{2,1,0:T(8,128)(2,1)S(1)}, u32[]{:S(2)}, u32[]{:S(2)}) collective-permute-start(bf16[4,288,128]{2,1,0:T(8,128)(2,1)S(1)} %get-tuple-element.88), channel_id=1, source_target_pairs={{0,2},{1,7},{2,4},{3,1},{4,6},{5,3},{6,0},{7,5},{8,10},{9,15},{10,... | collective-permute-start | bytes 884744 | tf_op jit(solution)/shard_map/ppermute | solution.py:25
  66.5 18.4 %copy-start.7 = (bf16[4,288,128]{2,1,0:T(8,128)(2,1)S(1)}, bf16[4,288,128]{2,1,0:T(8,128)(2,1)}, u32[]{:S(2)}) copy-start(bf16[4,288,128]{2,1,0:T(8,128)(2,1)} %get-tuple-element.105) | copy-start | bytes 884740
  66.5 11.2 %collective-permute-start.14 = (bf16[4,288,128]{2,1,0:T(8,128)(2,1)S(1)}, bf16[4,288,128]{2,1,0:T(8,128)(2,1)S(1)}, u32[]{:S(2)}, u32[]{:S(2)}) collective-permute-start(bf16[4,288,128]{2,1,0:T(8,128)(2,1)S(1)} %get-tuple-element.98), channel_id=1, source_target_pairs={{0,8},{1,9},{2,10},{3,11},{4,12},{5,13},{6,14},{7,15},{8,16},{9,17... | collective-permute-start | bytes 884744 | tf_op jit(solution)/shard_map/ppermute | solution.py:31
  67.7 12.4 %collective-permute-start.16 = (bf16[4,288,128]{2,1,0:T(8,128)(2,1)S(1)}, bf16[4,288,128]{2,1,0:T(8,128)(2,1)S(1)}, u32[]{:S(2)}, u32[]{:S(2)}) collective-permute-start(bf16[4,288,128]{2,1,0:T(8,128)(2,1)S(1)} %get-tuple-element.101), channel_id=1, source_target_pairs={{0,16},{1,17},{2,18},{3,19},{4,20},{5,21},{6,22},{7,23},{8,24},{9,... | collective-permute-start | bytes 884744 | tf_op jit(solution)/shard_map/ppermute | solution.py:31
  69.4 11.8 %collective-permute-start.18 = (bf16[4,288,128]{2,1,0:T(8,128)(2,1)S(1)}, bf16[4,288,128]{2,1,0:T(8,128)(2,1)S(1)}, u32[]{:S(2)}, u32[]{:S(2)}) collective-permute-start(bf16[4,288,128]{2,1,0:T(8,128)(2,1)S(1)} %get-tuple-element.104), channel_id=1, source_target_pairs={{0,24},{1,25},{2,26},{3,27},{4,28},{5,29},{6,30},{7,31},{8,0},{9,1... | collective-permute-start | bytes 884744 | tf_op jit(solution)/shard_map/ppermute | solution.py:31
  71.0 13.9 %collective-permute-start.9 = (bf16[4,288,128]{2,1,0:T(8,128)(2,1)S(1)}, bf16[4,288,128]{2,1,0:T(8,128)(2,1)S(1)}, u32[]{:S(2)}, u32[]{:S(2)}) collective-permute-start(bf16[4,288,128]{2,1,0:T(8,128)(2,1)S(1)} %copy-done.8), channel_id=1, source_target_pairs={{0,1},{1,2},{2,3},{3,4},{4,5},{5,6},{6,7},{7,0},{8,9},{9,10},{10,1... | collective-permute-start | bytes 884744 | tf_op jit(solution)/shard_map/ppermute | solution.py:25
  74.2 26.8 %collective-permute-start.11 = (bf16[4,288,128]{2,1,0:T(8,128)(2,1)}, bf16[4,288,128]{2,1,0:T(8,128)(2,1)S(1)}, u32[]{:S(2)}, u32[]{:S(2)}) collective-permute-start(bf16[4,288,128]{2,1,0:T(8,128)(2,1)} %get-tuple-element.86), channel_id=1, source_target_pairs={{0,7},{1,0},{2,1},{3,2},{4,3},{5,4},{6,5},{7,6},{8,15},{9,8},{10,9... | collective-permute-start | bytes 884744 | tf_op jit(solution)/shard_map/ppermute | solution.py:25
  77.7 23.3 %collective-permute-start.13 = (bf16[4,288,128]{2,1,0:T(8,128)(2,1)}, bf16[4,288,128]{2,1,0:T(8,128)(2,1)}, u32[]{:S(2)}, u32[]{:S(2)}) collective-permute-start(bf16[4,288,128]{2,1,0:T(8,128)(2,1)} %get-tuple-element.89), channel_id=1, source_target_pairs={{0,2},{1,7},{2,4},{3,1},{4,6},{5,3},{6,0},{7,5},{8,10},{9,15},{10,... | collective-permute-start | bytes 884744 | tf_op jit(solution)/shard_map/ppermute | solution.py:25
  80.1 21.0 %collective-permute-start.15 = (bf16[4,288,128]{2,1,0:T(8,128)(2,1)}, bf16[4,288,128]{2,1,0:T(8,128)(2,1)}, u32[]{:S(2)}, u32[]{:S(2)}) collective-permute-start(bf16[4,288,128]{2,1,0:T(8,128)(2,1)} %get-tuple-element.99), channel_id=1, source_target_pairs={{0,8},{1,9},{2,10},{3,11},{4,12},{5,13},{6,14},{7,15},{8,16},{9,17... | collective-permute-start | bytes 884744 | tf_op jit(solution)/shard_map/ppermute | solution.py:31
  81.1 20.0 %collective-permute-start.17 = (bf16[4,288,128]{2,1,0:T(8,128)(2,1)}, bf16[4,288,128]{2,1,0:T(8,128)(2,1)}, u32[]{:S(2)}, u32[]{:S(2)}) collective-permute-start(bf16[4,288,128]{2,1,0:T(8,128)(2,1)} %get-tuple-element.102), channel_id=1, source_target_pairs={{0,16},{1,17},{2,18},{3,19},{4,20},{5,21},{6,22},{7,23},{8,24},{9,... | collective-permute-start | bytes 884744 | tf_op jit(solution)/shard_map/ppermute | solution.py:31
  84.9 7.6 %copy-start.9 = (bf16[4,288,128]{2,1,0:T(8,128)(2,1)}, bf16[4,288,128]{2,1,0:T(8,128)(2,1)S(1)}, u32[]{:S(2)}) copy-start(bf16[4,288,128]{2,1,0:T(8,128)(2,1)S(1)} %collective-permute-done.9.rest_1_) | copy-start | bytes 884740
  84.9 16.2 %collective-permute-start.19 = (bf16[4,288,128]{2,1,0:T(8,128)(2,1)S(1)}, bf16[4,288,128]{2,1,0:T(8,128)(2,1)}, u32[]{:S(2)}, u32[]{:S(2)}) collective-permute-start(bf16[4,288,128]{2,1,0:T(8,128)(2,1)S(1)} %copy-done.7), channel_id=1, source_target_pairs={{0,24},{1,25},{2,26},{3,27},{4,28},{5,29},{6,30},{7,31},{8,0},{9,1... | collective-permute-start | bytes 884744 | tf_op jit(solution)/shard_map/ppermute | solution.py:31
  92.6 19.3 %all-to-all-start.1 = ((bf16[8,64,640]{2,1,0:T(8,128)(2,1)}), bf16[8,64,640]{2,1,0:T(8,128)(2,1)S(1)}, u32[]{:S(2)}, u32[]{:S(2)}) async-start(bf16[8,64,640]{2,1,0:T(8,128)(2,1)} %bitcast.59), calls=%async_computation.1 | async-start | bytes 1310720 | tf_op jit(solution)/shard_map/all_to_all | solution.py:280
  101.0 0.7 copy-start.10
  112.1 18.5 %all-to-all-start.2 = ((bf16[8,64,640]{2,1,0:T(8,128)(2,1)}), bf16[8,64,640]{2,1,0:T(8,128)(2,1)S(1)}, u32[]{:S(2)}, u32[]{:S(2)}) async-start(bf16[8,64,640]{2,1,0:T(8,128)(2,1)} %bitcast.60), calls=%async_computation.2 | async-start | bytes 1310720 | tf_op jit(solution)/shard_map/all_to_all | solution.py:288
  116.0 14.7 %collective-permute-start.20 = (bf16[2,64,640]{2,1,0:T(8,128)(2,1)S(1)}, bf16[2,64,640]{2,1,0:T(8,128)(2,1)S(1)}, u32[]{:S(2)}, u32[]{:S(2)}) collective-permute-start(bf16[2,64,640]{2,1,0:T(8,128)(2,1)S(1)} %shard_map.87), channel_id=1, source_target_pairs={{0,4},{1,5},{2,6},{3,7},{4,0},{5,1},{6,2},{7,3},{8,12},{9,13},{10,... | collective-permute-start | bytes 491528 | tf_op jit(solution)/shard_map/ppermute | solution.py:35

commit v6 on v5

--- a/solution.py
+++ b/solution.py
@@ -260,11 +260,11 @@
     heads = 2 * lax.axis_size("ctx")
     spread = jnp.broadcast_to(both[:, None], (req_dev, lax.axis_size("ctx"), *both.shape[1:]))
     every = lax.all_to_all(spread.reshape(heads, *both.shape[1:]), ("role", "ctx"), 0, 0, tiled=True)
-    first = [move_z(picked[1], 1, 1), move_x(picked[5], 1), move_z(picked[2], 2, 1), move_x(picked[7], 3),
-             move_z(picked[3], 3, 1), move_x(picked[6], 2), move_z(picked[0], 0, 1)]
+    first = [move_z(picked[3], 3, 1), move_x(picked[6], 2), move_z(picked[1], 1, 1), move_x(picked[5], 1),
+             move_z(picked[2], 2, 1), move_x(picked[7], 3), move_z(picked[0], 0, 1)]
     first, every = lax.optimization_barrier((first, every))
-    got_z = [first[6], first[0], first[2], first[4]]
-    got_x = [picked[4], first[1], first[5], first[3]]
+    got_z = [first[6], first[2], first[4], first[0]]
+    got_x = [picked[4], first[3], first[1], first[5]]
     every = jnp.moveaxis(every, 1, 0).reshape(2, -1, latent + rope_dim)
     mine_f, mine_n = second(got_x, move_z)
     recv_f, recv_n = second(got_z, move_x)

time: 135 us -> 130 us (0.963)
  waiting for transfers between devices: 30.8 us -> 24.1 us
  starting transfers between devices: 65.6 us -> 68.3 us
    ppermute x10, waiting for transfers between devices: 18.7 us -> 10.2 us  [move_z(): return lax.ppermute(a, ('role', 'req'), pairs)]
    ppermute x9, starting transfers between devices: 15.8 us -> 18.3 us  [move_x(): lax.ppermute(a, 'req', [(x * NZ + z, (x + dx) % NX * NZ + z) for x in ran...]
    ppermute x9, waiting for transfers between devices: 1.65 us -> 3.73 us  [move_x(): lax.ppermute(a, 'req', [(x * NZ + z, (x + dx) % NX * NZ + z) for x in ran...]
  transfers between devices with their start and end apart: 24 -> 24, of which waited for: 6 -> 8; matrix products, arithmetic and copies ran while one was open for 5% -> 5% of each run, Pallas kernels for 14% -> 15%
where the time goes in v6:
time: 130 us
  starting transfers between devices  68.3 us (53%)
  waiting for transfers between devices  24.1 us (19%)
  Pallas kernels  21.7 us (17%)
  local copies, waits for them, and re-layouts  8.94 us (7%)
  matrix products  3.17 us (2%)
  other arithmetic  3.13 us (2%)
    ppermute x9, starting transfers between devices, move_x(): lax.ppermute(a, 'req', [(x * NZ + z, (x + dx) % NX * NZ + z) for x in ran...  18.3 us
    ppermute x10, starting transfers between devices, move_z(): return lax.ppermute(a, ('role', 'req'), pairs)  17.7 us
    ppermute x2, starting transfers between devices, move_far(): lax.ppermute(a, 'req', [(x * NZ + z, x * NZ + (z + 4) % NZ) for x in rang...  15.2 us
    pallas_call x2, Pallas kernels, attend(): pl.pallas_call(functools.partial(attend_kernel, fresh, scale), in_specs=[...  13.1 us
    ppermute x10, waiting for transfers between devices, move_z(): return lax.ppermute(a, ('role', 'req'), pairs)  10.2 us
    all_to_all x1, starting transfers between devices, shards(): lax.all_to_all(part_f.reshape(heads, -1, latent + LANES), ('role', 'ctx')...  8.63 us
    ppermute x2, waiting for transfers between devices, move_far(): lax.ppermute(a, 'req', [(x * NZ + z, x * NZ + (z + 4) % NZ) for x in rang...  7.63 us
    pallas_call x2, Pallas kernels, regroup(): pl.pallas_call(regroup_kernel, in_specs=[vm] * 4, out_specs=[vm] * 8, out...  5.29 us
  transfers between devices with their start and end apart: 24, of which 8 were waited for; matrix products, arithmetic and copies ran while one was open for 5% of the time, Pallas kernels for 15%

profile of v6, /device:TPU:1, one launch (start us, length us, event | category | flops | bytes accessed | tf_op | source)
XLA Modules:
  0.0 129.6 jit_solution(656024786099474939)
XLA Ops:
  0.0 1.0 reshape.132
  1.0 0.6 copy-done
  1.6 1.1 fusion.7
  2.8 7.8 %collective-permute-start = (bf16[2,4,16,576]{3,1,0,2:T(4,128)(2,1)S(1)}, bf16[2,4,16,576]{3,1,0,2:T(4,128)(2,1)S(1)}, u32[]{:S(2)}, u32[]{:S(2)}) collective-permute-start(bf16[2,4,16,576]{3,1,0,2:T(4,128)(2,1)S(1)} %pad_maximum_fusion.2), channel_id=1, source_target_pairs={{0,4},{1,5},{2,6},{3,7},{4,0},{5,1},{6,2},{7,3},{8,12},{9,13},{10,... | collective-permute-start | bytes 442376 | tf_op jit(solution)/shard_map/ppermute | solution.py:35
  10.9 2.3 %copy-done.1 = bf16[64,128,288]{1,2,0:T(8,128)(2,1)S(1)} copy-done((bf16[64,128,288]{1,2,0:T(8,128)(2,1)S(1)}, bf16[64,128,288]{1,2,0:T(8,128)(2,1)}, u32[]{:S(2)}) %copy-start.1) | copy-done | bytes 4718616
  13.2 3.0 %shard_map.82 = (bf16[2,4,288,128]{3,2,1,0:T(8,128)(2,1)}, bf16[2,4,288,128]{3,2,1,0:T(8,128)(2,1)}, bf16[2,4,288,128]{3,2,1,0:T(8,128)(2,1)}, bf16[2,4,288,128]...) custom-call(s32[64]{0:T(128)S(1)} %select_reduce_fusion.idx_ref, ...), custom_call_target="tpu_custom_call" | custom-call | bytes 9437184 | tf_op jit(solution)/shard_map/pallas_call | solution.py:56
  16.2 4.6 %collective-permute-start.1 = (bf16[2,4,288,128]{3,2,1,0:T(8,128)(2,1)}, bf16[2,4,288,128]{3,2,1,0:T(8,128)(2,1)S(1)}, u32[]{:S(2)}, u32[]{:S(2)}) collective-permute-start(bf16[2,4,288,128]{3,2,1,0:T(8,128)(2,1)} %get-tuple-element.64), channel_id=1, source_target_pairs={{0,130},{1,135},{2,132},{3,129},{4,134},{5,131},{6,128},{7,133},{8... | collective-permute-start | bytes 1769480 | tf_op jit(solution)/shard_map/ppermute | solution.py:25
  20.8 2.7 %collective-permute-start.2 = (bf16[2,4,288,128]{3,2,1,0:T(8,128)(2,1)}, bf16[2,4,288,128]{3,2,1,0:T(8,128)(2,1)}, u32[]{:S(2)}, u32[]{:S(2)}) collective-permute-start(bf16[2,4,288,128]{3,2,1,0:T(8,128)(2,1)} %get-tuple-element.65), channel_id=1, source_target_pairs={{0,16},{1,17},{2,18},{3,19},{4,20},{5,21},{6,22},{7,23},{8,24},{9,... | collective-permute-start | bytes 1769480 | tf_op jit(solution)/shard_map/ppermute | solution.py:31
  23.6 0.2 pad_maximum_fusion
  23.9 1.2 broadcast_in_dim.71
  25.1 4.7 %all-to-all-start = ((bf16[8,2,4,16,576]{4,3,2,1,0:T(8,128)(2,1)}), bf16[8,2,4,16,576]{4,3,2,1,0:T(8,128)(2,1)}, u32[]{:S(2)}, u32[]{:S(2)}) async-start(bf16[8,2,4,16,576]{4,3,2,1,0:T(8,128)(2,1)} %bitcast.8), calls=%async_computation | async-start | bytes 2621440 | tf_op jit(solution)/shard_map/all_to_all | solution.py:262
  29.8 2.5 %collective-permute-start.3 = (bf16[2,4,288,128]{3,2,1,0:T(8,128)(2,1)}, bf16[2,4,288,128]{3,2,1,0:T(8,128)(2,1)S(1)}, u32[]{:S(2)}, u32[]{:S(2)}) collective-permute-start(bf16[2,4,288,128]{3,2,1,0:T(8,128)(2,1)} %get-tuple-element.66), channel_id=1, source_target_pairs={{0,129},{1,130},{2,131},{3,132},{4,133},{5,134},{6,135},{7,128},{8... | collective-permute-start | bytes 1769480 | tf_op jit(solution)/shard_map/ppermute | solution.py:25
  32.3 0.3 collective-permute-start.4
  32.6 1.4 %collective-permute-start.5 = (bf16[2,4,288,128]{3,2,1,0:T(8,128)(2,1)}, bf16[2,4,288,128]{3,2,1,0:T(8,128)(2,1)}, u32[]{:S(2)}, u32[]{:S(2)}) collective-permute-start(bf16[2,4,288,128]{3,2,1,0:T(8,128)(2,1)} %get-tuple-element.68), channel_id=1, source_target_pairs={{0,135},{1,128},{2,129},{3,130},{4,131},{5,132},{6,133},{7,134},{8... | collective-permute-start | bytes 1769480 | tf_op jit(solution)/shard_map/ppermute | solution.py:25
  34.0 3.0 %collective-permute-done.1.refs_3_ = bf16[2,4,288,128]{3,2,1,0:T(8,128)(2,1)S(1)} collective-permute-done((bf16[2,4,288,128]{3,2,1,0:T(8,128)(2,1)}, bf16[2,4,288,128]{3,2,1,0:T(8,128)(2,1)S(1)}, u32[]{:S(2)}, u32[]{:S(2)}) %collective-permute-start.1) | collective-permute-done | bytes 589856 | tf_op jit(solution)/shard_map/ppermute | solution.py:25
  37.0 3.7 %collective-permute-start.6 = (bf16[2,4,288,128]{3,2,1,0:T(8,128)(2,1)}, bf16[2,4,288,128]{3,2,1,0:T(8,128)(2,1)}, u32[]{:S(2)}, u32[]{:S(2)}) collective-permute-start(bf16[2,4,288,128]{3,2,1,0:T(8,128)(2,1)} %get-tuple-element.69), channel_id=1, source_target_pairs={{0,24},{1,25},{2,26},{3,27},{4,28},{5,29},{6,30},{7,31},{8,0},{9,1... | collective-permute-start | bytes 1769480 | tf_op jit(solution)/shard_map/ppermute | solution.py:31
  40.7 0.7 fusion.36
  41.3 0.7 broadcast_subtract_fusion
  42.0 0.6 broadcast_subtract_fusion.1
  42.6 6.6 %collective-permute-done.3.refs_1_ = bf16[2,4,288,128]{3,2,1,0:T(8,128)(2,1)S(1)} collective-permute-done((bf16[2,4,288,128]{3,2,1,0:T(8,128)(2,1)}, bf16[2,4,288,128]{3,2,1,0:T(8,128)(2,1)S(1)}, u32[]{:S(2)}, u32[]{:S(2)}) %collective-permute-start.3) | collective-permute-done | bytes 589856 | tf_op jit(solution)/shard_map/ppermute | solution.py:25
  49.2 1.0 collective-permute-done.4.refs_1_
  50.2 1.5 %collective-permute-done.6.refs_3_ = bf16[2,4,288,128]{3,2,1,0:T(8,128)(2,1)} collective-permute-done((bf16[2,4,288,128]{3,2,1,0:T(8,128)(2,1)}, bf16[2,4,288,128]{3,2,1,0:T(8,128)(2,1)}, u32[]{:S(2)}, u32[]{:S(2)}) %collective-permute-start.6) | collective-permute-done | bytes 589856 | tf_op jit(solution)/shard_map/ppermute | solution.py:31
  51.7 2.6 %shard_map.83 = (bf16[4,288,128]{2,1,0:T(8,128)(2,1)S(1)}, bf16[4,288,128]{2,1,0:T(8,128)(2,1)S(1)}, bf16[4,288,128]{2,1,0:T(8,128)(2,1)S(1)}, bf16[4,288,128]{2...) custom-call(bf16[2,4,288,128]{3,2,1,0:T(8,128)(2,1)} %get-tuple-elem, ...), custom_call_target="tpu_custom_call" | custom-call | bytes 4718592 | tf_op jit(solution)/shard_map/pallas_call | solution.py:77
  54.3 1.4 %collective-permute-start.8 = (bf16[4,288,128]{2,1,0:T(8,128)(2,1)S(1)}, bf16[4,288,128]{2,1,0:T(8,128)(2,1)S(1)}, u32[]{:S(2)}, u32[]{:S(2)}) collective-permute-start(bf16[4,288,128]{2,1,0:T(8,128)(2,1)S(1)} %get-tuple-element.82), channel_id=1, source_target_pairs={{0,1},{1,2},{2,3},{3,4},{4,5},{5,6},{6,7},{7,0},{8,9},{9,10},{10,1... | collective-permute-start | bytes 884744 | tf_op jit(solution)/shard_map/ppermute | solution.py:25
  55.8 2.1 %collective-permute-start.10 = (bf16[4,288,128]{2,1,0:T(8,128)(2,1)S(1)}, bf16[4,288,128]{2,1,0:T(8,128)(2,1)S(1)}, u32[]{:S(2)}, u32[]{:S(2)}) collective-permute-start(bf16[4,288,128]{2,1,0:T(8,128)(2,1)S(1)} %get-tuple-element.85), channel_id=1, source_target_pairs={{0,7},{1,0},{2,1},{3,2},{4,3},{5,4},{6,5},{7,6},{8,15},{9,8},{10,9... | collective-permute-start | bytes 884744 | tf_op jit(solution)/shard_map/ppermute | solution.py:25
  58.1 2.6 %shard_map.84 = (bf16[4,288,128]{2,1,0:T(8,128)(2,1)S(1)}, bf16[4,288,128]{2,1,0:T(8,128)(2,1)S(1)}, bf16[4,288,128]{2,1,0:T(8,128)(2,1)S(1)}, bf16[4,288,128]{2...) custom-call(bf16[2,4,288,128]{3,2,1,0:T(8,128)(2,1)} %collective-per, ...), custom_call_target="tpu_custom_call" | custom-call | bytes 4718592 | tf_op jit(solution)/shard_map/pallas_call | solution.py:77
  60.7 0.9 collective-permute-start.14
  61.7 3.7 %collective-permute-start.16 = (bf16[4,288,128]{2,1,0:T(8,128)(2,1)S(1)}, bf16[4,288,128]{2,1,0:T(8,128)(2,1)S(1)}, u32[]{:S(2)}, u32[]{:S(2)}) collective-permute-start(bf16[4,288,128]{2,1,0:T(8,128)(2,1)S(1)} %get-tuple-element.101), channel_id=1, source_target_pairs={{0,16},{1,17},{2,18},{3,19},{4,20},{5,21},{6,22},{7,23},{8,24},{9,... | collective-permute-start | bytes 884744 | tf_op jit(solution)/shard_map/ppermute | solution.py:31
  65.3 2.0 %collective-permute-start.18 = (bf16[4,288,128]{2,1,0:T(8,128)(2,1)S(1)}, bf16[4,288,128]{2,1,0:T(8,128)(2,1)S(1)}, u32[]{:S(2)}, u32[]{:S(2)}) collective-permute-start(bf16[4,288,128]{2,1,0:T(8,128)(2,1)S(1)} %get-tuple-element.104), channel_id=1, source_target_pairs={{0,24},{1,25},{2,26},{3,27},{4,28},{5,29},{6,30},{7,31},{8,0},{9,1... | collective-permute-start | bytes 884744 | tf_op jit(solution)/shard_map/ppermute | solution.py:31
  67.4 0.8 collective-permute-start.9
  68.2 2.3 %fusion.45 = (bf16[1,8,4,16,576]{4,3,2,0,1:T(8,128)(2,1)S(1)}, bf16[1,8,4,16,576]{4,3,2,0,1:T(8,128)(2,1)}) fusion(bf16[2,8,4,16,576]{4,3,2,0,1:T(8,128)(2,1)} %bitcast.9), kind=kLoop, calls=%fused_computation.90 | loop fusion | bytes 2359296 | tf_op jit(solution)/shard_map/slice | solution.py:279
  70.5 0.6 collective-permute-done.12.rest_3_
  71.2 1.3 collective-permute-start.11
  72.4 3.5 %collective-permute-start.13 = (bf16[4,288,128]{2,1,0:T(8,128)(2,1)}, bf16[4,288,128]{2,1,0:T(8,128)(2,1)}, u32[]{:S(2)}, u32[]{:S(2)}) collective-permute-start(bf16[4,288,128]{2,1,0:T(8,128)(2,1)} %get-tuple-element.89), channel_id=1, source_target_pairs={{0,2},{1,7},{2,4},{3,1},{4,6},{5,3},{6,0},{7,5},{8,10},{9,15},{10,... | collective-permute-start | bytes 884744 | tf_op jit(solution)/shard_map/ppermute | solution.py:25
  76.0 1.2 collective-permute-done.16.rest_6_
  77.4 2.4 %collective-permute-start.17 = (bf16[4,288,128]{2,1,0:T(8,128)(2,1)}, bf16[4,288,128]{2,1,0:T(8,128)(2,1)}, u32[]{:S(2)}, u32[]{:S(2)}) collective-permute-start(bf16[4,288,128]{2,1,0:T(8,128)(2,1)} %get-tuple-element.102), channel_id=1, source_target_pairs={{0,16},{1,17},{2,18},{3,19},{4,20},{5,21},{6,22},{7,23},{8,24},{9,... | collective-permute-start | bytes 884744 | tf_op jit(solution)/shard_map/ppermute | solution.py:31
  79.8 2.3 %collective-permute-start.19 = (bf16[4,288,128]{2,1,0:T(8,128)(2,1)S(1)}, bf16[4,288,128]{2,1,0:T(8,128)(2,1)}, u32[]{:S(2)}, u32[]{:S(2)}) collective-permute-start(bf16[4,288,128]{2,1,0:T(8,128)(2,1)S(1)} %copy-done.7), channel_id=1, source_target_pairs={{0,24},{1,25},{2,26},{3,27},{4,28},{5,29},{6,30},{7,31},{8,0},{9,1... | collective-permute-start | bytes 884744 | tf_op jit(solution)/shard_map/ppermute | solution.py:31
  82.1 5.6 %shard_map.86 = bf16[512,640]{1,0:T(8,128)(2,1)} custom-call(s32[18]{0:T(128)S(1)} %add_add_fusion.1.scal_ref, bf16[512,576]{1,0:T(8,128)(2,1)S(1)} %bitcast.53, bf16[4,288,128]{2,1,0:T(8,128)(2,1)S(1)} %get-tuple-element.79.rest_0_, bf16[4,288,128]{2,1,0:T(8,128)(2,1)S(1)} %collective-permute-done.8.rest_1_, ...), custom_call_target="tpu_custom_call" | custom-call | flops 18253611008 | bytes 3473408 | tf_op jit(solution)/shard_map/pallas_call | solution.py:174
  87.7 8.6 %all-to-all-start.1 = ((bf16[8,64,640]{2,1,0:T(8,128)(2,1)}), bf16[8,64,640]{2,1,0:T(8,128)(2,1)S(1)}, u32[]{:S(2)}, u32[]{:S(2)}) async-start(bf16[8,64,640]{2,1,0:T(8,128)(2,1)} %bitcast.59), calls=%async_computation.1 | async-start | bytes 1310720 | tf_op jit(solution)/shard_map/all_to_all | solution.py:280
  96.4 0.7 copy-done.10
  97.1 7.6 %shard_map.85 = bf16[512,640]{1,0:T(8,128)(2,1)} custom-call(s32[18]{0:T(128)S(1)} %add_add_fusion.scal_ref, bf16[512,576]{1,0:T(8,128)(2,1)} %bitcast.57, bf16[4,288,128]{2,1,0:T(8,128)(2,1)} %get-tuple-element.80.rest_0_, bf16[4,288,128]{2,1,0:T(8,128)(2,1)} %copy-done.9, bf16[4,288,128]{2,1,0:T(8,128)(2,1)} %copy-done.10, ...), custom_call_target="tpu_custom_call" | custom-call | flops 18253611008 | bytes 3473408 | tf_op jit(solution)/shard_map/pallas_call | solution.py:174
  104.6 2.5 %all-to-all-done.1.parts_ref = bf16[8,64,640]{2,1,0:T(8,128)(2,1)S(1)} async-done(((bf16[8,64,640]{2,1,0:T(8,128)(2,1)}), bf16[8,64,640]{2,1,0:T(8,128)(2,1)S(1)}, u32[]{:S(2)}, u32[]{:S(2)}) %all-to-all-start.1) | async-done | bytes 655392 | tf_op jit(solution)/shard_map/all_to_all | solution.py:280
  107.1 0.3 shard_map.87
  107.4 3.8 %all-to-all-start.2 = ((bf16[8,64,640]{2,1,0:T(8,128)(2,1)}), bf16[8,64,640]{2,1,0:T(8,128)(2,1)S(1)}, u32[]{:S(2)}, u32[]{:S(2)}) async-start(bf16[8,64,640]{2,1,0:T(8,128)(2,1)} %bitcast.60), calls=%async_computation.2 | async-start | bytes 1310720 | tf_op jit(solution)/shard_map/all_to_all | solution.py:288
  111.3 7.4 %collective-permute-start.20 = (bf16[2,64,640]{2,1,0:T(8,128)(2,1)S(1)}, bf16[2,64,640]{2,1,0:T(8,128)(2,1)S(1)}, u32[]{:S(2)}, u32[]{:S(2)}) collective-permute-start(bf16[2,64,640]{2,1,0:T(8,128)(2,1)S(1)} %shard_map.87), channel_id=1, source_target_pairs={{0,4},{1,5},{2,6},{3,7},{4,0},{5,1},{6,2},{7,3},{8,12},{9,13},{10,... | collective-permute-start | bytes 491528 | tf_op jit(solution)/shard_map/ppermute | solution.py:35
  118.7 7.6 %collective-permute-done.20 = bf16[2,64,640]{2,1,0:T(8,128)(2,1)S(1)} collective-permute-done((bf16[2,64,640]{2,1,0:T(8,128)(2,1)S(1)}, bf16[2,64,640]{2,1,0:T(8,128)(2,1)S(1)}, u32[]{:S(2)}, u32[]{:S(2)}) %collective-permute-start.20) | collective-permute-done | bytes 163872 | tf_op jit(solution)/shard_map/ppermute | solution.py:35
  126.9 2.0 %fusion.13 = bf16[16,2,1,4,128]{4,3,2,1,0:T(4,128)(2,1)S(1)} fusion(bf16[16,512,128]{2,1,0:T(8,128)(2,1)} %param.15, bf16[2,4,16,512]{3,2,1,0:T(8,128)(2,1)S(1)} %divide_convert_fusion), kind=kOutput, calls=%fused_computation.8 | convolution fusion | flops 16793600 | bytes 2260992 | tf_op jit(solution)/shard_map/bshk,hkv->bshv/dot_general | solution.py:292
  129.0 0.6 copy.42
  (52 shorter events, 1.5 us)
Async XLA Ops:
  0.0 1.6 %copy-start = (bf16[16,128,512]{2,1,0:T(8,128)(2,1)S(1)}, bf16[16,128,512]{2,1,0:T(8,128)(2,1)}, u32[]{:S(2)}) copy-start(bf16[16,128,512]{2,1,0:T(8,128)(2,1)} %param.14) | copy-start | bytes 6291460
  0.0 10.7 %copy-start.6 = (s32[64]{0:T(128)S(1)}, s32[64]{0:T(128)}, u32[]{:S(2)}) copy-start(s32[64]{0:T(128)} %param.10) | copy-start | bytes 772
  2.8 13.4 %collective-permute-start = (bf16[2,4,16,576]{3,1,0,2:T(4,128)(2,1)S(1)}, bf16[2,4,16,576]{3,1,0,2:T(4,128)(2,1)S(1)}, u32[]{:S(2)}, u32[]{:S(2)}) collective-permute-start(bf16[2,4,16,576]{3,1,0,2:T(4,128)(2,1)S(1)} %pad_maximum_fusion.2), channel_id=1, source_target_pairs={{0,4},{1,5},{2,6},{3,7},{4,0},{5,1},{6,2},{7,3},{8,12},{9,13},{10,... | collective-permute-start | bytes 442376 | tf_op jit(solution)/shard_map/ppermute | solution.py:35
  10.9 2.3 %copy-start.1 = (bf16[64,128,288]{1,2,0:T(8,128)(2,1)S(1)}, bf16[64,128,288]{1,2,0:T(8,128)(2,1)}, u32[]{:S(2)}) copy-start(bf16[64,128,288]{1,2,0:T(8,128)(2,1)} %param.8) | copy-start | bytes 14155780
  16.2 20.7 %collective-permute-start.1 = (bf16[2,4,288,128]{3,2,1,0:T(8,128)(2,1)}, bf16[2,4,288,128]{3,2,1,0:T(8,128)(2,1)S(1)}, u32[]{:S(2)}, u32[]{:S(2)}) collective-permute-start(bf16[2,4,288,128]{3,2,1,0:T(8,128)(2,1)} %get-tuple-element.64), channel_id=1, source_target_pairs={{0,130},{1,135},{2,132},{3,129},{4,134},{5,131},{6,128},{7,133},{8... | collective-permute-start | bytes 1769480 | tf_op jit(solution)/shard_map/ppermute | solution.py:25
  20.8 19.9 %collective-permute-start.2 = (bf16[2,4,288,128]{3,2,1,0:T(8,128)(2,1)}, bf16[2,4,288,128]{3,2,1,0:T(8,128)(2,1)}, u32[]{:S(2)}, u32[]{:S(2)}) collective-permute-start(bf16[2,4,288,128]{3,2,1,0:T(8,128)(2,1)} %get-tuple-element.65), channel_id=1, source_target_pairs={{0,16},{1,17},{2,18},{3,19},{4,20},{5,21},{6,22},{7,23},{8,24},{9,... | collective-permute-start | bytes 1769480 | tf_op jit(solution)/shard_map/ppermute | solution.py:31
  23.8 16.8 %copy-start.5 = (s32[64]{0:T(128)S(1)}, s32[64]{0:T(128)}, u32[]{:S(2)}) copy-start(s32[64]{0:T(128)} %param.9) | copy-start | bytes 772
  25.1 32.9 %copy-start.4 = (bf16[2,4,576]{2,1,0:T(4,128)(2,1)S(1)}, bf16[2,4,576]{2,1,0:T(4,128)(2,1)}, u32[]{:S(2)}) copy-start(bf16[2,4,576]{2,1,0:T(4,128)(2,1)} %param.13) | copy-start | bytes 27652
  25.1 26.6 %all-to-all-start = ((bf16[8,2,4,16,576]{4,3,2,1,0:T(8,128)(2,1)}), bf16[8,2,4,16,576]{4,3,2,1,0:T(8,128)(2,1)}, u32[]{:S(2)}, u32[]{:S(2)}) async-start(bf16[8,2,4,16,576]{4,3,2,1,0:T(8,128)(2,1)} %bitcast.8), calls=%async_computation | async-start | bytes 2621440 | tf_op jit(solution)/shard_map/all_to_all | solution.py:262
  29.8 19.4 %collective-permute-start.3 = (bf16[2,4,288,128]{3,2,1,0:T(8,128)(2,1)}, bf16[2,4,288,128]{3,2,1,0:T(8,128)(2,1)S(1)}, u32[]{:S(2)}, u32[]{:S(2)}) collective-permute-start(bf16[2,4,288,128]{3,2,1,0:T(8,128)(2,1)} %get-tuple-element.66), channel_id=1, source_target_pairs={{0,129},{1,130},{2,131},{3,132},{4,133},{5,134},{6,135},{7,128},{8... | collective-permute-start | bytes 1769480 | tf_op jit(solution)/shard_map/ppermute | solution.py:25
  32.3 17.9 %collective-permute-start.4 = (bf16[2,4,288,128]{3,2,1,0:T(8,128)(2,1)}, bf16[2,4,288,128]{3,2,1,0:T(8,128)(2,1)}, u32[]{:S(2)}, u32[]{:S(2)}) collective-permute-start(bf16[2,4,288,128]{3,2,1,0:T(8,128)(2,1)} %get-tuple-element.67), channel_id=1, source_target_pairs={{0,8},{1,9},{2,10},{3,11},{4,12},{5,13},{6,14},{7,15},{8,16},{9,17... | collective-permute-start | bytes 1769480 | tf_op jit(solution)/shard_map/ppermute | solution.py:31
  32.6 17.6 %collective-permute-start.5 = (bf16[2,4,288,128]{3,2,1,0:T(8,128)(2,1)}, bf16[2,4,288,128]{3,2,1,0:T(8,128)(2,1)}, u32[]{:S(2)}, u32[]{:S(2)}) collective-permute-start(bf16[2,4,288,128]{3,2,1,0:T(8,128)(2,1)} %get-tuple-element.68), channel_id=1, source_target_pairs={{0,135},{1,128},{2,129},{3,130},{4,131},{5,132},{6,133},{7,134},{8... | collective-permute-start | bytes 1769480 | tf_op jit(solution)/shard_map/ppermute | solution.py:25
  37.0 21.1 %copy-start.2 = (bf16[2,4,288,128]{3,2,1,0:T(8,128)(2,1)}, bf16[2,4,288,128]{3,2,1,0:T(8,128)(2,1)S(1)}, u32[]{:S(2)}) copy-start(bf16[2,4,288,128]{3,2,1,0:T(8,128)(2,1)S(1)} %collective-permute-done.1.refs_3_) | copy-start | bytes 1769476
  37.0 14.7 %collective-permute-start.6 = (bf16[2,4,288,128]{3,2,1,0:T(8,128)(2,1)}, bf16[2,4,288,128]{3,2,1,0:T(8,128)(2,1)}, u32[]{:S(2)}, u32[]{:S(2)}) collective-permute-start(bf16[2,4,288,128]{3,2,1,0:T(8,128)(2,1)} %get-tuple-element.69), channel_id=1, source_target_pairs={{0,24},{1,25},{2,26},{3,27},{4,28},{5,29},{6,30},{7,31},{8,0},{9,1... | collective-permute-start | bytes 1769480 | tf_op jit(solution)/shard_map/ppermute | solution.py:31
  40.7 11.0 %collective-permute-start.7 = (bf16[2,4,288,128]{3,2,1,0:T(8,128)(2,1)}, bf16[2,4,288,128]{3,2,1,0:T(8,128)(2,1)}, u32[]{:S(2)}, u32[]{:S(2)}) collective-permute-start(bf16[2,4,288,128]{3,2,1,0:T(8,128)(2,1)} %get-tuple-element.70), channel_id=1, source_target_pairs={{0,128},{1,129},{2,130},{3,131},{4,132},{5,133},{6,134},{7,135},{8... | collective-permute-start | bytes 1769480 | tf_op jit(solution)/shard_map/ppermute | solution.py:25
  49.2 8.9 %copy-start.3 = (bf16[2,4,288,128]{3,2,1,0:T(8,128)(2,1)}, bf16[2,4,288,128]{3,2,1,0:T(8,128)(2,1)S(1)}, u32[]{:S(2)}) copy-start(bf16[2,4,288,128]{3,2,1,0:T(8,128)(2,1)S(1)} %collective-permute-done.3.refs_1_) | copy-start | bytes 1769476
  54.3 13.0 %copy-start.8 = (bf16[4,288,128]{2,1,0:T(8,128)(2,1)S(1)}, bf16[4,288,128]{2,1,0:T(8,128)(2,1)}, u32[]{:S(2)}) copy-start(bf16[4,288,128]{2,1,0:T(8,128)(2,1)} %get-tuple-element.83) | copy-start | bytes 884740
  54.3 11.0 %collective-permute-start.8 = (bf16[4,288,128]{2,1,0:T(8,128)(2,1)S(1)}, bf16[4,288,128]{2,1,0:T(8,128)(2,1)S(1)}, u32[]{:S(2)}, u32[]{:S(2)}) collective-permute-start(bf16[4,288,128]{2,1,0:T(8,128)(2,1)S(1)} %get-tuple-element.82), channel_id=1, source_target_pairs={{0,1},{1,2},{2,3},{3,4},{4,5},{5,6},{6,7},{7,0},{8,9},{9,10},{10,1... | collective-permute-start | bytes 884744 | tf_op jit(solution)/shard_map/ppermute | solution.py:25
  55.8 11.6 %collective-permute-start.10 = (bf16[4,288,128]{2,1,0:T(8,128)(2,1)S(1)}, bf16[4,288,128]{2,1,0:T(8,128)(2,1)S(1)}, u32[]{:S(2)}, u32[]{:S(2)}) collective-permute-start(bf16[4,288,128]{2,1,0:T(8,128)(2,1)S(1)} %get-tuple-element.85), channel_id=1, source_target_pairs={{0,7},{1,0},{2,1},{3,2},{4,3},{5,4},{6,5},{7,6},{8,15},{9,8},{10,9... | collective-permute-start | bytes 884744 | tf_op jit(solution)/shard_map/ppermute | solution.py:25
  58.0 13.2 %collective-permute-start.12 = (bf16[4,288,128]{2,1,0:T(8,128)(2,1)S(1)}, bf16[4,288,128]{2,1,0:T(8,128)(2,1)S(1)}, u32[]{:S(2)}, u32[]{:S(2)}) collective-permute-start(bf16[4,288,128]{2,1,0:T(8,128)(2,1)S(1)} %get-tuple-element.88), channel_id=1, source_target_pairs={{0,2},{1,7},{2,4},{3,1},{4,6},{5,3},{6,0},{7,5},{8,10},{9,15},{10,... | collective-permute-start | bytes 884744 | tf_op jit(solution)/shard_map/ppermute | solution.py:25
  60.7 19.1 %copy-start.7 = (bf16[4,288,128]{2,1,0:T(8,128)(2,1)S(1)}, bf16[4,288,128]{2,1,0:T(8,128)(2,1)}, u32[]{:S(2)}) copy-start(bf16[4,288,128]{2,1,0:T(8,128)(2,1)} %get-tuple-element.105) | copy-start | bytes 884740
  60.7 11.7 %collective-permute-start.14 = (bf16[4,288,128]{2,1,0:T(8,128)(2,1)S(1)}, bf16[4,288,128]{2,1,0:T(8,128)(2,1)S(1)}, u32[]{:S(2)}, u32[]{:S(2)}) collective-permute-start(bf16[4,288,128]{2,1,0:T(8,128)(2,1)S(1)} %get-tuple-element.98), channel_id=1, source_target_pairs={{0,8},{1,9},{2,10},{3,11},{4,12},{5,13},{6,14},{7,15},{8,16},{9,17... | collective-permute-start | bytes 884744 | tf_op jit(solution)/shard_map/ppermute | solution.py:31
  61.7 15.5 %collective-permute-start.16 = (bf16[4,288,128]{2,1,0:T(8,128)(2,1)S(1)}, bf16[4,288,128]{2,1,0:T(8,128)(2,1)S(1)}, u32[]{:S(2)}, u32[]{:S(2)}) collective-permute-start(bf16[4,288,128]{2,1,0:T(8,128)(2,1)S(1)} %get-tuple-element.101), channel_id=1, source_target_pairs={{0,16},{1,17},{2,18},{3,19},{4,20},{5,21},{6,22},{7,23},{8,24},{9,... | collective-permute-start | bytes 884744 | tf_op jit(solution)/shard_map/ppermute | solution.py:31
  65.3 12.1 %collective-permute-start.18 = (bf16[4,288,128]{2,1,0:T(8,128)(2,1)S(1)}, bf16[4,288,128]{2,1,0:T(8,128)(2,1)S(1)}, u32[]{:S(2)}, u32[]{:S(2)}) collective-permute-start(bf16[4,288,128]{2,1,0:T(8,128)(2,1)S(1)} %get-tuple-element.104), channel_id=1, source_target_pairs={{0,24},{1,25},{2,26},{3,27},{4,28},{5,29},{6,30},{7,31},{8,0},{9,1... | collective-permute-start | bytes 884744 | tf_op jit(solution)/shard_map/ppermute | solution.py:31
  67.4 12.4 %collective-permute-start.9 = (bf16[4,288,128]{2,1,0:T(8,128)(2,1)S(1)}, bf16[4,288,128]{2,1,0:T(8,128)(2,1)S(1)}, u32[]{:S(2)}, u32[]{:S(2)}) collective-permute-start(bf16[4,288,128]{2,1,0:T(8,128)(2,1)S(1)} %copy-done.8), channel_id=1, source_target_pairs={{0,1},{1,2},{2,3},{3,4},{4,5},{5,6},{6,7},{7,0},{8,9},{9,10},{10,1... | collective-permute-start | bytes 884744 | tf_op jit(solution)/shard_map/ppermute | solution.py:25
  71.2 25.2 %collective-permute-start.11 = (bf16[4,288,128]{2,1,0:T(8,128)(2,1)}, bf16[4,288,128]{2,1,0:T(8,128)(2,1)S(1)}, u32[]{:S(2)}, u32[]{:S(2)}) collective-permute-start(bf16[4,288,128]{2,1,0:T(8,128)(2,1)} %get-tuple-element.86), channel_id=1, source_target_pairs={{0,7},{1,0},{2,1},{3,2},{4,3},{5,4},{6,5},{7,6},{8,15},{9,8},{10,9... | collective-permute-start | bytes 884744 | tf_op jit(solution)/shard_map/ppermute | solution.py:25
  72.4 23.9 %collective-permute-start.13 = (bf16[4,288,128]{2,1,0:T(8,128)(2,1)}, bf16[4,288,128]{2,1,0:T(8,128)(2,1)}, u32[]{:S(2)}, u32[]{:S(2)}) collective-permute-start(bf16[4,288,128]{2,1,0:T(8,128)(2,1)} %get-tuple-element.89), channel_id=1, source_target_pairs={{0,2},{1,7},{2,4},{3,1},{4,6},{5,3},{6,0},{7,5},{8,10},{9,15},{10,... | collective-permute-start | bytes 884744 | tf_op jit(solution)/shard_map/ppermute | solution.py:25
  77.2 19.1 %collective-permute-start.15 = (bf16[4,288,128]{2,1,0:T(8,128)(2,1)}, bf16[4,288,128]{2,1,0:T(8,128)(2,1)}, u32[]{:S(2)}, u32[]{:S(2)}) collective-permute-start(bf16[4,288,128]{2,1,0:T(8,128)(2,1)} %get-tuple-element.99), channel_id=1, source_target_pairs={{0,8},{1,9},{2,10},{3,11},{4,12},{5,13},{6,14},{7,15},{8,16},{9,17... | collective-permute-start | bytes 884744 | tf_op jit(solution)/shard_map/ppermute | solution.py:31
  77.4 18.9 %collective-permute-start.17 = (bf16[4,288,128]{2,1,0:T(8,128)(2,1)}, bf16[4,288,128]{2,1,0:T(8,128)(2,1)}, u32[]{:S(2)}, u32[]{:S(2)}) collective-permute-start(bf16[4,288,128]{2,1,0:T(8,128)(2,1)} %get-tuple-element.102), channel_id=1, source_target_pairs={{0,16},{1,17},{2,18},{3,19},{4,20},{5,21},{6,22},{7,23},{8,24},{9,... | collective-permute-start | bytes 884744 | tf_op jit(solution)/shard_map/ppermute | solution.py:31
  79.8 7.9 %copy-start.9 = (bf16[4,288,128]{2,1,0:T(8,128)(2,1)}, bf16[4,288,128]{2,1,0:T(8,128)(2,1)S(1)}, u32[]{:S(2)}) copy-start(bf16[4,288,128]{2,1,0:T(8,128)(2,1)S(1)} %collective-permute-done.9.rest_1_) | copy-start | bytes 884740
  79.8 16.6 %collective-permute-start.19 = (bf16[4,288,128]{2,1,0:T(8,128)(2,1)S(1)}, bf16[4,288,128]{2,1,0:T(8,128)(2,1)}, u32[]{:S(2)}, u32[]{:S(2)}) collective-permute-start(bf16[4,288,128]{2,1,0:T(8,128)(2,1)S(1)} %copy-done.7), channel_id=1, source_target_pairs={{0,24},{1,25},{2,26},{3,27},{4,28},{5,29},{6,30},{7,31},{8,0},{9,1... | collective-permute-start | bytes 884744 | tf_op jit(solution)/shard_map/ppermute | solution.py:31
  87.7 19.4 %all-to-all-start.1 = ((bf16[8,64,640]{2,1,0:T(8,128)(2,1)}), bf16[8,64,640]{2,1,0:T(8,128)(2,1)S(1)}, u32[]{:S(2)}, u32[]{:S(2)}) async-start(bf16[8,64,640]{2,1,0:T(8,128)(2,1)} %bitcast.59), calls=%async_computation.1 | async-start | bytes 1310720 | tf_op jit(solution)/shard_map/all_to_all | solution.py:280
  96.3 0.7 copy-start.10
  107.4 18.9 %all-to-all-start.2 = ((bf16[8,64,640]{2,1,0:T(8,128)(2,1)}), bf16[8,64,640]{2,1,0:T(8,128)(2,1)S(1)}, u32[]{:S(2)}, u32[]{:S(2)}) async-start(bf16[8,64,640]{2,1,0:T(8,128)(2,1)} %bitcast.60), calls=%async_computation.2 | async-start | bytes 1310720 | tf_op jit(solution)/shard_map/all_to_all | solution.py:288
  111.3 15.0 %collective-permute-start.20 = (bf16[2,64,640]{2,1,0:T(8,128)(2,1)S(1)}, bf16[2,64,640]{2,1,0:T(8,128)(2,1)S(1)}, u32[]{:S(2)}, u32[]{:S(2)}) collective-permute-start(bf16[2,64,640]{2,1,0:T(8,128)(2,1)S(1)} %shard_map.87), channel_id=1, source_target_pairs={{0,4},{1,5},{2,6},{3,7},{4,0},{5,1},{6,2},{7,3},{8,12},{9,13},{10,... | collective-permute-start | bytes 491528 | tf_op jit(solution)/shard_map/ppermute | solution.py:35
